TPU v7x, 32 devices: a whole 2x2x4 slice. The times are simulated.
32 devices in a mesh: group: 2 (over x), patch: 8 (over z, y), uly: 2 (over core).
Axes of the slice: x: 2, y: 2, z: 4, core: 2. Of those that a mesh axis runs over, the one named last changes fastest.
Arguments:
- fresh_first: bfloat16 [3, 1536, 1536], P(None, ('group', 'patch', 'uly')), parts along dimension 1, may hold values from -200 to 200
- fresh_second: bfloat16 [3, 1536, 1536], P(None, ('group', 'patch', 'uly')), parts along dimension 1, may hold values from -200 to 200
- stale_cache: bfloat16 [2, 1536, 1536], P(None, ('group', 'patch'), 'uly'), parts along dimension 1, may hold values from -40 to 40
- stale_exponent: int32 [4, 12], P('group'), parts along dimension 0, may hold values from -2 to 1
- text_first: bfloat16 [2, 512, 1536], P(None, 'group', 'uly'), parts along dimension 1, may hold values from -40 to 40
- text_second: bfloat16 [2, 512, 1536], P(None, 'group', 'uly'), parts along dimension 1, may hold values from -40 to 40
Outputs:
- attended_first: bfloat16 [1536, 1536], P(('group', 'patch', 'uly')), parts along dimension 0
- attended_second: bfloat16 [1536, 1536], P(('group', 'patch', 'uly')), parts along dimension 0
There are 2 independent parts, one for each index of `group`. A program takes and returns all parts, laid end to end along the dimension named above; each array names one. Nothing has to cross between parts.
All inputs are finite; a program needn't handle non-finite values.
Results may differ from a plain program's by a relative error of at most 0.0065.
Values may be sent and summed in bfloat16 or wider, within the bound.
No kernel may reach another device: no remote copies, remote signals or barrier semaphores. Data moves between devices by JAX's collectives and lax.ppermute only.
A program may use at most 128 MiB of HBM per device.

v0:
```python
import jax
import jax.numpy as jnp
from jax import lax
from jax.sharding import PartitionSpec as P

HEAD = 128


def heads_view(array):
    return array.reshape(array.shape[0], array.shape[1] // HEAD, HEAD)


def absorb(carry, queries, keys_rows, values, key_scale, value_scale, keep):
    top, total, accum = carry
    inverse = 1.0 / HEAD**0.5
    score = jnp.einsum("qhd,khd->hqk", queries, keys_rows, preferred_element_type=jnp.float32)
    score = score * (key_scale * inverse)[:, None, None]
    if keep is not None:
        score = jnp.where(keep[None, None, :], score, -jnp.inf)
    new_top = jnp.maximum(top, score.max(-1))
    fade = jnp.exp(top - new_top)
    weight = jnp.exp(score - new_top[:, :, None])
    total = total * fade + weight.sum(-1)
    addend = jnp.einsum(
        "hqk,khd->qhd", weight.astype(jnp.bfloat16), values, preferred_element_type=jnp.float32
    )
    accum = accum * fade.T[:, :, None] + addend * value_scale[None, :, None]
    return (new_top, total, accum)


def step_attention(mine, text, key_scale, value_scale, far_pass, site_back):
    queries = heads_view(mine[0])
    rows = queries.shape[0]
    local_heads = queries.shape[1]
    unit = jnp.ones((local_heads,), jnp.float32)
    carry = (
        jnp.full((local_heads, rows), -jnp.inf, jnp.float32),
        jnp.zeros((local_heads, rows), jnp.float32),
        jnp.zeros((rows, local_heads, HEAD), jnp.float32),
    )
    carry = absorb(carry, queries, heads_view(text[0]), heads_view(text[1]), unit, unit, None)
    carry = absorb(carry, queries, heads_view(mine[1]), heads_view(mine[2]), unit, unit, None)
    carry = far_pass(carry, queries, key_scale, value_scale)
    top, total, accum = carry
    result = (accum / total.T[:, :, None]).reshape(rows, local_heads * HEAD).astype(jnp.bfloat16)
    if site_back == 1:
        return lax.all_to_all(result, "uly", split_axis=0, concat_axis=1, tiled=True)
    return lax.all_to_all(result, "uly", split_axis=0, concat_axis=1, tiled=True)


def shards(fresh_first, fresh_second, stale_cache, stale_exponent, text_first, text_second):
    lanes = lax.axis_size("uly")
    local_heads = stale_exponent.shape[1] // lanes
    first_head = lax.axis_index("uly") * local_heads
    exponents = lax.dynamic_slice_in_dim(stale_exponent, first_head, local_heads, 1)
    scales = jnp.exp2(exponents.astype(jnp.float32))
    unit = jnp.ones((local_heads,), jnp.float32)
    mine_first = lax.all_to_all(fresh_first, "uly", split_axis=2, concat_axis=1, tiled=True)
    mine_second = None
    rows = mine_first.shape[1]
    own_start = lax.axis_index("patch") * rows

    def outside(count):
        places = jnp.arange(count, dtype=jnp.int32)
        return (places < own_start) | (places >= own_start + rows)

    def stale_pass(carry, queries, key_scale, value_scale):
        piece = lax.all_gather(stale_cache, "patch", axis=1, tiled=True)
        keep = outside(piece.shape[1])
        return absorb(
            carry, queries, heads_view(piece[0]), heads_view(piece[1]), key_scale, value_scale, keep
        )

    attended_first = step_attention(mine_first, text_first, scales[0], scales[1], stale_pass, 1)
    mine_second = lax.all_to_all(fresh_second, "uly", split_axis=2, concat_axis=1, tiled=True)

    def refresh_pass(carry, queries, key_scale, value_scale):
        piece = lax.all_gather(mine_first[1:], "patch", axis=1, tiled=True)
        keep = outside(piece.shape[1])
        return absorb(
            carry, queries, heads_view(piece[0]), heads_view(piece[1]), key_scale, value_scale, keep
        )

    attended_second = step_attention(mine_second, text_second, unit, unit, refresh_pass, 2)
    return (attended_first, attended_second)


def solution(mesh):
    placed = (
        P(None, ("group", "patch", "uly"), None),
        P(None, ("group", "patch", "uly"), None),
        P(None, ("group", "patch"), "uly"),
        P("group", None),
        P(None, "group", "uly"),
        P(None, "group", "uly"),
    )
    return jax.shard_map(
        shards,
        mesh=mesh,
        in_specs=placed,
        out_specs=(P(("group", "patch", "uly"), None), P(("group", "patch", "uly"), None)),
        check_vma=False,
    )
```

profile of v0, /device:TPU:0, one launch (start us, length us, event | category | flops | bytes accessed | tf_op | source)
XLA Modules:
  0.0 147.8 jit_solution(14437617630779452056)
XLA Ops:
  7.2 2.0 %copy.90 = bf16[2,96,768]{2,0,1:T(2,128)(2,1)} copy(bf16[2,96,768]{2,1,0:T(8,128)(2,1)} %param.8) | data formatting | bytes 589824 | tf_op args[2]
  9.3 2.5 %copy.76 = bf16[3,48,1536]{1,0,2:T(4,128)(2,1)S(1)} copy(bf16[3,48,1536]{2,1,0:T(8,128)(2,1)} %param.6) | data formatting | bytes 884736 | tf_op args[0]
  11.8 2.0 %reshape.78 = bf16[2,2,55296]{2,1,0:T(2,128)(2,1)S(1)} reshape(bf16[1536,3,48]{2,1,0:T(4,128)(2,1)S(1)} %bitcast.175) | data formatting | bytes 884736
  13.7 4.1 %all_to_all.62 = bf16[2,2,55296]{2,1,0:T(2,128)(2,1)S(1)} all-to-all(bf16[2,2,55296]{2,1,0:T(2,128)(2,1)S(1)} %reshape.78), channel_id=1, replica_groups=mesh['group'=2,'patch'=8,'uly'=2] {'uly'}, dimensions={0} | all-to-all | bytes 884736 | tf_op jit(solution)/shard_map/all_to_all | solution.py:58
  17.8 2.0 %reshape.79 = bf16[1536,3,48]{2,1,0:T(4,128)(2,1)S(1)} reshape(bf16[2,2,55296]{2,1,0:T(2,128)(2,1)S(1)} %all_to_all.62) | data formatting | bytes 884736
  19.9 1.3 copy.127
  22.1 1.0 copy.98
  23.2 2.7 %reshape.80 = bf16[2,2,55296]{2,1,0:T(2,128)(2,1)} reshape(bf16[1536,3,48]{2,1,0:T(4,128)(2,1)S(1)} %bitcast.176) | data formatting | bytes 884736
  25.8 3.7 %all-to-all-start.2 = ((bf16[2,2,55296]{2,1,0:T(2,128)(2,1)}), bf16[2,2,55296]{2,1,0:T(2,128)(2,1)S(1)}, u32[]{:S(2)}, u32[]{:S(2)}) async-start(bf16[2,2,55296]{2,1,0:T(2,128)(2,1)} %reshape.80), calls=%async_computation.2 | async-start | bytes 884736 | tf_op jit(solution)/shard_map/all_to_all | solution.py:75
  30.1 0.9 all-to-all-done.2
  31.0 2.0 %reshape.81 = bf16[1536,3,48]{2,1,0:T(4,128)(2,1)S(1)} reshape(bf16[2,2,55296]{2,1,0:T(2,128)(2,1)S(1)} %all-to-all-done.2) | data formatting | bytes 884736
  35.3 0.9 copy.129
  36.7 0.9 reshape_squeeze.46
  37.6 1.0 copy.133
  41.1 0.9 fusion.33
  43.2 0.9 fusion.31
  44.7 0.9 fusion.88
  45.7 1.0 fusion.90
  46.6 18.4 %all-gather.3.cloned.1.call-done = bf16[2,768,768]{2,0,1:T(2,128)(2,1)} async-done(((bf16[2,96,768]{2,0,1:T(2,128)(2,1)}), bf16[2,768,768]{2,0,1:T(2,128)(2,1)}) %all-gather.3.cloned.1.call-update) | async-done | bytes 2359312 | tf_op jit(solution)/shard_map/all_gather | solution.py:68
  65.0 8.0 %fusion.82 = (bf16[1,768,768]{2,0,1:T(2,128)(2,1)S(1)}, bf16[1,768,768]{2,0,1:T(2,128)(2,1)}) fusion(bf16[2,768,768]{2,0,1:T(2,128)(2,1)} %all-gather.3.cloned.1.call-done), kind=kLoop, calls=%fused_computation.109 | loop fusion | bytes 4718592 | tf_op jit(solution)/shard_map/slice | solution.py:71
  73.0 6.5 %copy.131 = bf16[1,768,768]{1,2,0:T(8,128)(2,1)} copy(bf16[1,768,768]{2,0,1:T(2,128)(2,1)} %get-tuple-element.19) | data formatting | bytes 2359296
  79.4 2.0 %copy.130 = bf16[1,768,768]{1,2,0:T(8,128)(2,1)S(1)} copy(bf16[1,768,768]{2,0,1:T(2,128)(2,1)S(1)} %get-tuple-element.18) | data formatting | bytes 2359296
  81.5 1.3 fusion.55
  82.8 35.1 %all-gather.5.cloned.1.call-done = bf16[2,768,768]{2,1,0:T(8,128)(2,1)} async-done(((bf16[2,96,768]{2,1,0:T(8,128)(2,1)}), bf16[2,768,768]{2,1,0:T(8,128)(2,1)}) %all-gather.5.cloned.1.call-update) | async-done | bytes 2359312 | tf_op jit(solution)/shard_map/all_gather | solution.py:78
  117.8 2.8 %fusion.81 = (bf16[1,768,768]{2,1,0:T(8,128)(2,1)}, bf16[1,768,768]{2,1,0:T(8,128)(2,1)S(1)}) fusion(bf16[2,768,768]{2,1,0:T(8,128)(2,1)} %all-gather.5.cloned.1.call-done), kind=kLoop, calls=%fused_computation.108 | loop fusion | bytes 4718592 | tf_op jit(solution)/shard_map/slice | solution.py:81
  120.7 1.5 copy.110
  122.1 2.0 %fusion.1 = (f32[6,96]{1,0:T(8,128)S(1)}, f32[6,96]{1,0:T(8,128)S(1)}, f32[6,96,768]{2,1,0:T(8,128)S(1)}) fusion(pred[768]{0:T(1024)(128)(4,1)} %fusion.71, f32[6,96,768]{2,1,0:T(8,128)S(1)} %fusion.55, f32[6]{0:T(128)} %get-tuple-element.33, bf16[768,6,128]{0,2,1:T(8,128)(2,1)} %bitcast.178, bf16[96,6,128]{2,1,0:T(8,128)(2,1)} %copy-done.6), kind=kOutput, calls=%fused_computation.5 | convolution fusion | flops 115899264 | bytes 4871448 | tf_op jit(solution)/shard_map/qhd,khd->hqk/dot_general | solution.py:16
  124.9 0.9 fusion.4
  127.5 3.8 %all_to_all.63 = bf16[2,48,768]{2,1,0:T(8,128)(2,1)S(1)} all-to-all(bf16[2,48,768]{2,1,0:T(8,128)(2,1)S(1)} %convert_element_type.40), channel_id=1, replica_groups=mesh['group'=2,'patch'=8,'uly'=2] {'uly'}, dimensions={0} | all-to-all | bytes 294912 | tf_op jit(solution)/shard_map/all_to_all | solution.py:47
  132.0 1.5 copy.113
  133.5 2.0 %convolution_bitcast_fusion.4 = f32[96,6,128]{2,0,1:T(8,128)S(1)} fusion(bf16[768,6,128]{0,2,1:T(8,128)(2,1)} %bitcast.187, f32[6,96,768]{2,1,0:T(8,128)S(1)} %get-tuple-element.34, f32[6,96]{1,0:T(8,128)S(1)} %copy-done.24, pred[768]{0:T(1024)(128)(4,1)S(1)} %copy-done.26), kind=kOutput, calls=%fused_computation.30 | convolution fusion | flops 115015680 | bytes 3247104 | tf_op jit(solution)/shard_map/hqk,khd->qhd/dot_general | solution.py:24
  136.4 3.8 %all_to_all.64 = bf16[2,48,768]{2,1,0:T(8,128)(2,1)S(1)} all-to-all(bf16[2,48,768]{2,1,0:T(8,128)(2,1)S(1)} %convert_element_type.45), channel_id=1, replica_groups=mesh['group'=2,'patch'=8,'uly'=2] {'uly'}, dimensions={0} | all-to-all | bytes 294912 | tf_op jit(solution)/shard_map/all_to_all | solution.py:48
  (102 shorter events, 13.0 us)
Async XLA Ops:
  7.2 57.8 %all-gather.3.cloned.1.call-start = ((), (), s32[]{:S(2)}) async-start(), calls=%async_computation.4 | async-start | bytes 2654208 | tf_op jit(solution)/shard_map/all_gather | solution.py:68
  9.2 108.6 %all-gather.5.cloned.1.call-start = ((), (), s32[]{:S(2)}) async-start(), calls=%async_computation.5 | async-start | bytes 2654208 | tf_op jit(solution)/shard_map/all_gather | solution.py:78
  19.9 2.3 %copy-start.16 = (bf16[3,48,1536]{2,1,0:T(8,128)(2,1)S(1)}, bf16[3,48,1536]{2,1,0:T(8,128)(2,1)}, u32[]{:S(2)}) copy-start(bf16[3,48,1536]{2,1,0:T(8,128)(2,1)} %param.7) | copy-start | bytes 1327108
  25.8 5.2 %all-to-all-start.2 = ((bf16[2,2,55296]{2,1,0:T(2,128)(2,1)}), bf16[2,2,55296]{2,1,0:T(2,128)(2,1)S(1)}, u32[]{:S(2)}, u32[]{:S(2)}) async-start(bf16[2,2,55296]{2,1,0:T(2,128)(2,1)} %reshape.80), calls=%async_computation.2 | async-start | bytes 884736 | tf_op jit(solution)/shard_map/all_to_all | solution.py:75
  30.0 14.7 %copy-start.5 = (bf16[96,6,128]{2,1,0:T(8,128)(2,1)}, bf16[96,6,128]{2,1,0:T(8,128)(2,1)S(1)}, u32[]{:S(2)}) copy-start(bf16[96,6,128]{2,1,0:T(8,128)(2,1)S(1)} %reshape_squeeze.42) | copy-start | bytes 442372
  33.0 1.7 %copy-start.13 = (bf16[2,256,768]{2,1,0:T(8,128)(2,1)S(1)}, bf16[2,256,768]{2,1,0:T(8,128)(2,1)}, u32[]{:S(2)}) copy-start(bf16[2,256,768]{2,1,0:T(8,128)(2,1)} %param.10) | copy-start | bytes 2359300
  34.8 10.9 %copy-start.6 = (bf16[96,6,128]{2,1,0:T(8,128)(2,1)}, bf16[96,6,128]{2,1,0:T(8,128)(2,1)S(1)}, u32[]{:S(2)}) copy-start(bf16[96,6,128]{2,1,0:T(8,128)(2,1)S(1)} %reshape_squeeze.49) | copy-start | bytes 442372
  34.8 1.4 copy-start.14
  35.0 1.4 copy-start.15
  36.3 3.6 %copy-start.28 = (s32[2,12]{1,0:T(2,128)S(1)}, s32[2,12]{1,0:T(2,128)}, u32[]{:S(2)}) copy-start(s32[2,12]{1,0:T(2,128)} %param.9) | copy-start | bytes 292
  40.3 0.8 copy-start
  42.4 0.9 copy-start.2
  122.1 2.1 %copy-start.9 = (bf16[1,768,768]{1,2,0:T(8,128)(2,1)S(1)}, bf16[1,768,768]{1,2,0:T(8,128)(2,1)}, u32[]{:S(2)}) copy-start(bf16[1,768,768]{1,2,0:T(8,128)(2,1)} %copy.131) | copy-start | bytes 3538948
  122.1 2.1 %copy-start.25 = (pred[768]{0:T(1024)(128)(4,1)S(1)}, pred[768]{0:T(1024)(128)(4,1)}, u32[]{:S(2)}) copy-start(pred[768]{0:T(1024)(128)(4,1)} %fusion.71) | copy-start | bytes 2308
  122.1 2.1 %copy-start.27 = (f32[6]{0:T(128)S(1)}, f32[6]{0:T(128)}, u32[]{:S(2)}) copy-start(f32[6]{0:T(128)} %get-tuple-element.33) | copy-start | bytes 76
  122.1 2.1 %copy-start.29 = (f32[6]{0:T(128)S(1)}, f32[6]{0:T(128)}, u32[]{:S(2)}) copy-start(f32[6]{0:T(128)} %get-tuple-element.32) | copy-start | bytes 76
  124.2 1.7 %copy-start.21 = (f32[6,96]{1,0:T(8,128)}, f32[6,96]{1,0:T(8,128)S(1)}, u32[]{:S(2)}) copy-start(f32[6,96]{1,0:T(8,128)S(1)} %get-tuple-element.13) | copy-start | bytes 6916
  124.9 1.0 copy-start.10
  124.9 1.1 copy-start.12
  124.9 1.2 copy-start.19
  124.9 1.2 copy-start.20
  124.9 1.2 copy-start.3
  124.9 1.3 copy-start.8
  125.8 1.0 copy-start.18
  126.3 5.7 %copy-start.4 = (bf16[1,768,768]{2,1,0:T(8,128)(2,1)S(1)}, bf16[1,768,768]{2,1,0:T(8,128)(2,1)}, u32[]{:S(2)}) copy-start(bf16[1,768,768]{2,1,0:T(8,128)(2,1)} %get-tuple-element.16) | copy-start | bytes 3538948
  127.2 6.2 %copy-start.24 = (f32[6,96]{1,0:T(8,128)S(1)}, f32[6,96]{1,0:T(8,128)}, u32[]{:S(2)}) copy-start(f32[6,96]{1,0:T(8,128)} %copy-done.23) | copy-start | bytes 6916
  127.2 6.2 %copy-start.26 = (pred[768]{0:T(1024)(128)(4,1)S(1)}, pred[768]{0:T(1024)(128)(4,1)}, u32[]{:S(2)}) copy-start(pred[768]{0:T(1024)(128)(4,1)} %fusion.71) | copy-start | bytes 2308
  133.4 2.0 %copy-start.1 = (f32[6,96,256]{2,1,0:T(8,128)S(1)}, f32[6,96,256]{2,1,0:T(8,128)}, u32[]{:S(2)}) copy-start(f32[6,96,256]{2,1,0:T(8,128)} %copy-done) | copy-start | bytes 1769476
  133.4 2.0 %copy-start.7 = (bf16[1,256,768]{1,2,0:T(8,128)(2,1)S(1)}, bf16[1,256,768]{1,2,0:T(8,128)(2,1)}, u32[]{:S(2)}) copy-start(bf16[1,256,768]{1,2,0:T(8,128)(2,1)} %copy.133) | copy-start | bytes 1179652
  133.4 2.4 %copy-start.11 = (f32[6,96,96]{1,2,0:T(8,128)S(1)}, f32[6,96,96]{1,2,0:T(8,128)}, u32[]{:S(2)}) copy-start(f32[6,96,96]{1,2,0:T(8,128)} %get-tuple-element.42) | copy-start | bytes 663556
  133.4 2.4 %copy-start.17 = (bf16[96,6,128]{2,1,0:T(8,128)(2,1)S(1)}, bf16[96,6,128]{2,1,0:T(8,128)(2,1)}, u32[]{:S(2)}) copy-start(bf16[96,6,128]{2,1,0:T(8,128)(2,1)} %reshape_squeeze.53) | copy-start | bytes 442372
  133.4 2.4 %copy-start.22 = (f32[6,96]{1,0:T(8,128)S(1)}, f32[6,96]{1,0:T(8,128)}, u32[]{:S(2)}) copy-start(f32[6,96]{1,0:T(8,128)} %copy-done.21) | copy-start | bytes 6916
  (1 other events, 0.7 us)
Sparse Core Ops, SparseCore 0:
  10.2 54.7 all-gather.2
  67.2 50.6 all-gather.4
where the time goes:
time: 148 us
  waiting for transfers between devices  54.4 us (37%)
  local copies, waits for them, and re-layouts  49.4 us (33%)
  between operations  14.7 us (10%)
  blocking collectives  11.7 us (8%)
  matrix products  9.75 us (7%)
  other arithmetic  4.06 us (3%)
  starting transfers between devices  3.74 us (3%)
    all_gather x1, waiting for transfers between devices, refresh_pass(): piece = lax.all_gather(mine_first[1:], 'patch', axis=1, tiled=True)  35.1 us
    unnamed x73, local copies, waits for them, and re-layouts  27.2 us
    all_gather x1, waiting for transfers between devices, stale_pass(): piece = lax.all_gather(stale_cache, 'patch', axis=1, tiled=True)  18.4 us
    slice x1, local copies, waits for them, and re-layouts, stale_pass(): piece[0]  7.96 us
    all_to_all x2, blocking collectives, step_attention(): lax.all_to_all(result, 'uly', split_axis=0, concat_axis=1, tiled=True)  7.65 us
    dot_general x6, matrix products, absorb(): jnp.einsum('qhd,khd->hqk', queries, keys_rows, preferred_element_type=jnp...  5.87 us
    slice x2, local copies, waits for them, and re-layouts, refresh_pass(): piece[1]  4.28 us
    all_to_all x1, blocking collectives, shards(): lax.all_to_all(fresh_first, 'uly', split_axis=2, concat_axis=1, tiled=True)  4.08 us
  transfers between devices with their start and end apart: 3, of which 3 were waited for; matrix products, arithmetic and copies ran while one was open for 30% of the time, Pallas kernels for 0%

commit v1 on v0

v1 whole, which is shorter than its diff:
```python
import functools

import jax
import jax.numpy as jnp
from jax import lax
from jax.experimental import pallas as pl
from jax.experimental.pallas import tpu as pltpu
from jax.sharding import PartitionSpec as P

HEAD = 128
COLUMNS = 2
BF16 = jnp.bfloat16
F32 = jnp.float32


def heads_view(array):
    return array.reshape(array.shape[0], array.shape[1] // HEAD, HEAD)


def absorb(carry, queries, keys_rows, values, key_scale, value_scale, keep):
    top, total, accum = carry
    inverse = 1.0 / HEAD**0.5
    score = jnp.einsum("qhd,khd->hqk", queries, keys_rows, preferred_element_type=F32)
    score = score * (key_scale * inverse)[:, None, None]
    if keep is not None:
        score = jnp.where(keep[None, None, :], score, -jnp.inf)
    new_top = jnp.maximum(top, score.max(-1))
    fade = jnp.exp(top - new_top)
    weight = jnp.exp(score - new_top[:, :, None])
    total = total * fade + weight.sum(-1)
    addend = jnp.einsum("hqk,khd->qhd", weight.astype(BF16), values, preferred_element_type=F32)
    accum = accum * fade.T[:, :, None] + addend * value_scale[None, :, None]
    return (new_top, total, accum)


def general_step(mine, text, far, keep, key_scale, value_scale):
    queries = heads_view(mine[0])
    rows, local_heads = queries.shape[:2]
    unit = jnp.ones((local_heads,), F32)
    carry = (
        jnp.full((local_heads, rows), -jnp.inf, F32),
        jnp.zeros((local_heads, rows), F32),
        jnp.zeros((rows, local_heads, HEAD), F32),
    )
    carry = absorb(carry, queries, heads_view(text[0]), heads_view(text[1]), unit, unit, None)
    carry = absorb(carry, queries, heads_view(mine[1]), heads_view(mine[2]), unit, unit, None)
    carry = absorb(carry, queries, heads_view(far[0]), heads_view(far[1]), key_scale, value_scale, keep)
    top, total, accum = carry
    result = (accum / total.T[:, :, None]).reshape(rows, local_heads * HEAD).astype(BF16)
    return lax.all_to_all(result, "uly", split_axis=0, concat_axis=1, tiled=True)


def general_shards(fresh_first, fresh_second, stale_cache, stale_exponent, text_first, text_second):
    local_heads = stale_exponent.shape[1] // lax.axis_size("uly")
    first_head = lax.axis_index("uly") * local_heads
    exponents = lax.dynamic_slice_in_dim(stale_exponent, first_head, local_heads, 1)
    scales = jnp.exp2(exponents.astype(F32))
    unit = jnp.ones((local_heads,), F32)
    mine_first = lax.all_to_all(fresh_first, "uly", split_axis=2, concat_axis=1, tiled=True)
    mine_second = lax.all_to_all(fresh_second, "uly", split_axis=2, concat_axis=1, tiled=True)
    rows = mine_first.shape[1]
    own_start = lax.axis_index("patch") * rows
    stale = lax.all_gather(stale_cache, "patch", axis=1, tiled=True)
    refreshed = lax.all_gather(mine_first[1:], "patch", axis=1, tiled=True)
    places = jnp.arange(stale.shape[1], dtype=jnp.int32)
    keep = (places < own_start) | (places >= own_start + rows)
    return (
        general_step(mine_first, text_first, stale, keep, scales[0], scales[1]),
        general_step(mine_second, text_second, refreshed, keep, unit, unit),
    )


def attention_kernel(scale_ref, q_ref, tk_ref, tv_ref, ok_ref, ov_ref, *rest, rows):
    fk_refs, fv_refs, out_ref = rest[0:4], rest[4:8], rest[8]
    head = pl.program_id(0)
    inverse = 1.0 / HEAD**0.5
    key_factor = scale_ref[0, head] * inverse
    value_factor = scale_ref[1, head]

    def dot_t(a, b):
        return lax.dot_general(a, b, (((1,), (1,)), ((), ())), preferred_element_type=F32)

    def dot(a, b):
        return jnp.dot(a, b, preferred_element_type=F32)

    q = q_ref[...]
    count = q.shape[0]
    block = lax.broadcasted_iota(jnp.int32, (count, count), 0) // rows
    inside = block == lax.broadcasted_iota(jnp.int32, (count, count), 1) // rows
    text = dot_t(q, tk_ref[...]) * inverse
    near = [
        jnp.where(inside, dot_t(q, ok_ref[i]) * inverse, dot_t(q, fk_refs[i][...]) * key_factor)
        for i in range(2)
    ]
    away = [dot_t(q, fk_refs[i][...]) * key_factor for i in range(2, 4)]
    scores = [text] + near + away
    top = functools.reduce(jnp.maximum, [s.max(-1, keepdims=True) for s in scores])
    weights = [jnp.exp(s - top) for s in scores]
    total = functools.reduce(jnp.add, [w.sum(-1, keepdims=True) for w in weights])
    rounded = [w.astype(BF16) for w in weights]
    zero = jnp.zeros((), BF16)
    own = dot(rounded[0], tv_ref[...])
    for i in range(2):
        own = own + dot(jnp.where(inside, rounded[1 + i], zero), ov_ref[i])
    far = dot(rounded[3], fv_refs[2][...]) + dot(rounded[4], fv_refs[3][...])
    for i in range(2):
        far = far + dot(jnp.where(inside, zero, rounded[1 + i]), fv_refs[i][...])
    out_ref[...] = ((own + value_factor * far) / total).astype(BF16)


def attention(scales, q, text, own_keys, own_values, far_keys, far_values, rows):
    count, width = q.shape
    heads = width // HEAD
    text_rows = text.shape[1]
    flat = pl.BlockSpec((count, HEAD), lambda h: (0, h))
    pair = pl.BlockSpec((2, count, HEAD), lambda h: (0, 0, h))
    text_spec = pl.BlockSpec((text_rows, HEAD), lambda h: (0, h))
    keys = text_rows + 4 * count
    return pl.pallas_call(
        functools.partial(attention_kernel, rows=rows),
        grid=(heads,),
        out_shape=jax.ShapeDtypeStruct((count, width), BF16),
        in_specs=[pl.BlockSpec(memory_space=pltpu.SMEM), flat, text_spec, text_spec, pair, pair] + [flat] * 8,
        out_specs=flat,
        cost_estimate=pl.CostEstimate(
            flops=4 * count * keys * width, bytes_accessed=2 * width * (2 * keys + 4 * count), transcendentals=count * keys * heads
        ),
    )(scales, q, text[0], text[1], own_keys, own_values, *far_keys, *far_values)


def layered_shards(layers, fresh_first, fresh_second, stale_cache, stale_exponent, text_first, text_second):
    core = lax.axis_index("uly")
    patch = lax.axis_index("patch")
    layer = patch // COLUMNS
    rows, features = fresh_first.shape[1:]
    width = features // layers
    heads = width // HEAD
    half = features // 2

    def layer_shift(x, shift):
        pairs = [
            (z * COLUMNS + y, (z + shift) % layers * COLUMNS + y) for z in range(layers) for y in range(COLUMNS)
        ]
        return lax.ppermute(x, "patch", pairs)

    def other_column(x):
        return lax.ppermute(x, "patch", [(p, p ^ 1) for p in range(layers * COLUMNS)])

    def other_core(x):
        return lax.ppermute(x, "uly", [(0, 1), (1, 0)])

    def columns_of(x, shift):
        start = (layer + shift) % layers * width
        return lax.dynamic_slice_in_dim(x, start, width, x.ndim - 1)

    keep = lax.dynamic_slice_in_dim(stale_cache, core * rows, rows, 1)
    give = lax.dynamic_slice_in_dim(stale_cache, (1 - core) * rows, rows, 1)
    got = other_core(give)
    stale = jnp.where(core == 0, jnp.concatenate([keep, got], 2), jnp.concatenate([got, keep], 2))

    source = jnp.concatenate([stale, fresh_first[1:]], 0)
    pieces = [columns_of(source, 0)] + [layer_shift(columns_of(source, s), s) for s in range(1, layers)]
    later = jnp.concatenate([fresh_first[:1], fresh_second], 0)
    later = [columns_of(later, 0)] + [layer_shift(columns_of(later, s), s) for s in range(1, layers)]

    count = layers * rows
    here = jnp.concatenate(pieces, 1)
    there = other_column(here)
    here_twin = other_core(here)
    there_twin = other_core(there)
    later = jnp.concatenate(later, 1)
    second_twin = other_core(later[2:])

    text = jnp.concatenate([text_first, text_second], 0)
    text = lax.dynamic_slice_in_dim(text, layer * width % half, width, 2)
    text = jnp.where(core == layer * width // half, text, other_core(text))

    scales = jnp.exp2(lax.dynamic_slice_in_dim(stale_exponent, layer * heads, heads, 1).astype(F32))
    far = [here, here_twin, there, there_twin]
    first = attention(
        scales,
        later[0],
        text[:2],
        jnp.stack([here[2], here_twin[2]]),
        jnp.stack([here[3], here_twin[3]]),
        [f[0] for f in far],
        [f[1] for f in far],
        rows,
    )
    second = attention(
        jnp.ones_like(scales),
        later[1],
        text[2:],
        jnp.stack([later[2], second_twin[0]]),
        jnp.stack([later[3], second_twin[1]]),
        [f[2] for f in far],
        [f[3] for f in far],
        rows,
    )

    def back(result):
        blocks = result.reshape(layers, rows, width)
        out = jnp.zeros((rows, features), BF16)
        for s in range(layers):
            block = blocks[s] if s == 0 else layer_shift(blocks[s], -s)
            out = lax.dynamic_update_slice_in_dim(out, block, (layer + s) % layers * width, 1)
        return out

    return back(first), back(second)


def solution(mesh):
    placed = (
        P(None, ("group", "patch", "uly"), None),
        P(None, ("group", "patch", "uly"), None),
        P(None, ("group", "patch"), "uly"),
        P("group", None),
        P(None, "group", "uly"),
        P(None, "group", "uly"),
    )

    def shards(*arrays):
        layers = mesh.shape["patch"] // COLUMNS
        heads = arrays[0].shape[2] // HEAD
        if mesh.shape["uly"] == 2 and layers % 2 == 0 and heads % layers == 0:
            return layered_shards(layers, *arrays)
        return general_shards(*arrays)

    return jax.shard_map(
        shards,
        mesh=mesh,
        in_specs=placed,
        out_specs=(P(("group", "patch", "uly"), None), P(("group", "patch", "uly"), None)),
        check_vma=False,
    )
```

time: 148 us -> 77.4 us (0.52)
  local copies, waits for them, and re-layouts: 49.4 us -> 9.91 us
  waiting for transfers between devices: 54.4 us -> 17 us
  starting transfers between devices: 3.74 us -> 34.4 us
  between operations: 14.7 us -> 0.94 us
  blocking collectives: 11.7 us -> 0 us
  matrix products: 9.75 us -> 0 us
  Pallas kernels: 0 us -> 9.17 us
    all_gather x2 -> x0, waiting for transfers between devices: 53.4 us -> none  [the longest x1 35.1 us: refresh_pass(): piece = lax.all_gather(mine_first[1:], 'patch', axis=1, tiled=True)]
    ppermute x0 -> x18, starting transfers between devices: none -> 34.4 us  [the longest x12 32.2 us: layer_shift(): return lax.ppermute(x, 'patch', pairs)]
    unnamed x73 -> x12, local copies, waits for them, and re-layouts: 27.2 us -> 0.69 us
    ppermute x0 -> x18, waiting for transfers between devices: none -> 17 us  [the longest x1 10.2 us: other_column(): lax.ppermute(x, 'patch', [(p, p ^ 1) for p in range(layers * COLUMNS)])]
    slice x13 -> x8, local copies, waits for them, and re-layouts: 15.8 us -> 3.5 us  [the longest x2 1.7 us: back(): block = blocks[s] if s == 0 else layer_shift(blocks[s], -s)]
    all_to_all x3 -> x0, blocking collectives: 11.7 us -> none  [the longest x2 7.65 us: step_attention(): lax.all_to_all(result, 'uly', split_axis=0, concat_axis=1, tiled=True)]
    dot_general x12 -> x0, matrix products: 9.75 us -> none  [the longest x6 5.87 us: absorb(): jnp.einsum('qhd,khd->hqk', queries, keys_rows, preferred_element_type=jnp...]
    pallas_call x0 -> x2, Pallas kernels: none -> 9.17 us  [attention(): pl.pallas_call(functools.partial(attention_kernel, rows=rows), grid=(head...]
  transfers between devices with their start and end apart: 3 -> 18, of which waited for: 3 -> 7; matrix products, arithmetic and copies ran while one was open for 30% -> 13% of each run, Pallas kernels for 0% -> 6%
where the time goes in v1:
time: 77.4 us; the launch traced here: 76.9 us
  starting transfers between devices  34.4 us (44%)
  waiting for transfers between devices  17 us (22%)
  local copies, waits for them, and re-layouts  9.91 us (13%)
  Pallas kernels  9.17 us (12%)
  other arithmetic  5.43 us (7%)
  between operations  0.94 us (1%)
    ppermute x12, starting transfers between devices, layer_shift(): return lax.ppermute(x, 'patch', pairs)  32.2 us
    ppermute x1, waiting for transfers between devices, other_column(): lax.ppermute(x, 'patch', [(p, p ^ 1) for p in range(layers * COLUMNS)])  10.2 us
    pallas_call x2, Pallas kernels, attention(): pl.pallas_call(functools.partial(attention_kernel, rows=rows), grid=(head...  9.17 us
    ppermute x12, waiting for transfers between devices, layer_shift(): return lax.ppermute(x, 'patch', pairs)  6.74 us
    squeeze x4, local copies, waits for them, and re-layouts, layered_shards(): f[3]  3.45 us
    slice x2, local copies, waits for them, and re-layouts, back(): block = blocks[s] if s == 0 else layer_shift(blocks[s], -s)  1.7 us
    ppermute x1, starting transfers between devices, other_column(): lax.ppermute(x, 'patch', [(p, p ^ 1) for p in range(layers * COLUMNS)])  1.58 us
  transfers between devices with their start and end apart: 18, of which 7 were waited for; matrix products, arithmetic and copies ran while one was open for 13% of the time, Pallas kernels for 6%

profile of v1, /device:TPU:0, one launch (start us, length us, event | category | flops | bytes accessed | tf_op | source)
XLA Modules:
  0.0 76.9 jit_solution(8129423668949040324)
XLA Ops:
  0.7 1.0 %slice.129 = bf16[1,48,1536]{2,1,0:T(8,128)(2,1)S(1)} slice(bf16[3,48,1536]{2,1,0:T(8,128)(2,1)} %param.6), slice={[0:1], [0:48], [0:1536]} | slice | bytes 294912 | tf_op jit(solution)/shard_map/slice | solution.py:163
  1.7 1.2 %fusion.2 = (bf16[4,48,384]{2,1,0:T(8,128)(2,1)S(1)}, bf16[4,48,384]{2,1,0:T(8,128)(2,1)S(1)}, bf16[4,48,384]{2,1,0:T(8,128)(2,1)S(1)}, bf16[4,48,384]{2,1,0:T(8,128)(2,1)S(1)}) fusion(s32[]{:T(128)S(6)} %select_n.109, bf16[3,48,1536]{2,1,0:T(8,128)(2,1)} %param.7, bf16[1,48,1536]{2,1,0:T(8,128)(2,1)S(1)} %slice.129, s32[]{:T(128)S(6)} %select_n.111, ...), kind=kLoop, calls=%fused_computation.32 | loop fusion | flops 1179648 | bytes 1179664 | tf_op jit(solution)/shard_map/concatenate | solution.py:163
  3.0 3.1 %collective-permute-start = (bf16[4,48,384]{2,1,0:T(8,128)(2,1)S(1)}, bf16[4,48,384]{2,1,0:T(8,128)(2,1)S(1)}, u32[]{:S(2)}, u32[]{:S(2)}) collective-permute-start(bf16[4,48,384]{2,1,0:T(8,128)(2,1)S(1)} %get-tuple-element.35), channel_id=1, source_target_pairs={{0,4},{2,6},{4,8},{6,10},{8,12},{10,14},{12,0},{14,2},{1,5},{3,7},... | collective-permute-start | bytes 442376 | tf_op jit(solution)/shard_map/ppermute | solution.py:144
  6.1 2.6 %collective-permute-start.1 = (bf16[4,48,384]{2,1,0:T(8,128)(2,1)S(1)}, bf16[4,48,384]{2,1,0:T(8,128)(2,1)S(1)}, u32[]{:S(2)}, u32[]{:S(2)}) collective-permute-start(bf16[4,48,384]{2,1,0:T(8,128)(2,1)S(1)} %get-tuple-element.36), channel_id=1, source_target_pairs={{0,8},{2,10},{4,12},{6,14},{8,0},{10,2},{12,4},{14,6},{1,9},{3,11}... | collective-permute-start | bytes 442376 | tf_op jit(solution)/shard_map/ppermute | solution.py:144
  8.7 1.3 %collective-permute-start.2 = (bf16[4,48,384]{2,1,0:T(8,128)(2,1)S(1)}, bf16[4,48,384]{2,1,0:T(8,128)(2,1)S(1)}, u32[]{:S(2)}, u32[]{:S(2)}) collective-permute-start(bf16[4,48,384]{2,1,0:T(8,128)(2,1)S(1)} %get-tuple-element.37), channel_id=1, source_target_pairs={{0,12},{2,14},{4,0},{6,2},{8,4},{10,6},{12,8},{14,10},{1,13},{3,15... | collective-permute-start | bytes 442376 | tf_op jit(solution)/shard_map/ppermute | solution.py:144
  10.0 0.7 constant_dynamic-slice_fusion.1
  12.4 1.1 %maximum_select_fusion = bf16[2,48,1536]{2,1,0:T(8,128)(2,1)S(1)} fusion(bf16[2,48,768]{2,1,0:T(8,128)(2,1)} %collective-permute-done.4, bf16[2,48,768]{2,1,0:T(8,128)(2,1)S(1)} %get-tuple-element.40, pred[]{:T(512)S(6)} %eq.25), kind=kLoop, calls=%fused_computation.22 | loop fusion | flops 1327104 | bytes 589825 | tf_op jit(solution)/shard_map/jit(_where)/select_n | solution.py:159
  13.6 0.7 collective-permute-start.5
  14.3 5.9 %collective-permute-start.6 = (bf16[4,48,384]{2,1,0:T(8,128)(2,1)S(1)}, bf16[4,48,384]{2,1,0:T(8,128)(2,1)S(1)}, u32[]{:S(2)}, u32[]{:S(2)}) collective-permute-start(bf16[4,48,384]{2,1,0:T(8,128)(2,1)S(1)} %get-tuple-element.32), channel_id=1, source_target_pairs={{0,8},{2,10},{4,12},{6,14},{8,0},{10,2},{12,4},{14,6},{1,9},{3,11}... | collective-permute-start | bytes 442376 | tf_op jit(solution)/shard_map/ppermute | solution.py:144
  20.2 8.8 %collective-permute-start.7 = (bf16[4,48,384]{2,1,0:T(8,128)(2,1)S(1)}, bf16[4,48,384]{2,1,0:T(8,128)(2,1)S(1)}, u32[]{:S(2)}, u32[]{:S(2)}) collective-permute-start(bf16[4,48,384]{2,1,0:T(8,128)(2,1)S(1)} %get-tuple-element.33), channel_id=1, source_target_pairs={{0,12},{2,14},{4,0},{6,2},{8,4},{10,6},{12,8},{14,10},{1,13},{3,15... | collective-permute-start | bytes 442376 | tf_op jit(solution)/shard_map/ppermute | solution.py:144
  29.0 0.8 %fusion.12 = (bf16[1,192,384]{2,1,0:T(8,128)(2,1)S(1)}, bf16[1,192,384]{2,1,0:T(8,128)(2,1)S(1)}, bf16[192,384]{1,0:T(8,128)(2,1)}, bf16[192,384]{1,0:T(8,128)(2,1)}) fusion(bf16[4,192,384]{2,1,0:T(8,128)(2,1)S(1)} %pad_maximum_fusion), kind=kLoop, calls=%fused_computation.71 | loop fusion | bytes 1179648 | tf_op jit(solution)/shard_map/slice | solution.py:195
  29.9 1.1 %collective-permute-done.6 = bf16[4,48,384]{2,1,0:T(8,128)(2,1)S(1)} collective-permute-done((bf16[4,48,384]{2,1,0:T(8,128)(2,1)S(1)}, bf16[4,48,384]{2,1,0:T(8,128)(2,1)S(1)}, u32[]{:S(2)}, u32[]{:S(2)}) %collective-permute-start.6) | collective-permute-done | bytes 147488 | tf_op jit(solution)/shard_map/ppermute | solution.py:144
  31.0 0.7 collective-permute-done.7
  31.7 1.6 %collective-permute-start.9 = (bf16[4,192,384]{2,1,0:T(8,128)(2,1)S(1)}, bf16[4,192,384]{2,1,0:T(8,128)(2,1)S(1)}, u32[]{:S(2)}, u32[]{:S(2)}) collective-permute-start(bf16[4,192,384]{2,1,0:T(8,128)(2,1)S(1)} %pad_maximum_fusion.1), channel_id=1, source_target_pairs={{0,2},{2,0},{4,6},{6,4},{8,10},{10,8},{12,14},{14,12},{1,3},{3,1},... | collective-permute-start | bytes 1769480 | tf_op jit(solution)/shard_map/ppermute | solution.py:147
  33.3 0.8 %slice_bitcast_fusion.19 = (bf16[192,384]{1,0:T(8,128)(2,1)}, bf16[192,384]{1,0:T(8,128)(2,1)}, bf16[192,384]{1,0:T(8,128)(2,1)}, bf16[192,384]{1,0:T(8,128)(2,1...) fusion(bf16[4,192,384]{2,1,0:T(8,128)(2,1)S(1)} %pad_maximum_fusion.1), kind=kLoop, calls=%fused_computation.68 | loop fusion | bytes 1474560 | tf_op jit(solution)/shard_map/squeeze | solution.py:197
  34.2 0.9 %pad_maximum_fusion.4 = (bf16[2,192,384]{2,1,0:T(8,128)(2,1)}, bf16[2,192,384]{2,1,0:T(8,128)(2,1)}) fusion(bf16[1,192,384]{2,1,0:T(8,128)(2,1)S(1)} %get-tuple-element.39, bf16[1,192,384]{2,1,0:T(8,128)(2,1)S(1)} %get-tuple-element.27, bf16[1,192,384]{2,1,0:T(8,128)(2,1)S(1)} %get-tuple-element.38, bf16[1,192,384]{2,1,0:T(8,128)(2,1)S(1)} %get-tuple-element.26), kind=kLoop, calls=%fused_computation.25 | loop fusion | flops 294912 | bytes 1179648 | tf_op jit(solution)/shard_map/stack | solution.py:194
  35.2 0.9 %slice_bitcast_fusion = (bf16[256,384]{1,0:T(8,128)(2,1)}, bf16[256,384]{1,0:T(8,128)(2,1)}, bf16[256,384]{1,0:T(8,128)(2,1)}, bf16[256,384]{1,0:T(8,128)(2,1)}) fusion(bf16[4,256,384]{2,1,0:T(8,128)(2,1)S(1)} %broadcast_select_fusion), kind=kLoop, calls=%fused_computation.27 | loop fusion | bytes 1572864 | tf_op jit(solution)/shard_map/squeeze | solution.py:128
  36.1 10.2 %collective-permute-done.9 = bf16[4,192,384]{2,1,0:T(8,128)(2,1)S(1)} collective-permute-done((bf16[4,192,384]{2,1,0:T(8,128)(2,1)S(1)}, bf16[4,192,384]{2,1,0:T(8,128)(2,1)S(1)}, u32[]{:S(2)}, u32[]{:S(2)}) %collective-permute-start.9) | collective-permute-done | bytes 589856 | tf_op jit(solution)/shard_map/ppermute | solution.py:147
  46.3 0.9 %slice_bitcast_fusion.18 = (bf16[192,384]{1,0:T(8,128)(2,1)}, bf16[192,384]{1,0:T(8,128)(2,1)}, bf16[192,384]{1,0:T(8,128)(2,1)}, bf16[192,384]{1,0:T(8,128)(2,1...) fusion(bf16[4,192,384]{2,1,0:T(8,128)(2,1)S(1)} %collective-permute-done.8), kind=kLoop, calls=%fused_computation.67 | loop fusion | bytes 1474560 | tf_op jit(solution)/shard_map/squeeze | solution.py:197
  47.2 0.9 %pad_maximum_fusion.2 = (bf16[2,192,384]{2,1,0:T(8,128)(2,1)}, bf16[2,192,384]{2,1,0:T(8,128)(2,1)}) fusion(bf16[1,192,384]{2,1,0:T(8,128)(2,1)S(1)} %get-tuple-element.19, bf16[1,192,384]{2,1,0:T(8,128)(2,1)S(1)} %get-tuple-element.25, bf16[1,192,384]{2,1,0:T(8,128)(2,1)S(1)} %get-tuple-element.18, bf16[1,192,384]{2,1,0:T(8,128)(2,1)S(1)} %get-tuple-element.24), kind=kLoop, calls=%fused_computation.23 | loop fusion | flops 294912 | bytes 1179648 | tf_op jit(solution)/shard_map/stack | solution.py:184
  48.1 0.9 %slice_bitcast_fusion.5 = (bf16[192,384]{1,0:T(8,128)(2,1)}, bf16[192,384]{1,0:T(8,128)(2,1)}, bf16[192,384]{1,0:T(8,128)(2,1)}, bf16[192,384]{1,0:T(8,128)(2,1)}) fusion(bf16[4,192,384]{2,1,0:T(8,128)(2,1)S(1)} %collective-permute-done.9), kind=kLoop, calls=%fused_computation.40 | loop fusion | bytes 1179648 | tf_op jit(solution)/shard_map/squeeze | solution.py:197
  49.0 0.8 %slice_bitcast_fusion.4 = (bf16[192,384]{1,0:T(8,128)(2,1)}, bf16[192,384]{1,0:T(8,128)(2,1)}, bf16[192,384]{1,0:T(8,128)(2,1)}, bf16[192,384]{1,0:T(8,128)(2,1)}) fusion(bf16[4,192,384]{2,1,0:T(8,128)(2,1)S(1)} %collective-permute-done.10), kind=kLoop, calls=%fused_computation.39 | loop fusion | bytes 1179648 | tf_op jit(solution)/shard_map/squeeze | solution.py:197
  50.4 4.6 %shard_map.78 = bf16[192,384]{1,0:T(8,128)(2,1)} custom-call(f32[2,3]{1,0:T(2,128)} %broadcast_4_scale_ref.2.scale_ref, bf16[192,384]{1,0:T(8,128)(2,1)} %get-tuple-element.28.q_ref, bf16[256,384]{1,0:T(8,128)(2,1)} %get-tuple-element.3.tk_ref, bf16[256,384]{1,0:T(8,128)(2,1)} %get-tuple-element.2.tv_ref, bf16[2,192,384]{2,1,0:T(8,128)(2,1)} %get-tuple-element.50.ok_ref, ...), custom_call_target="tpu_custom_call" | custom-call | flops 301989888 | bytes 2162688 | tf_op jit(solution)/shard_map/pallas_call | solution.py:119
  55.0 0.9 %fusion.14 = (bf16[48,384]{1,0:T(8,128)(2,1)S(1)}, bf16[48,384]{1,0:T(8,128)(2,1)S(1)}, bf16[48,384]{1,0:T(8,128)(2,1)S(1)}, bf16[48,1536]{1,0:T(8,128)(2,1)S(1)}) fusion(bf16[192,384]{1,0:T(8,128)(2,1)} %shard_map.78, bf16[48,1536]{1,0:T(8,128)(2,1)S(1)} %broadcast.12.clone.1, s32[]{:T(128)S(6)} %select_n.109), kind=kLoop, calls=%fused_computation.73 | loop fusion | bytes 294916 | tf_op jit(solution)/shard_map/slice | solution.py:205
  55.8 2.2 %collective-permute-start.15 = (bf16[48,384]{1,0:T(8,128)(2,1)S(1)}, bf16[48,384]{1,0:T(8,128)(2,1)S(1)}, u32[]{:S(2)}, u32[]{:S(2)}) collective-permute-start(bf16[48,384]{1,0:T(8,128)(2,1)S(1)} %get-tuple-element.44), channel_id=1, source_target_pairs={{0,12},{2,14},{4,0},{6,2},{8,4},{10,6},{12,8},{14,10},{1,13},{3,15... | collective-permute-start | bytes 110600 | tf_op jit(solution)/shard_map/ppermute | solution.py:144
  58.1 3.0 %collective-permute-start.16 = (bf16[48,384]{1,0:T(8,128)(2,1)S(1)}, bf16[48,384]{1,0:T(8,128)(2,1)S(1)}, u32[]{:S(2)}, u32[]{:S(2)}) collective-permute-start(bf16[48,384]{1,0:T(8,128)(2,1)S(1)} %get-tuple-element.43), channel_id=1, source_target_pairs={{0,8},{2,10},{4,12},{6,14},{8,0},{10,2},{12,4},{14,6},{1,9},{3,11}... | collective-permute-start | bytes 110600 | tf_op jit(solution)/shard_map/ppermute | solution.py:144
  61.1 4.6 %shard_map.77 = bf16[192,384]{1,0:T(8,128)(2,1)} custom-call(f32[2,3]{1,0:T(2,128)} %fusion.11.scale_ref, bf16[192,384]{1,0:T(8,128)(2,1)} %get-tuple-element.29.q_ref, bf16[256,384]{1,0:T(8,128)(2,1)} %get-tuple-element.5.tk_ref, bf16[256,384]{1,0:T(8,128)(2,1)} %get-tuple-element.4.tv_ref, bf16[2,192,384]{2,1,0:T(8,128)(2,1)} %get-tuple-element.52.ok_ref, ...), custom_call_target="tpu_custom_call" | custom-call | flops 301989888 | bytes 2162688 | tf_op jit(solution)/shard_map/pallas_call | solution.py:119
  65.7 0.9 %fusion.15 = (bf16[48,384]{1,0:T(8,128)(2,1)S(1)}, bf16[48,384]{1,0:T(8,128)(2,1)S(1)}, bf16[48,384]{1,0:T(8,128)(2,1)S(1)}, bf16[48,1536]{1,0:T(8,128)(2,1)S(1)}) fusion(bf16[192,384]{1,0:T(8,128)(2,1)} %shard_map.77, bf16[48,1536]{1,0:T(8,128)(2,1)S(1)} %broadcast.12.clone, s32[]{:T(128)S(6)} %select_n.109), kind=kLoop, calls=%fused_computation.74 | loop fusion | bytes 294916 | tf_op jit(solution)/shard_map/slice | solution.py:205
  66.5 3.9 %collective-permute-start.11 = (bf16[48,384]{1,0:T(8,128)(2,1)S(1)}, bf16[48,384]{1,0:T(8,128)(2,1)S(1)}, u32[]{:S(2)}, u32[]{:S(2)}) collective-permute-start(bf16[48,384]{1,0:T(8,128)(2,1)S(1)} %get-tuple-element.48), channel_id=1, source_target_pairs={{0,12},{2,14},{4,0},{6,2},{8,4},{10,6},{12,8},{14,10},{1,13},{3,15... | collective-permute-start | bytes 110600 | tf_op jit(solution)/shard_map/ppermute | solution.py:144
  71.1 0.9 %collective-permute-done.11 = bf16[48,384]{1,0:T(8,128)(2,1)S(1)} collective-permute-done((bf16[48,384]{1,0:T(8,128)(2,1)S(1)}, bf16[48,384]{1,0:T(8,128)(2,1)S(1)}, u32[]{:S(2)}, u32[]{:S(2)}) %collective-permute-start.11) | collective-permute-done | bytes 36896 | tf_op jit(solution)/shard_map/ppermute | solution.py:144
  72.1 3.2 %collective-permute-done.12 = bf16[48,384]{1,0:T(8,128)(2,1)S(1)} collective-permute-done((bf16[48,384]{1,0:T(8,128)(2,1)S(1)}, bf16[48,384]{1,0:T(8,128)(2,1)S(1)}, u32[]{:S(2)}, u32[]{:S(2)}) %collective-permute-start.12) | collective-permute-done | bytes 36896 | tf_op jit(solution)/shard_map/ppermute | solution.py:144
  75.3 0.9 %collective-permute-done.13 = bf16[48,384]{1,0:T(8,128)(2,1)S(1)} collective-permute-done((bf16[48,384]{1,0:T(8,128)(2,1)S(1)}, bf16[48,384]{1,0:T(8,128)(2,1)S(1)}, u32[]{:S(2)}, u32[]{:S(2)}) %collective-permute-start.13) | collective-permute-done | bytes 36896 | tf_op jit(solution)/shard_map/ppermute | solution.py:144
  (51 shorter events, 4.2 us)
Async XLA Ops:
  0.7 9.3 %copy-start.2 = (bf16[2,96,768]{2,1,0:T(8,128)(2,1)S(1)}, bf16[2,96,768]{2,1,0:T(8,128)(2,1)}, u32[]{:S(2)}) copy-start(bf16[2,96,768]{2,1,0:T(8,128)(2,1)} %param.8) | copy-start | bytes 884740
  1.7 9.0 %copy-start = (bf16[2,256,768]{2,1,0:T(8,128)(2,1)S(1)}, bf16[2,256,768]{2,1,0:T(8,128)(2,1)}, u32[]{:S(2)}) copy-start(bf16[2,256,768]{2,1,0:T(8,128)(2,1)} %param.10) | copy-start | bytes 2359300
  1.7 9.0 %copy-start.1 = (bf16[2,256,768]{2,1,0:T(8,128)(2,1)S(1)}, bf16[2,256,768]{2,1,0:T(8,128)(2,1)}, u32[]{:S(2)}) copy-start(bf16[2,256,768]{2,1,0:T(8,128)(2,1)} %param.11) | copy-start | bytes 2359300
  3.0 11.3 %collective-permute-start = (bf16[4,48,384]{2,1,0:T(8,128)(2,1)S(1)}, bf16[4,48,384]{2,1,0:T(8,128)(2,1)S(1)}, u32[]{:S(2)}, u32[]{:S(2)}) collective-permute-start(bf16[4,48,384]{2,1,0:T(8,128)(2,1)S(1)} %get-tuple-element.35), channel_id=1, source_target_pairs={{0,4},{2,6},{4,8},{6,10},{8,12},{10,14},{12,0},{14,2},{1,5},{3,7},... | collective-permute-start | bytes 442376 | tf_op jit(solution)/shard_map/ppermute | solution.py:144
  6.1 14.1 %collective-permute-start.1 = (bf16[4,48,384]{2,1,0:T(8,128)(2,1)S(1)}, bf16[4,48,384]{2,1,0:T(8,128)(2,1)S(1)}, u32[]{:S(2)}, u32[]{:S(2)}) collective-permute-start(bf16[4,48,384]{2,1,0:T(8,128)(2,1)S(1)} %get-tuple-element.36), channel_id=1, source_target_pairs={{0,8},{2,10},{4,12},{6,14},{8,0},{10,2},{12,4},{14,6},{1,9},{3,11}... | collective-permute-start | bytes 442376 | tf_op jit(solution)/shard_map/ppermute | solution.py:144
  8.7 20.3 %collective-permute-start.2 = (bf16[4,48,384]{2,1,0:T(8,128)(2,1)S(1)}, bf16[4,48,384]{2,1,0:T(8,128)(2,1)S(1)}, u32[]{:S(2)}, u32[]{:S(2)}) collective-permute-start(bf16[4,48,384]{2,1,0:T(8,128)(2,1)S(1)} %get-tuple-element.37), channel_id=1, source_target_pairs={{0,12},{2,14},{4,0},{6,2},{8,4},{10,6},{12,8},{14,10},{1,13},{3,15... | collective-permute-start | bytes 442376 | tf_op jit(solution)/shard_map/ppermute | solution.py:144
  10.7 1.7 %collective-permute-start.4 = (bf16[2,48,768]{2,1,0:T(8,128)(2,1)}, bf16[2,48,768]{2,1,0:T(8,128)(2,1)}, u32[]{:S(2)}, u32[]{:S(2)}) collective-permute-start(bf16[2,48,768]{2,1,0:T(8,128)(2,1)} %get-tuple-element.41), channel_id=1, source_target_pairs={{0,1},{1,0},{2,3},{3,2},{4,5},{5,4},{6,7},{7,6},{8,9},{9,8},{10,11... | collective-permute-start | bytes 442376 | tf_op jit(solution)/shard_map/ppermute | solution.py:150
  10.7 1.0 %copy-start.5 = (s32[2,12]{1,0:T(2,128)S(1)}, s32[2,12]{1,0:T(2,128)}, u32[]{:S(2)}) copy-start(s32[2,12]{1,0:T(2,128)} %param.9) | copy-start | bytes 292
  11.1 2.4 %slice-start = ((bf16[3,48,1536]{2,1,0:T(8,128)(2,1)}), bf16[2,48,1536]{2,1,0:T(8,128)(2,1)S(1)}, s32[]{:S(2)}) async-start(bf16[3,48,1536]{2,1,0:T(8,128)(2,1)} %param.6), calls=%async_computation | async-start | bytes 589824 | tf_op jit(solution)/shard_map/slice | solution.py:161
  11.1 24.0 %collective-permute-start.3 = (bf16[4,256,384]{2,1,0:T(8,128)(2,1)S(1)}, bf16[4,256,384]{2,1,0:T(8,128)(2,1)S(1)}, u32[]{:S(2)}, u32[]{:S(2)}) collective-permute-start(bf16[4,256,384]{2,1,0:T(8,128)(2,1)S(1)} %fusion), channel_id=1, source_target_pairs={{0,1},{1,0},{2,3},{3,2},{4,5},{5,4},{6,7},{7,6},{8,9},{9,8},{10,11... | collective-permute-start | bytes 2359304 | tf_op jit(solution)/shard_map/ppermute | solution.py:150
  13.6 16.4 %collective-permute-start.5 = (bf16[4,48,384]{2,1,0:T(8,128)(2,1)S(1)}, bf16[4,48,384]{2,1,0:T(8,128)(2,1)S(1)}, u32[]{:S(2)}, u32[]{:S(2)}) collective-permute-start(bf16[4,48,384]{2,1,0:T(8,128)(2,1)S(1)} %get-tuple-element.31), channel_id=1, source_target_pairs={{0,4},{2,6},{4,8},{6,10},{8,12},{10,14},{12,0},{14,2},{1,5},{3,7},... | collective-permute-start | bytes 442376 | tf_op jit(solution)/shard_map/ppermute | solution.py:144
  14.3 16.7 %collective-permute-start.6 = (bf16[4,48,384]{2,1,0:T(8,128)(2,1)S(1)}, bf16[4,48,384]{2,1,0:T(8,128)(2,1)S(1)}, u32[]{:S(2)}, u32[]{:S(2)}) collective-permute-start(bf16[4,48,384]{2,1,0:T(8,128)(2,1)S(1)} %get-tuple-element.32), channel_id=1, source_target_pairs={{0,8},{2,10},{4,12},{6,14},{8,0},{10,2},{12,4},{14,6},{1,9},{3,11}... | collective-permute-start | bytes 442376 | tf_op jit(solution)/shard_map/ppermute | solution.py:144
  20.2 11.5 %collective-permute-start.7 = (bf16[4,48,384]{2,1,0:T(8,128)(2,1)S(1)}, bf16[4,48,384]{2,1,0:T(8,128)(2,1)S(1)}, u32[]{:S(2)}, u32[]{:S(2)}) collective-permute-start(bf16[4,48,384]{2,1,0:T(8,128)(2,1)S(1)} %get-tuple-element.33), channel_id=1, source_target_pairs={{0,12},{2,14},{4,0},{6,2},{8,4},{10,6},{12,8},{14,10},{1,13},{3,15... | collective-permute-start | bytes 442376 | tf_op jit(solution)/shard_map/ppermute | solution.py:144
  29.9 4.3 %collective-permute-start.14 = (bf16[2,192,384]{2,1,0:T(8,128)(2,1)S(1)}, bf16[2,192,384]{2,1,0:T(8,128)(2,1)S(1)}, u32[]{:S(2)}, u32[]{:S(2)}) collective-permute-start(bf16[2,192,384]{2,1,0:T(8,128)(2,1)S(1)} %slice.189), channel_id=1, source_target_pairs={{0,1},{1,0},{2,3},{3,2},{4,5},{5,4},{6,7},{7,6},{8,9},{9,8},{10,11... | collective-permute-start | bytes 884744 | tf_op jit(solution)/shard_map/ppermute | solution.py:150
  31.7 14.6 %collective-permute-start.9 = (bf16[4,192,384]{2,1,0:T(8,128)(2,1)S(1)}, bf16[4,192,384]{2,1,0:T(8,128)(2,1)S(1)}, u32[]{:S(2)}, u32[]{:S(2)}) collective-permute-start(bf16[4,192,384]{2,1,0:T(8,128)(2,1)S(1)} %pad_maximum_fusion.1), channel_id=1, source_target_pairs={{0,2},{2,0},{4,6},{6,4},{8,10},{10,8},{12,14},{14,12},{1,3},{3,1},... | collective-permute-start | bytes 1769480 | tf_op jit(solution)/shard_map/ppermute | solution.py:147
  33.3 13.0 %collective-permute-start.8 = (bf16[4,192,384]{2,1,0:T(8,128)(2,1)S(1)}, bf16[4,192,384]{2,1,0:T(8,128)(2,1)S(1)}, u32[]{:S(2)}, u32[]{:S(2)}) collective-permute-start(bf16[4,192,384]{2,1,0:T(8,128)(2,1)S(1)} %pad_maximum_fusion.1), channel_id=1, source_target_pairs={{0,1},{1,0},{2,3},{3,2},{4,5},{5,4},{6,7},{7,6},{8,9},{9,8},{10,11... | collective-permute-start | bytes 1769480 | tf_op jit(solution)/shard_map/ppermute | solution.py:150
  46.3 2.7 %collective-permute-start.10 = (bf16[4,192,384]{2,1,0:T(8,128)(2,1)S(1)}, bf16[4,192,384]{2,1,0:T(8,128)(2,1)S(1)}, u32[]{:S(2)}, u32[]{:S(2)}) collective-permute-start(bf16[4,192,384]{2,1,0:T(8,128)(2,1)S(1)} %collective-permute-done.9), channel_id=1, source_target_pairs={{0,1},{1,0},{2,3},{3,2},{4,5},{5,4},{6,7},{7,6},{8,9},{9,8},{10,11... | collective-permute-start | bytes 1769480 | tf_op jit(solution)/shard_map/ppermute | solution.py:150
  55.8 14.6 %collective-permute-start.15 = (bf16[48,384]{1,0:T(8,128)(2,1)S(1)}, bf16[48,384]{1,0:T(8,128)(2,1)S(1)}, u32[]{:S(2)}, u32[]{:S(2)}) collective-permute-start(bf16[48,384]{1,0:T(8,128)(2,1)S(1)} %get-tuple-element.44), channel_id=1, source_target_pairs={{0,12},{2,14},{4,0},{6,2},{8,4},{10,6},{12,8},{14,10},{1,13},{3,15... | collective-permute-start | bytes 110600 | tf_op jit(solution)/shard_map/ppermute | solution.py:144
  58.1 13.0 %collective-permute-start.16 = (bf16[48,384]{1,0:T(8,128)(2,1)S(1)}, bf16[48,384]{1,0:T(8,128)(2,1)S(1)}, u32[]{:S(2)}, u32[]{:S(2)}) collective-permute-start(bf16[48,384]{1,0:T(8,128)(2,1)S(1)} %get-tuple-element.43), channel_id=1, source_target_pairs={{0,8},{2,10},{4,12},{6,14},{8,0},{10,2},{12,4},{14,6},{1,9},{3,11}... | collective-permute-start | bytes 110600 | tf_op jit(solution)/shard_map/ppermute | solution.py:144
  61.1 10.0 %collective-permute-start.17 = (bf16[48,384]{1,0:T(8,128)(2,1)S(1)}, bf16[48,384]{1,0:T(8,128)(2,1)S(1)}, u32[]{:S(2)}, u32[]{:S(2)}) collective-permute-start(bf16[48,384]{1,0:T(8,128)(2,1)S(1)} %get-tuple-element.42), channel_id=1, source_target_pairs={{0,4},{2,6},{4,8},{6,10},{8,12},{10,14},{12,0},{14,2},{1,5},{3,7},... | collective-permute-start | bytes 110600 | tf_op jit(solution)/shard_map/ppermute | solution.py:144
  66.5 5.5 %collective-permute-start.11 = (bf16[48,384]{1,0:T(8,128)(2,1)S(1)}, bf16[48,384]{1,0:T(8,128)(2,1)S(1)}, u32[]{:S(2)}, u32[]{:S(2)}) collective-permute-start(bf16[48,384]{1,0:T(8,128)(2,1)S(1)} %get-tuple-element.48), channel_id=1, source_target_pairs={{0,12},{2,14},{4,0},{6,2},{8,4},{10,6},{12,8},{14,10},{1,13},{3,15... | collective-permute-start | bytes 110600 | tf_op jit(solution)/shard_map/ppermute | solution.py:144
  70.4 4.9 %collective-permute-start.12 = (bf16[48,384]{1,0:T(8,128)(2,1)S(1)}, bf16[48,384]{1,0:T(8,128)(2,1)S(1)}, u32[]{:S(2)}, u32[]{:S(2)}) collective-permute-start(bf16[48,384]{1,0:T(8,128)(2,1)S(1)} %get-tuple-element.47), channel_id=1, source_target_pairs={{0,8},{2,10},{4,12},{6,14},{8,0},{10,2},{12,4},{14,6},{1,9},{3,11}... | collective-permute-start | bytes 110600 | tf_op jit(solution)/shard_map/ppermute | solution.py:144
  70.4 5.8 %collective-permute-start.13 = (bf16[48,384]{1,0:T(8,128)(2,1)S(1)}, bf16[48,384]{1,0:T(8,128)(2,1)S(1)}, u32[]{:S(2)}, u32[]{:S(2)}) collective-permute-start(bf16[48,384]{1,0:T(8,128)(2,1)S(1)} %get-tuple-element.46), channel_id=1, source_target_pairs={{0,4},{2,6},{4,8},{6,10},{8,12},{10,14},{12,0},{14,2},{1,5},{3,7},... | collective-permute-start | bytes 110600 | tf_op jit(solution)/shard_map/ppermute | solution.py:144
  71.1 5.1 %copy-start.4 = (bf16[48,1536]{1,0:T(8,128)(2,1)}, bf16[48,1536]{1,0:T(8,128)(2,1)S(1)}, u32[]{:S(2)}) copy-start(bf16[48,1536]{1,0:T(8,128)(2,1)S(1)} %constant_dynamic-update-slice_fusion) | copy-start | bytes 442372
  76.2 0.7 copy-start.3

commit v2 on v1

v2 whole, which is shorter than its diff:
```python
import functools

import jax
import jax.numpy as jnp
from jax import lax
from jax.experimental import pallas as pl
from jax.experimental.pallas import tpu as pltpu
from jax.sharding import PartitionSpec as P

HEAD = 128
COLUMNS = 2
BF16 = jnp.bfloat16
F32 = jnp.float32


def heads_view(array):
    return array.reshape(array.shape[0], array.shape[1] // HEAD, HEAD)


def absorb(carry, queries, keys_rows, values, key_scale, value_scale, keep):
    top, total, accum = carry
    inverse = 1.0 / HEAD**0.5
    score = jnp.einsum("qhd,khd->hqk", queries, keys_rows, preferred_element_type=F32)
    score = score * (key_scale * inverse)[:, None, None]
    if keep is not None:
        score = jnp.where(keep[None, None, :], score, -jnp.inf)
    new_top = jnp.maximum(top, score.max(-1))
    fade = jnp.exp(top - new_top)
    weight = jnp.exp(score - new_top[:, :, None])
    total = total * fade + weight.sum(-1)
    addend = jnp.einsum("hqk,khd->qhd", weight.astype(BF16), values, preferred_element_type=F32)
    accum = accum * fade.T[:, :, None] + addend * value_scale[None, :, None]
    return (new_top, total, accum)


def general_step(mine, text, far, keep, key_scale, value_scale):
    queries = heads_view(mine[0])
    rows, local_heads = queries.shape[:2]
    unit = jnp.ones((local_heads,), F32)
    carry = (
        jnp.full((local_heads, rows), -jnp.inf, F32),
        jnp.zeros((local_heads, rows), F32),
        jnp.zeros((rows, local_heads, HEAD), F32),
    )
    carry = absorb(carry, queries, heads_view(text[0]), heads_view(text[1]), unit, unit, None)
    carry = absorb(carry, queries, heads_view(mine[1]), heads_view(mine[2]), unit, unit, None)
    carry = absorb(carry, queries, heads_view(far[0]), heads_view(far[1]), key_scale, value_scale, keep)
    top, total, accum = carry
    result = (accum / total.T[:, :, None]).reshape(rows, local_heads * HEAD).astype(BF16)
    return lax.all_to_all(result, "uly", split_axis=0, concat_axis=1, tiled=True)


def general_shards(fresh_first, fresh_second, stale_cache, stale_exponent, text_first, text_second):
    local_heads = stale_exponent.shape[1] // lax.axis_size("uly")
    first_head = lax.axis_index("uly") * local_heads
    exponents = lax.dynamic_slice_in_dim(stale_exponent, first_head, local_heads, 1)
    scales = jnp.exp2(exponents.astype(F32))
    unit = jnp.ones((local_heads,), F32)
    mine_first = lax.all_to_all(fresh_first, "uly", split_axis=2, concat_axis=1, tiled=True)
    mine_second = lax.all_to_all(fresh_second, "uly", split_axis=2, concat_axis=1, tiled=True)
    rows = mine_first.shape[1]
    own_start = lax.axis_index("patch") * rows
    stale = lax.all_gather(stale_cache, "patch", axis=1, tiled=True)
    refreshed = lax.all_gather(mine_first[1:], "patch", axis=1, tiled=True)
    places = jnp.arange(stale.shape[1], dtype=jnp.int32)
    keep = (places < own_start) | (places >= own_start + rows)
    return (
        general_step(mine_first, text_first, stale, keep, scales[0], scales[1]),
        general_step(mine_second, text_second, refreshed, keep, unit, unit),
    )


def dot_t(a, b):
    return lax.dot_general(a, b, (((1,), (1,)), ((), ())), preferred_element_type=F32)


def dot(a, b):
    return jnp.dot(a, b, preferred_element_type=F32)


def attend(q, text, own, near, away, inside, key_factor, value_factor):
    inverse = 1.0 / HEAD**0.5
    scores = [
        dot_t(q, text[0]) * inverse,
        jnp.where(inside, dot_t(q, own[0]) * inverse, dot_t(q, near[0]) * key_factor),
        dot_t(q, away[0]) * key_factor,
    ]
    top = functools.reduce(jnp.maximum, [s.max(-1, keepdims=True) for s in scores])
    weights = [jnp.exp(s - top) for s in scores]
    total = functools.reduce(jnp.add, [w.sum(-1, keepdims=True) for w in weights])
    w_text, w_near, w_away = [w.astype(BF16) for w in weights]
    zero = jnp.zeros((), BF16)
    kept = dot(w_text, text[1]) + dot(jnp.where(inside, w_near, zero), own[1])
    far = dot(jnp.where(inside, zero, w_near), near[1]) + dot(w_away, away[1])
    return (kept + value_factor * far) / total


def store_blocks(out_refs, result, lanes):
    rows = out_refs[0].shape[0]
    for i, out_ref in enumerate(out_refs):
        out_ref[:, lanes] = result[i * rows : (i + 1) * rows].astype(BF16)


def first_kernel(scale_ref, order_ref, q_ref, text_ref, own_ref, twin_ref, near_ref, other_ref, away_ref, away_twin_ref, *out_refs):
    count, width = q_ref.shape
    layers, rows = len(out_refs), out_refs[0].shape[0]
    shape = (count, 2 * count)
    inside = (
        lax.broadcasted_iota(jnp.int32, shape, 0) // rows == lax.broadcasted_iota(jnp.int32, shape, 1) // (2 * rows)
    )
    for head in range(width // HEAD):
        lanes = slice(head * HEAD, (head + 1) * HEAD)

        def own(i):
            cut = [slice(s * rows, (s + 1) * rows) for s in range(layers)]
            return jnp.concatenate([r[i, c, lanes] for c in cut for r in (own_ref, twin_ref)], 0)

        def near(i):
            blocks = []
            for s in range(layers):
                place = order_ref[1, s]
                mine, other = near_ref[place, i, :, lanes], other_ref[place, i, :, lanes]
                blocks.append(jnp.where(order_ref[0, s] == 0, mine, other))
            return jnp.concatenate(blocks, 0)

        def away(i):
            return jnp.concatenate([r[k, i, :, lanes] for r in (away_ref, away_twin_ref) for k in range(layers // 2)], 0)

        result = attend(
            q_ref[:, lanes],
            (text_ref[0, :, lanes], text_ref[1, :, lanes]),
            (own(0), own(1)),
            (near(0), near(1)),
            (away(0), away(1)),
            inside,
            scale_ref[0, head] * (1.0 / HEAD**0.5),
            scale_ref[1, head],
        )
        store_blocks(out_refs, result, lanes)


def second_kernel(q_ref, text_ref, own_ref, own_twin_ref, near_ref, near_twin_ref, away_ref, away_twin_ref, *out_refs):
    count, width = q_ref.shape
    rows = out_refs[0].shape[0]
    shape = (count, 2 * count)
    inside = (
        lax.broadcasted_iota(jnp.int32, shape, 0) // rows
        == lax.broadcasted_iota(jnp.int32, shape, 1) % count // rows
    )
    for head in range(width // HEAD):
        lanes = slice(head * HEAD, (head + 1) * HEAD)

        def pair(a, b):
            return tuple(jnp.concatenate([a[i, :, lanes], b[i, :, lanes]], 0) for i in range(2))

        result = attend(
            q_ref[:, lanes],
            (text_ref[2, :, lanes], text_ref[3, :, lanes]),
            pair(own_ref, own_twin_ref),
            pair(near_ref, near_twin_ref),
            pair(away_ref, away_twin_ref),
            inside,
            1.0 / HEAD**0.5,
            1.0,
        )
        store_blocks(out_refs, result, lanes)


def call_attention(kernel, layers, scalars, q, text, *others):
    count, width = q.shape
    keys = text.shape[1] + 4 * count
    in_vmem = pl.BlockSpec(memory_space=pltpu.VMEM)
    return pl.pallas_call(
        kernel,
        out_shape=[jax.ShapeDtypeStruct((count // layers, width), BF16)] * layers,
        in_specs=[pl.BlockSpec(memory_space=pltpu.SMEM)] * len(scalars) + [in_vmem] * (2 + len(others)),
        out_specs=[in_vmem] * layers,
        compiler_params=pltpu.CompilerParams(vmem_limit_bytes=32 * 1024 * 1024),
        cost_estimate=pl.CostEstimate(
            flops=4 * count * keys * width, bytes_accessed=4 * width * (keys + count), transcendentals=count * keys * width // HEAD
        ),
    )(*scalars, q, text, *others)


def layered_shards(layers, fresh_first, fresh_second, stale_cache, stale_exponent, text_first, text_second):
    core = lax.axis_index("uly")
    layer = lax.axis_index("patch") // COLUMNS
    rows, features = fresh_first.shape[1:]
    width = features // layers
    heads = width // HEAD
    half = features // 2
    rounds = layers // 2

    def layer_shift(x, shift):
        pairs = [
            (z * COLUMNS + y, (z + shift) % layers * COLUMNS + y) for z in range(layers) for y in range(COLUMNS)
        ]
        return lax.ppermute(x, "patch", pairs)

    def stale_round(x, k):
        pairs = []
        for z in range(layers):
            for y in range(COLUMNS):
                for u in range(2):
                    to = (u * rounds + (z + k) % rounds) * COLUMNS + y
                    pairs.append(((z * COLUMNS + y) * 2 + u, to * 2 + z // rounds))
        return lax.ppermute(x, ("patch", "uly"), pairs)

    def other_column(x):
        return lax.ppermute(x, "patch", [(p, p ^ 1) for p in range(layers * COLUMNS)])

    def other_core(x):
        return lax.ppermute(x, "uly", [(0, 1), (1, 0)])

    def columns_of(x, index):
        return lax.dynamic_slice_in_dim(x, index * width, width, x.ndim - 1)

    def over_layers(x):
        sends = [columns_of(x, (layer + s) % layers) for s in range(layers)]
        return sends[:1] + [layer_shift(sends[s], s) for s in range(1, layers)]

    stale = jnp.stack([stale_round(columns_of(stale_cache, (layer + k) % rounds), k) for k in range(rounds)])
    stale_away = other_column(stale)
    stale_twin = other_core(stale)
    stale_away_twin = other_core(stale_away)
    source = [(layer - s) % layers for s in range(layers)]
    order = jnp.stack(
        [jnp.stack([(L // rounds != core).astype(jnp.int32) for L in source]), jnp.stack([(L - layer) % rounds for L in source])]
    )

    first = over_layers(fresh_first)
    query_first = jnp.concatenate([p[0] for p in first], 0)
    fresh = jnp.concatenate([p[1:] for p in first], 1)
    fresh_away = other_column(fresh)
    fresh_twin = other_core(fresh)
    fresh_away_twin = other_core(fresh_away)

    second = over_layers(fresh_second)
    query_second = jnp.concatenate([p[0] for p in second], 0)
    last = jnp.concatenate([p[1:] for p in second], 1)
    last_twin = other_core(last)

    text = jnp.concatenate([text_first, text_second], 0)
    text = lax.dynamic_slice_in_dim(text, layer * width % half, width, 2)
    text = jnp.where(core == layer * width // half, text, other_core(text))

    scales = jnp.exp2(lax.dynamic_slice_in_dim(stale_exponent, layer * heads, heads, 1).astype(F32))
    first_blocks = call_attention(
        first_kernel, layers, [scales, order], query_first, text, fresh, fresh_twin, stale, stale_twin, stale_away, stale_away_twin
    )
    second_blocks = call_attention(
        second_kernel, layers, [], query_second, text, last, last_twin, fresh, fresh_twin, fresh_away, fresh_away_twin
    )

    def back(blocks):
        out = jnp.zeros((rows, features), BF16)
        for s in range(layers):
            block = blocks[s] if s == 0 else layer_shift(blocks[s], -s)
            out = lax.dynamic_update_slice_in_dim(out, block, (layer + s) % layers * width, 1)
        return out

    return back(first_blocks), back(second_blocks)


def solution(mesh):
    placed = (
        P(None, ("group", "patch", "uly"), None),
        P(None, ("group", "patch", "uly"), None),
        P(None, ("group", "patch"), "uly"),
        P("group", None),
        P(None, "group", "uly"),
        P(None, "group", "uly"),
    )

    def shards(*arrays):
        layers = mesh.shape["patch"] // COLUMNS
        heads = arrays[0].shape[2] // HEAD
        if mesh.shape["uly"] == 2 and layers % 2 == 0 and heads % layers == 0:
            return layered_shards(layers, *arrays)
        return general_shards(*arrays)

    return jax.shard_map(
        shards,
        mesh=mesh,
        in_specs=placed,
        out_specs=(P(("group", "patch", "uly"), None), P(("group", "patch", "uly"), None)),
        check_vma=False,
    )
```

time: 77.4 us -> 67.1 us (0.87)
  waiting for transfers between devices: 17 us -> 24.1 us
  local copies, waits for them, and re-layouts: 9.91 us -> 4.45 us
  Pallas kernels: 9.17 us -> 4.1 us
  other arithmetic: 5.43 us -> 1.92 us
  starting transfers between devices: 34.4 us -> 31.1 us
    ppermute x12, starting transfers between devices: 32.2 us -> 25 us  [layer_shift(): return lax.ppermute(x, 'patch', pairs)]
    pallas_call x2, Pallas kernels: 9.17 us -> 4.1 us  [call_attention(): pl.pallas_call(kernel, out_shape=[jax.ShapeDtypeStruct((count // layers,...]
    ppermute x12, waiting for transfers between devices: 6.74 us -> 11.5 us  [layer_shift(): return lax.ppermute(x, 'patch', pairs)]
    squeeze x5 -> x8, local copies, waits for them, and re-layouts: 4.35 us -> 0.81 us  [the longest x4 0.79 us: layered_shards(): query_first = jnp.concatenate([p[0] for p in first], 0)]
    ppermute x0 -> x2, starting transfers between devices: none -> 3.18 us  [stale_round(): return lax.ppermute(x, ('patch', 'uly'), pairs)]
    slice x8, local copies, waits for them, and re-layouts: 3.5 us -> 0.95 us  [the longest x4 0.92 us: layered_shards(): fresh = jnp.concatenate([p[1:] for p in first], 1)]
    ppermute x1 -> x2, waiting for transfers between devices: 10.2 us -> 11.8 us  [other_column(): lax.ppermute(x, 'patch', [(p, p ^ 1) for p in range(layers * COLUMNS)])]
    another operation x2 -> x4, other arithmetic: 1.81 us -> 0.2 us  [the longest x3 0.16 us: layered_shards(): jnp.stack([jnp.stack([(L // rounds != core).astype(jnp.int32) for L in so...]
  transfers between devices with their start and end apart: 18 -> 22, of which waited for: 7 -> 8; matrix products, arithmetic and copies ran while one was open for 13% -> 7% of each run, Pallas kernels for 6% -> 6%
where the time goes in v2:
time: 67.1 us; the launch traced here: 66.9 us
  starting transfers between devices  31.1 us (46%)
  waiting for transfers between devices  24.1 us (36%)
  local copies, waits for them, and re-layouts  4.45 us (7%)
  Pallas kernels  4.1 us (6%)
  other arithmetic  1.92 us (3%)
  between operations  1.22 us (2%)
    ppermute x12, starting transfers between devices, layer_shift(): return lax.ppermute(x, 'patch', pairs)  25 us
    ppermute x2, waiting for transfers between devices, other_column(): lax.ppermute(x, 'patch', [(p, p ^ 1) for p in range(layers * COLUMNS)])  11.8 us
    ppermute x12, waiting for transfers between devices, layer_shift(): return lax.ppermute(x, 'patch', pairs)  11.5 us
    pallas_call x2, Pallas kernels, call_attention(): pl.pallas_call(kernel, out_shape=[jax.ShapeDtypeStruct((count // layers,...  4.1 us
    ppermute x2, starting transfers between devices, stale_round(): return lax.ppermute(x, ('patch', 'uly'), pairs)  3.18 us
    ppermute x2, starting transfers between devices, other_column(): lax.ppermute(x, 'patch', [(p, p ^ 1) for p in range(layers * COLUMNS)])  2.09 us
    dynamic_slice x3, local copies, waits for them, and re-layouts, columns_of(): return lax.dynamic_slice_in_dim(x, index * width, width, x.ndim - 1)  1.86 us
    concatenate x1, other arithmetic, layered_shards(): text = jnp.concatenate([text_first, text_second], 0)  1.45 us
  transfers between devices with their start and end apart: 22, of which 8 were waited for; matrix products, arithmetic and copies ran while one was open for 7% of the time, Pallas kernels for 6%

profile of v2, /device:TPU:0, one launch (start us, length us, event | category | flops | bytes accessed | tf_op | source)
XLA Modules:
  0.0 66.9 jit_solution(2539079536634842384)
XLA Ops:
  0.7 1.1 %constant_dynamic-slice_fusion.8 = (bf16[3,48,384]{2,1,0:T(8,128)(2,1)S(1)}, bf16[3,48,384]{2,1,0:T(8,128)(2,1)S(1)}, bf16[3,48,384]{2,1,0:T(8,128)(2,1)S(1)}) fusion(bf16[3,48,1536]{2,1,0:T(8,128)(2,1)} %param.6, s32[]{:T(128)S(6)} %select_n.164, s32[]{:T(128)S(6)} %select_n.168, s32[]{:T(128)S(6)} %select_n.166), kind=kLoop, calls=%fused_computation.33 | loop fusion | bytes 663564 | tf_op jit(solution)/shard_map/dynamic_slice | solution.py:216
  1.8 5.1 %collective-permute-start.2 = (bf16[3,48,384]{2,1,0:T(8,128)(2,1)S(1)}, bf16[3,48,384]{2,1,0:T(8,128)(2,1)S(1)}, u32[]{:S(2)}, u32[]{:S(2)}) collective-permute-start(bf16[3,48,384]{2,1,0:T(8,128)(2,1)S(1)} %get-tuple-element.22), channel_id=1, source_target_pairs={{0,12},{2,14},{4,0},{6,2},{8,4},{10,6},{12,8},{14,10},{1,13},{3,15... | collective-permute-start | bytes 331784 | tf_op jit(solution)/shard_map/ppermute | solution.py:198
  6.9 1.0 %collective-permute-start = (bf16[3,48,384]{2,1,0:T(8,128)(2,1)S(1)}, bf16[3,48,384]{2,1,0:T(8,128)(2,1)S(1)}, u32[]{:S(2)}, u32[]{:S(2)}) collective-permute-start(bf16[3,48,384]{2,1,0:T(8,128)(2,1)S(1)} %get-tuple-element.21), channel_id=1, source_target_pairs={{0,4},{2,6},{4,8},{6,10},{8,12},{10,14},{12,0},{14,2},{1,5},{3,7},... | collective-permute-start | bytes 331784 | tf_op jit(solution)/shard_map/ppermute | solution.py:198
  7.9 1.5 %fusion = bf16[4,256,384]{2,1,0:T(8,128)(2,1)S(1)} fusion(s32[]{:T(128)S(6)} %select_n.172, bf16[2,256,768]{2,1,0:T(8,128)(2,1)S(1)} %copy-done, bf16[2,256,768]{2,1,0:T(8,128)(2,1)} %param.11), kind=kLoop, calls=%fused_computation.2 | loop fusion | flops 1572864 | bytes 2359300 | tf_op jit(solution)/shard_map/concatenate | solution.py:243
  9.6 2.5 %collective-permute-start.6 = (bf16[2,96,384]{2,1,0:T(8,128)(2,1)S(1)}, bf16[2,96,384]{2,1,0:T(8,128)(2,1)S(1)}, u32[]{:S(2)}, u32[]{:S(2)}) collective-permute-start(bf16[2,96,384]{2,1,0:T(8,128)(2,1)S(1)} %get-tuple-element.25), channel_id=1, source_target_pairs={{0,4},{1,12},{2,6},{3,14},{4,0},{5,8},{6,2},{7,10},{8,5},{9,13},{1... | collective-permute-start | bytes 442376 | tf_op jit(solution)/shard_map/ppermute | solution.py:207
  12.1 0.8 %dynamic-slice_bitcast_fusion.1 = bf16[48,384]{1,0:T(8,128)(2,1)S(1)} fusion(bf16[3,48,1536]{2,1,0:T(8,128)(2,1)} %param.6, s32[]{:T(128)S(6)} %select_n.162), kind=kLoop, calls=%fused_computation.16 | loop fusion | bytes 73732 | tf_op jit(solution)/shard_map/squeeze | solution.py:232
  12.9 0.7 %constant_dynamic-slice_fusion.2 = (bf16[3,48,384]{2,1,0:T(8,128)(2,1)S(1)}, bf16[3,48,384]{2,1,0:T(8,128)(2,1)}, bf16[3,48,384]{2,1,0:T(8,128)(2,1)}) fusion(bf16[3,48,1536]{2,1,0:T(8,128)(2,1)S(1)} %copy-done.1, s32[]{:T(128)S(6)} %select_n.164, s32[]{:T(128)S(6)} %select_n.168, s32[]{:T(128)S(6)} %select_n.166), kind=kLoop, calls=%fused_computation.23 | loop fusion | bytes 663564 | tf_op jit(solution)/shard_map/dynamic_slice | solution.py:216
  13.6 0.9 %constant_dynamic-slice_fusion.9 = bf16[2,48,384]{2,1,0:T(8,128)(2,1)S(1)} fusion(bf16[3,48,1536]{2,1,0:T(8,128)(2,1)} %param.6, s32[]{:T(128)S(6)} %add.152, s32[]{:T(128)S(6)} %select_n.162), kind=kLoop, calls=%fused_computation.34 | loop fusion | bytes 147464 | tf_op jit(solution)/shard_map/slice | solution.py:233
  14.9 0.7 %collective-permute-start.5 = (bf16[2,96,384]{2,1,0:T(8,128)(2,1)S(1)}, bf16[2,96,384]{2,1,0:T(8,128)(2,1)S(1)}, u32[]{:S(2)}, u32[]{:S(2)}) collective-permute-start(bf16[2,96,384]{2,1,0:T(8,128)(2,1)S(1)} %get-tuple-element.24), channel_id=1, source_target_pairs={{0,0},{1,8},{2,2},{3,10},{4,4},{5,12},{6,6},{7,14},{8,1},{9,9},{10... | collective-permute-start | bytes 442376 | tf_op jit(solution)/shard_map/ppermute | solution.py:207
  15.6 2.7 %collective-permute-done.1 = bf16[3,48,384]{2,1,0:T(8,128)(2,1)S(1)} collective-permute-done((bf16[3,48,384]{2,1,0:T(8,128)(2,1)S(1)}, bf16[3,48,384]{2,1,0:T(8,128)(2,1)S(1)}, u32[]{:S(2)}, u32[]{:S(2)}) %collective-permute-start.1) | collective-permute-done | bytes 110624 | tf_op jit(solution)/shard_map/ppermute | solution.py:198
  18.3 1.2 %collective-permute-start.15 = (bf16[3,48,384]{2,1,0:T(8,128)(2,1)}, bf16[3,48,384]{2,1,0:T(8,128)(2,1)S(1)}, u32[]{:S(2)}, u32[]{:S(2)}) collective-permute-start(bf16[3,48,384]{2,1,0:T(8,128)(2,1)} %get-tuple-element.19), channel_id=1, source_target_pairs={{0,12},{2,14},{4,0},{6,2},{8,4},{10,6},{12,8},{14,10},{1,13},{3,15... | collective-permute-start | bytes 331784 | tf_op jit(solution)/shard_map/ppermute | solution.py:198
  19.5 1.9 %collective-permute-start.14 = (bf16[3,48,384]{2,1,0:T(8,128)(2,1)}, bf16[3,48,384]{2,1,0:T(8,128)(2,1)S(1)}, u32[]{:S(2)}, u32[]{:S(2)}) collective-permute-start(bf16[3,48,384]{2,1,0:T(8,128)(2,1)} %get-tuple-element.20), channel_id=1, source_target_pairs={{0,8},{2,10},{4,12},{6,14},{8,0},{10,2},{12,4},{14,6},{1,9},{3,11}... | collective-permute-start | bytes 331784 | tf_op jit(solution)/shard_map/ppermute | solution.py:198
  21.5 2.9 %collective-permute-done.15 = bf16[3,48,384]{2,1,0:T(8,128)(2,1)S(1)} collective-permute-done((bf16[3,48,384]{2,1,0:T(8,128)(2,1)}, bf16[3,48,384]{2,1,0:T(8,128)(2,1)S(1)}, u32[]{:S(2)}, u32[]{:S(2)}) %collective-permute-start.15) | collective-permute-done | bytes 110624 | tf_op jit(solution)/shard_map/ppermute | solution.py:198
  24.4 8.6 %collective-permute-start.13 = (bf16[3,48,384]{2,1,0:T(8,128)(2,1)S(1)}, bf16[3,48,384]{2,1,0:T(8,128)(2,1)S(1)}, u32[]{:S(2)}, u32[]{:S(2)}) collective-permute-start(bf16[3,48,384]{2,1,0:T(8,128)(2,1)S(1)} %get-tuple-element.18), channel_id=1, source_target_pairs={{0,4},{2,6},{4,8},{6,10},{8,12},{10,14},{12,0},{14,2},{1,5},{3,7},... | collective-permute-start | bytes 331784 | tf_op jit(solution)/shard_map/ppermute | solution.py:198
  33.0 0.6 collective-permute-done.14
  33.6 1.7 %collective-permute-done.13 = bf16[3,48,384]{2,1,0:T(8,128)(2,1)S(1)} collective-permute-done((bf16[3,48,384]{2,1,0:T(8,128)(2,1)S(1)}, bf16[3,48,384]{2,1,0:T(8,128)(2,1)S(1)}, u32[]{:S(2)}, u32[]{:S(2)}) %collective-permute-start.13) | collective-permute-done | bytes 110624 | tf_op jit(solution)/shard_map/ppermute | solution.py:198
  35.3 1.5 %collective-permute-start.17 = (bf16[2,192,384]{2,1,0:T(8,128)(2,1)S(1)}, bf16[2,192,384]{2,1,0:T(8,128)(2,1)S(1)}, u32[]{:S(2)}, u32[]{:S(2)}) collective-permute-start(bf16[2,192,384]{2,1,0:T(8,128)(2,1)S(1)} %pad_maximum_fusion.own_ref.near_ref), channel_id=1, source_target_pairs={{0,2},{2,0},{4,6},{6,4},{8,10},{10,8},{12,14},{14,12},{1,3},{3,1},... | collective-permute-start | bytes 884744 | tf_op jit(solution)/shard_map/ppermute | solution.py:210
  36.9 0.6 collective-permute-start.8
  37.6 11.8 %collective-permute-done.8.away_ref = bf16[2,2,96,384]{3,2,1,0:T(8,128)(2,1)S(1)} collective-permute-done((bf16[2,2,96,384]{3,2,1,0:T(8,128)(2,1)S(1)}, bf16[2,2,96,384]{3,2,1,0:T(8,128)(2,1)S(1)}, u32[]{:S(2)}, u32[]{:S(2)}) %collective-permute-start.8) | collective-permute-done | bytes 294944 | tf_op jit(solution)/shard_map/ppermute | solution.py:210
  49.5 0.6 collective-permute-start.16
  50.1 0.1 broadcast_select_fusion.text_ref
  50.3 0.8 %collective-permute-done.9.away_twin_ref = bf16[2,2,96,384]{3,2,1,0:T(8,128)(2,1)S(1)} collective-permute-done((bf16[2,2,96,384]{3,2,1,0:T(8,128)(2,1)S(1)}, bf16[2,2,96,384]{3,2,1,0:T(8,128)(2,1)S(1)}, u32[]{:S(2)}, u32[]{:S(2)}) %collective-permute-start.9) | collective-permute-done | bytes 294944 | tf_op jit(solution)/shard_map/ppermute | solution.py:213
  51.0 2.3 %shard_map.77 = (bf16[48,384]{1,0:T(8,128)(2,1)S(1)}, bf16[48,384]{1,0:T(8,128)(2,1)S(1)}, bf16[48,384]{1,0:T(8,128)(2,1)S(1)}, bf16[48,384]{1,0:T(8,128)(2,1)S(1)}) custom-call(f32[2,3]{1,0:T(2,128)S(1)} %fusion.3.scale_ref, s32[2,4]{1,0:T(2,128)S(1)} %pad_add_fusion.order_ref, bf16[192,384]{1,0:T(8,128)(2,1)S(1)} %pad_maximum_fusion.3.q_ref, ...), custom_call_target="tpu_custom_call" | custom-call | flops 301989888 | bytes 1867776 | tf_op jit(solution)/shard_map/pallas_call | solution.py:173
  53.4 1.0 %collective-permute-start.11 = (bf16[48,384]{1,0:T(8,128)(2,1)S(1)}, bf16[48,384]{1,0:T(8,128)(2,1)S(1)}, u32[]{:S(2)}, u32[]{:S(2)}) collective-permute-start(bf16[48,384]{1,0:T(8,128)(2,1)S(1)} %get-tuple-element.12), channel_id=1, source_target_pairs={{0,8},{2,10},{4,12},{6,14},{8,0},{10,2},{12,4},{14,6},{1,9},{3,11}... | collective-permute-start | bytes 110600 | tf_op jit(solution)/shard_map/ppermute | solution.py:198
  54.4 1.1 %collective-permute-start.12 = (bf16[48,384]{1,0:T(8,128)(2,1)S(1)}, bf16[48,384]{1,0:T(8,128)(2,1)S(1)}, u32[]{:S(2)}, u32[]{:S(2)}) collective-permute-start(bf16[48,384]{1,0:T(8,128)(2,1)S(1)} %get-tuple-element.13), channel_id=1, source_target_pairs={{0,4},{2,6},{4,8},{6,10},{8,12},{10,14},{12,0},{14,2},{1,5},{3,7},... | collective-permute-start | bytes 110600 | tf_op jit(solution)/shard_map/ppermute | solution.py:198
  55.5 1.8 %shard_map.78 = (bf16[48,384]{1,0:T(8,128)(2,1)S(1)}, bf16[48,384]{1,0:T(8,128)(2,1)S(1)}, bf16[48,384]{1,0:T(8,128)(2,1)S(1)}, bf16[48,384]{1,0:T(8,128)(2,1)S(1)}) custom-call(bf16[192,384]{1,0:T(8,128)(2,1)S(1)} %pad_maximum_fusion.4.q_ref, bf16[4,256,384]{2,1,0:T(8,128)(2,1)S(1)} %broadcast_select_fusion.text_ref, ...), custom_call_target="tpu_custom_call" | custom-call | flops 301989888 | bytes 1867776 | tf_op jit(solution)/shard_map/pallas_call | solution.py:173
  57.2 2.8 %collective-permute-start.19 = (bf16[48,384]{1,0:T(8,128)(2,1)S(1)}, bf16[48,384]{1,0:T(8,128)(2,1)S(1)}, u32[]{:S(2)}, u32[]{:S(2)}) collective-permute-start(bf16[48,384]{1,0:T(8,128)(2,1)S(1)} %get-tuple-element.15), channel_id=1, source_target_pairs={{0,12},{2,14},{4,0},{6,2},{8,4},{10,6},{12,8},{14,10},{1,13},{3,15... | collective-permute-start | bytes 110600 | tf_op jit(solution)/shard_map/ppermute | solution.py:198
  60.0 0.2 collective-permute-start.20
  60.4 2.0 %collective-permute-start.21 = (bf16[48,384]{1,0:T(8,128)(2,1)S(1)}, bf16[48,384]{1,0:T(8,128)(2,1)S(1)}, u32[]{:S(2)}, u32[]{:S(2)}) collective-permute-start(bf16[48,384]{1,0:T(8,128)(2,1)S(1)} %get-tuple-element.17), channel_id=1, source_target_pairs={{0,4},{2,6},{4,8},{6,10},{8,12},{10,14},{12,0},{14,2},{1,5},{3,7},... | collective-permute-start | bytes 110600 | tf_op jit(solution)/shard_map/ppermute | solution.py:198
  62.5 2.4 %collective-permute-done.20 = bf16[48,384]{1,0:T(8,128)(2,1)S(1)} collective-permute-done((bf16[48,384]{1,0:T(8,128)(2,1)S(1)}, bf16[48,384]{1,0:T(8,128)(2,1)S(1)}, u32[]{:S(2)}, u32[]{:S(2)}) %collective-permute-start.20) | collective-permute-done | bytes 36896 | tf_op jit(solution)/shard_map/ppermute | solution.py:198
  64.9 1.3 %collective-permute-done.21 = bf16[48,384]{1,0:T(8,128)(2,1)S(1)} collective-permute-done((bf16[48,384]{1,0:T(8,128)(2,1)S(1)}, bf16[48,384]{1,0:T(8,128)(2,1)S(1)}, u32[]{:S(2)}, u32[]{:S(2)}) %collective-permute-start.21) | collective-permute-done | bytes 36896 | tf_op jit(solution)/shard_map/ppermute | solution.py:198
  66.2 0.7 copy-done.3
  (66 shorter events, 1.0 us)
Async XLA Ops:
  0.6 7.3 %copy-start = (bf16[2,256,768]{2,1,0:T(8,128)(2,1)S(1)}, bf16[2,256,768]{2,1,0:T(8,128)(2,1)}, u32[]{:S(2)}) copy-start(bf16[2,256,768]{2,1,0:T(8,128)(2,1)} %param.10) | copy-start | bytes 2359300
  1.8 13.1 %collective-permute-start.2 = (bf16[3,48,384]{2,1,0:T(8,128)(2,1)S(1)}, bf16[3,48,384]{2,1,0:T(8,128)(2,1)S(1)}, u32[]{:S(2)}, u32[]{:S(2)}) collective-permute-start(bf16[3,48,384]{2,1,0:T(8,128)(2,1)S(1)} %get-tuple-element.22), channel_id=1, source_target_pairs={{0,12},{2,14},{4,0},{6,2},{8,4},{10,6},{12,8},{14,10},{1,13},{3,15... | collective-permute-start | bytes 331784 | tf_op jit(solution)/shard_map/ppermute | solution.py:198
  6.9 11.4 %collective-permute-start.1 = (bf16[3,48,384]{2,1,0:T(8,128)(2,1)S(1)}, bf16[3,48,384]{2,1,0:T(8,128)(2,1)S(1)}, u32[]{:S(2)}, u32[]{:S(2)}) collective-permute-start(bf16[3,48,384]{2,1,0:T(8,128)(2,1)S(1)} %get-tuple-element.23), channel_id=1, source_target_pairs={{0,8},{2,10},{4,12},{6,14},{8,0},{10,2},{12,4},{14,6},{1,9},{3,11}... | collective-permute-start | bytes 331784 | tf_op jit(solution)/shard_map/ppermute | solution.py:198
  6.9 12.6 %collective-permute-start = (bf16[3,48,384]{2,1,0:T(8,128)(2,1)S(1)}, bf16[3,48,384]{2,1,0:T(8,128)(2,1)S(1)}, u32[]{:S(2)}, u32[]{:S(2)}) collective-permute-start(bf16[3,48,384]{2,1,0:T(8,128)(2,1)S(1)} %get-tuple-element.21), channel_id=1, source_target_pairs={{0,4},{2,6},{4,8},{6,10},{8,12},{10,14},{12,0},{14,2},{1,5},{3,7},... | collective-permute-start | bytes 331784 | tf_op jit(solution)/shard_map/ppermute | solution.py:198
  7.9 1.6 %copy-start.2 = (bf16[2,96,768]{2,1,0:T(8,128)(2,1)S(1)}, bf16[2,96,768]{2,1,0:T(8,128)(2,1)}, u32[]{:S(2)}) copy-start(bf16[2,96,768]{2,1,0:T(8,128)(2,1)} %param.8) | copy-start | bytes 884740
  9.4 3.5 %copy-start.1 = (bf16[3,48,1536]{2,1,0:T(8,128)(2,1)S(1)}, bf16[3,48,1536]{2,1,0:T(8,128)(2,1)}, u32[]{:S(2)}) copy-start(bf16[3,48,1536]{2,1,0:T(8,128)(2,1)} %param.7) | copy-start | bytes 1327108
  9.4 40.6 %collective-permute-start.3 = (bf16[4,256,384]{2,1,0:T(8,128)(2,1)S(1)}, bf16[4,256,384]{2,1,0:T(8,128)(2,1)S(1)}, u32[]{:S(2)}, u32[]{:S(2)}) collective-permute-start(bf16[4,256,384]{2,1,0:T(8,128)(2,1)S(1)} %fusion), channel_id=1, source_target_pairs={{0,1},{1,0},{2,3},{3,2},{4,5},{5,4},{6,7},{7,6},{8,9},{9,8},{10,11... | collective-permute-start | bytes 2359304 | tf_op jit(solution)/shard_map/ppermute | solution.py:213
  9.6 5.0 %copy-start.5 = (s32[2,12]{1,0:T(2,128)S(1)}, s32[2,12]{1,0:T(2,128)}, u32[]{:S(2)}) copy-start(s32[2,12]{1,0:T(2,128)} %param.9) | copy-start | bytes 292
  9.6 27.3 %collective-permute-start.6 = (bf16[2,96,384]{2,1,0:T(8,128)(2,1)S(1)}, bf16[2,96,384]{2,1,0:T(8,128)(2,1)S(1)}, u32[]{:S(2)}, u32[]{:S(2)}) collective-permute-start(bf16[2,96,384]{2,1,0:T(8,128)(2,1)S(1)} %get-tuple-element.25), channel_id=1, source_target_pairs={{0,4},{1,12},{2,6},{3,14},{4,0},{5,8},{6,2},{7,10},{8,5},{9,13},{1... | collective-permute-start | bytes 442376 | tf_op jit(solution)/shard_map/ppermute | solution.py:207
  14.9 22.0 %collective-permute-start.5 = (bf16[2,96,384]{2,1,0:T(8,128)(2,1)S(1)}, bf16[2,96,384]{2,1,0:T(8,128)(2,1)S(1)}, u32[]{:S(2)}, u32[]{:S(2)}) collective-permute-start(bf16[2,96,384]{2,1,0:T(8,128)(2,1)S(1)} %get-tuple-element.24), channel_id=1, source_target_pairs={{0,0},{1,8},{2,2},{3,10},{4,4},{5,12},{6,6},{7,14},{8,1},{9,9},{10... | collective-permute-start | bytes 442376 | tf_op jit(solution)/shard_map/ppermute | solution.py:207
  18.3 6.1 %collective-permute-start.15 = (bf16[3,48,384]{2,1,0:T(8,128)(2,1)}, bf16[3,48,384]{2,1,0:T(8,128)(2,1)S(1)}, u32[]{:S(2)}, u32[]{:S(2)}) collective-permute-start(bf16[3,48,384]{2,1,0:T(8,128)(2,1)} %get-tuple-element.19), channel_id=1, source_target_pairs={{0,12},{2,14},{4,0},{6,2},{8,4},{10,6},{12,8},{14,10},{1,13},{3,15... | collective-permute-start | bytes 331784 | tf_op jit(solution)/shard_map/ppermute | solution.py:198
  19.5 14.1 %collective-permute-start.14 = (bf16[3,48,384]{2,1,0:T(8,128)(2,1)}, bf16[3,48,384]{2,1,0:T(8,128)(2,1)S(1)}, u32[]{:S(2)}, u32[]{:S(2)}) collective-permute-start(bf16[3,48,384]{2,1,0:T(8,128)(2,1)} %get-tuple-element.20), channel_id=1, source_target_pairs={{0,8},{2,10},{4,12},{6,14},{8,0},{10,2},{12,4},{14,6},{1,9},{3,11}... | collective-permute-start | bytes 331784 | tf_op jit(solution)/shard_map/ppermute | solution.py:198
  24.4 10.9 %collective-permute-start.13 = (bf16[3,48,384]{2,1,0:T(8,128)(2,1)S(1)}, bf16[3,48,384]{2,1,0:T(8,128)(2,1)S(1)}, u32[]{:S(2)}, u32[]{:S(2)}) collective-permute-start(bf16[3,48,384]{2,1,0:T(8,128)(2,1)S(1)} %get-tuple-element.18), channel_id=1, source_target_pairs={{0,4},{2,6},{4,8},{6,10},{8,12},{10,14},{12,0},{14,2},{1,5},{3,7},... | collective-permute-start | bytes 331784 | tf_op jit(solution)/shard_map/ppermute | solution.py:198
  33.6 16.6 %collective-permute-start.4 = (bf16[2,192,384]{2,1,0:T(8,128)(2,1)S(1)}, bf16[2,192,384]{2,1,0:T(8,128)(2,1)S(1)}, u32[]{:S(2)}, u32[]{:S(2)}) collective-permute-start(bf16[2,192,384]{2,1,0:T(8,128)(2,1)S(1)} %pad_maximum_fusion.own_ref.near_ref), channel_id=1, source_target_pairs={{0,1},{1,0},{2,3},{3,2},{4,5},{5,4},{6,7},{7,6},{8,9},{9,8},{10,11... | collective-permute-start | bytes 884744 | tf_op jit(solution)/shard_map/ppermute | solution.py:213
  35.3 14.2 %collective-permute-start.17 = (bf16[2,192,384]{2,1,0:T(8,128)(2,1)S(1)}, bf16[2,192,384]{2,1,0:T(8,128)(2,1)S(1)}, u32[]{:S(2)}, u32[]{:S(2)}) collective-permute-start(bf16[2,192,384]{2,1,0:T(8,128)(2,1)S(1)} %pad_maximum_fusion.own_ref.near_ref), channel_id=1, source_target_pairs={{0,2},{2,0},{4,6},{6,4},{8,10},{10,8},{12,14},{14,12},{1,3},{3,1},... | collective-permute-start | bytes 884744 | tf_op jit(solution)/shard_map/ppermute | solution.py:210
  36.9 12.5 %collective-permute-start.8 = (bf16[2,2,96,384]{3,2,1,0:T(8,128)(2,1)S(1)}, bf16[2,2,96,384]{3,2,1,0:T(8,128)(2,1)S(1)}, u32[]{:S(2)}, u32[]{:S(2)}) collective-permute-start(bf16[2,2,96,384]{3,2,1,0:T(8,128)(2,1)S(1)} %pad_maximum_fusion.1.near_ref), channel_id=1, source_target_pairs={{0,2},{2,0},{4,6},{6,4},{8,10},{10,8},{12,14},{14,12},{1,3},{3,1},... | collective-permute-start | bytes 884744 | tf_op jit(solution)/shard_map/ppermute | solution.py:210
  37.5 12.7 %collective-permute-start.7 = (bf16[2,2,96,384]{3,2,1,0:T(8,128)(2,1)S(1)}, bf16[2,2,96,384]{3,2,1,0:T(8,128)(2,1)S(1)}, u32[]{:S(2)}, u32[]{:S(2)}) collective-permute-start(bf16[2,2,96,384]{3,2,1,0:T(8,128)(2,1)S(1)} %pad_maximum_fusion.1.near_ref), channel_id=1, source_target_pairs={{0,1},{1,0},{2,3},{3,2},{4,5},{5,4},{6,7},{7,6},{8,9},{9,8},{10,11... | collective-permute-start | bytes 884744 | tf_op jit(solution)/shard_map/ppermute | solution.py:213
  49.4 1.6 %collective-permute-start.9 = (bf16[2,2,96,384]{3,2,1,0:T(8,128)(2,1)S(1)}, bf16[2,2,96,384]{3,2,1,0:T(8,128)(2,1)S(1)}, u32[]{:S(2)}, u32[]{:S(2)}) collective-permute-start(bf16[2,2,96,384]{3,2,1,0:T(8,128)(2,1)S(1)} %collective-permute-done.8.away_ref), channel_id=1, source_target_pairs={{0,1},{1,0},{2,3},{3,2},{4,5},{5,4},{6,7},{7,6},{8,9},{9,8},{10,11... | collective-permute-start | bytes 884744 | tf_op jit(solution)/shard_map/ppermute | solution.py:213
  49.5 6.0 %collective-permute-start.16 = (bf16[2,192,384]{2,1,0:T(8,128)(2,1)S(1)}, bf16[2,192,384]{2,1,0:T(8,128)(2,1)S(1)}, u32[]{:S(2)}, u32[]{:S(2)}) collective-permute-start(bf16[2,192,384]{2,1,0:T(8,128)(2,1)S(1)} %pad_maximum_fusion.2.own_ref), channel_id=1, source_target_pairs={{0,1},{1,0},{2,3},{3,2},{4,5},{5,4},{6,7},{7,6},{8,9},{9,8},{10,11... | collective-permute-start | bytes 884744 | tf_op jit(solution)/shard_map/ppermute | solution.py:213
  50.0 5.4 %collective-permute-start.18 = (bf16[2,192,384]{2,1,0:T(8,128)(2,1)S(1)}, bf16[2,192,384]{2,1,0:T(8,128)(2,1)S(1)}, u32[]{:S(2)}, u32[]{:S(2)}) collective-permute-start(bf16[2,192,384]{2,1,0:T(8,128)(2,1)S(1)} %collective-permute-done.17.away_ref), channel_id=1, source_target_pairs={{0,1},{1,0},{2,3},{3,2},{4,5},{5,4},{6,7},{7,6},{8,9},{9,8},{10,11... | collective-permute-start | bytes 884744 | tf_op jit(solution)/shard_map/ppermute | solution.py:213
  53.4 7.0 %collective-permute-start.10 = (bf16[48,384]{1,0:T(8,128)(2,1)S(1)}, bf16[48,384]{1,0:T(8,128)(2,1)S(1)}, u32[]{:S(2)}, u32[]{:S(2)}) collective-permute-start(bf16[48,384]{1,0:T(8,128)(2,1)S(1)} %get-tuple-element.11), channel_id=1, source_target_pairs={{0,12},{2,14},{4,0},{6,2},{8,4},{10,6},{12,8},{14,10},{1,13},{3,15... | collective-permute-start | bytes 110600 | tf_op jit(solution)/shard_map/ppermute | solution.py:198
  53.4 8.9 %collective-permute-start.11 = (bf16[48,384]{1,0:T(8,128)(2,1)S(1)}, bf16[48,384]{1,0:T(8,128)(2,1)S(1)}, u32[]{:S(2)}, u32[]{:S(2)}) collective-permute-start(bf16[48,384]{1,0:T(8,128)(2,1)S(1)} %get-tuple-element.12), channel_id=1, source_target_pairs={{0,8},{2,10},{4,12},{6,14},{8,0},{10,2},{12,4},{14,6},{1,9},{3,11}... | collective-permute-start | bytes 110600 | tf_op jit(solution)/shard_map/ppermute | solution.py:198
  54.4 8.0 %collective-permute-start.12 = (bf16[48,384]{1,0:T(8,128)(2,1)S(1)}, bf16[48,384]{1,0:T(8,128)(2,1)S(1)}, u32[]{:S(2)}, u32[]{:S(2)}) collective-permute-start(bf16[48,384]{1,0:T(8,128)(2,1)S(1)} %get-tuple-element.13), channel_id=1, source_target_pairs={{0,4},{2,6},{4,8},{6,10},{8,12},{10,14},{12,0},{14,2},{1,5},{3,7},... | collective-permute-start | bytes 110600 | tf_op jit(solution)/shard_map/ppermute | solution.py:198
  57.2 5.2 %collective-permute-start.19 = (bf16[48,384]{1,0:T(8,128)(2,1)S(1)}, bf16[48,384]{1,0:T(8,128)(2,1)S(1)}, u32[]{:S(2)}, u32[]{:S(2)}) collective-permute-start(bf16[48,384]{1,0:T(8,128)(2,1)S(1)} %get-tuple-element.15), channel_id=1, source_target_pairs={{0,12},{2,14},{4,0},{6,2},{8,4},{10,6},{12,8},{14,10},{1,13},{3,15... | collective-permute-start | bytes 110600 | tf_op jit(solution)/shard_map/ppermute | solution.py:198
  60.0 4.9 %collective-permute-start.20 = (bf16[48,384]{1,0:T(8,128)(2,1)S(1)}, bf16[48,384]{1,0:T(8,128)(2,1)S(1)}, u32[]{:S(2)}, u32[]{:S(2)}) collective-permute-start(bf16[48,384]{1,0:T(8,128)(2,1)S(1)} %get-tuple-element.16), channel_id=1, source_target_pairs={{0,8},{2,10},{4,12},{6,14},{8,0},{10,2},{12,4},{14,6},{1,9},{3,11}... | collective-permute-start | bytes 110600 | tf_op jit(solution)/shard_map/ppermute | solution.py:198
  60.4 5.8 %collective-permute-start.21 = (bf16[48,384]{1,0:T(8,128)(2,1)S(1)}, bf16[48,384]{1,0:T(8,128)(2,1)S(1)}, u32[]{:S(2)}, u32[]{:S(2)}) collective-permute-start(bf16[48,384]{1,0:T(8,128)(2,1)S(1)} %get-tuple-element.17), channel_id=1, source_target_pairs={{0,4},{2,6},{4,8},{6,10},{8,12},{10,14},{12,0},{14,2},{1,5},{3,7},... | collective-permute-start | bytes 110600 | tf_op jit(solution)/shard_map/ppermute | solution.py:198
  62.4 3.8 %copy-start.4 = (bf16[48,1536]{1,0:T(8,128)(2,1)}, bf16[48,1536]{1,0:T(8,128)(2,1)S(1)}, u32[]{:S(2)}) copy-start(bf16[48,1536]{1,0:T(8,128)(2,1)S(1)} %constant_dynamic-update-slice_fusion.4) | copy-start | bytes 442372
  66.2 0.7 copy-start.3

commit v3 on v2

v3 whole, which is shorter than its diff:
```python
import functools

import jax
import jax.numpy as jnp
from jax import lax
from jax.experimental import pallas as pl
from jax.experimental.pallas import tpu as pltpu
from jax.sharding import PartitionSpec as P

HEAD = 128
COLUMNS = 2
BF16 = jnp.bfloat16
F32 = jnp.float32


def heads_view(array):
    return array.reshape(array.shape[0], array.shape[1] // HEAD, HEAD)


def absorb(carry, queries, keys_rows, values, key_scale, value_scale, keep):
    top, total, accum = carry
    inverse = 1.0 / HEAD**0.5
    score = jnp.einsum("qhd,khd->hqk", queries, keys_rows, preferred_element_type=F32)
    score = score * (key_scale * inverse)[:, None, None]
    if keep is not None:
        score = jnp.where(keep[None, None, :], score, -jnp.inf)
    new_top = jnp.maximum(top, score.max(-1))
    fade = jnp.exp(top - new_top)
    weight = jnp.exp(score - new_top[:, :, None])
    total = total * fade + weight.sum(-1)
    addend = jnp.einsum("hqk,khd->qhd", weight.astype(BF16), values, preferred_element_type=F32)
    accum = accum * fade.T[:, :, None] + addend * value_scale[None, :, None]
    return (new_top, total, accum)


def general_step(mine, text, far, keep, key_scale, value_scale):
    queries = heads_view(mine[0])
    rows, local_heads = queries.shape[:2]
    unit = jnp.ones((local_heads,), F32)
    carry = (
        jnp.full((local_heads, rows), -jnp.inf, F32),
        jnp.zeros((local_heads, rows), F32),
        jnp.zeros((rows, local_heads, HEAD), F32),
    )
    carry = absorb(carry, queries, heads_view(text[0]), heads_view(text[1]), unit, unit, None)
    carry = absorb(carry, queries, heads_view(mine[1]), heads_view(mine[2]), unit, unit, None)
    carry = absorb(carry, queries, heads_view(far[0]), heads_view(far[1]), key_scale, value_scale, keep)
    top, total, accum = carry
    result = (accum / total.T[:, :, None]).reshape(rows, local_heads * HEAD).astype(BF16)
    return lax.all_to_all(result, "uly", split_axis=0, concat_axis=1, tiled=True)


def general_shards(fresh_first, fresh_second, stale_cache, stale_exponent, text_first, text_second):
    local_heads = stale_exponent.shape[1] // lax.axis_size("uly")
    first_head = lax.axis_index("uly") * local_heads
    exponents = lax.dynamic_slice_in_dim(stale_exponent, first_head, local_heads, 1)
    scales = jnp.exp2(exponents.astype(F32))
    unit = jnp.ones((local_heads,), F32)
    mine_first = lax.all_to_all(fresh_first, "uly", split_axis=2, concat_axis=1, tiled=True)
    mine_second = lax.all_to_all(fresh_second, "uly", split_axis=2, concat_axis=1, tiled=True)
    rows = mine_first.shape[1]
    own_start = lax.axis_index("patch") * rows
    stale = lax.all_gather(stale_cache, "patch", axis=1, tiled=True)
    refreshed = lax.all_gather(mine_first[1:], "patch", axis=1, tiled=True)
    places = jnp.arange(stale.shape[1], dtype=jnp.int32)
    keep = (places < own_start) | (places >= own_start + rows)
    return (
        general_step(mine_first, text_first, stale, keep, scales[0], scales[1]),
        general_step(mine_second, text_second, refreshed, keep, unit, unit),
    )


def dot_t(a, b):
    return lax.dot_general(a, b, (((1,), (1,)), ((), ())), preferred_element_type=F32)


def dot(a, b):
    return jnp.dot(a, b, preferred_element_type=F32)


def attend(q, text, own, near, away, inside, key_factor, value_factor):
    inverse = 1.0 / HEAD**0.5
    scores = [
        dot_t(q, text[0]) * inverse,
        jnp.where(inside, dot_t(q, own[0]) * inverse, dot_t(q, near[0]) * key_factor),
        dot_t(q, away[0]) * key_factor,
    ]
    top = functools.reduce(jnp.maximum, [s.max(-1, keepdims=True) for s in scores])
    weights = [jnp.exp(s - top) for s in scores]
    total = functools.reduce(jnp.add, [w.sum(-1, keepdims=True) for w in weights])
    w_text, w_near, w_away = [w.astype(BF16) for w in weights]
    zero = jnp.zeros((), BF16)
    kept = dot(w_text, text[1]) + dot(jnp.where(inside, w_near, zero), own[1])
    far = dot(jnp.where(inside, zero, w_near), near[1]) + dot(w_away, away[1])
    return (kept + value_factor * far) / total


def store_blocks(out_refs, result, lanes):
    rows = out_refs[0].shape[0]
    for i, out_ref in enumerate(out_refs):
        out_ref[:, lanes] = result[i * rows : (i + 1) * rows].astype(BF16)


def kernel_columns(ref, index):
    width = index[1]
    return ref.at[..., pl.ds(pl.multiple_of(index[0] * width, width), width)]


def run_copies(copies, sems):
    started = [pltpu.make_async_copy(a, b, sems.at[i]) for i, (a, b) in enumerate(copies)]
    for c in started:
        c.start()
    for c in started:
        c.wait()


def pack_shared_kernel(stale_ref, first_ref, *refs, layers):
    rounds = layers // 2
    layer = lax.axis_index("patch") // COLUMNS
    out_refs, sems = refs[:-1], refs[-1]
    width = out_refs[0].shape[-1]
    copies = [
        (kernel_columns(stale_ref, ((layer + k) % rounds, width)), out_refs[k]) for k in range(rounds)
    ]
    for s in range(layers):
        copies.append((kernel_columns(first_ref.at[1:], ((layer + s) % layers, width)), out_refs[rounds + s]))
    run_copies(copies, sems)


def pack_owned_kernel(first_ref, second_ref, text_first_ref, text_second_ref, *refs, layers):
    layer = lax.axis_index("patch") // COLUMNS
    out_refs, text_ref, sems = refs[:-2], refs[-2], refs[-1]
    width = text_ref.shape[-1]
    copies = []
    for s, out_ref in enumerate(out_refs):
        copies.append((kernel_columns(first_ref.at[:1], ((layer + s) % layers, width)), out_ref.at[:1]))
        copies.append((kernel_columns(second_ref, ((layer + s) % layers, width)), out_ref.at[1:]))
    for i, ref in enumerate((text_first_ref, text_second_ref)):
        copies.append((kernel_columns(ref, (layer % (layers // 2), width)), text_ref.at[2 * i : 2 * i + 2]))
    run_copies(copies, sems)


def pack(kernel, shapes, copies, *operands):
    return pl.pallas_call(
        kernel,
        out_shape=[jax.ShapeDtypeStruct(shape, BF16) for shape in shapes],
        in_specs=[pl.BlockSpec(memory_space=pl.ANY)] * len(operands),
        out_specs=[pl.BlockSpec(memory_space=pltpu.VMEM)] * len(shapes),
        scratch_shapes=[pltpu.SemaphoreType.DMA((copies,))],
        cost_estimate=pl.CostEstimate(flops=0, bytes_accessed=1 << 20, transcendentals=0),
    )(*operands)


def both_kernel(scale_ref, order_ref, queries_ref, text_ref, text_twin_ref, last_ref, last_twin_ref, *refs, parts):
    sets, refs = [], list(refs)
    for p in parts:
        sets.append(refs[:p])
        refs = refs[p:]
    near_sets, away_sets = sets[:2], sets[2:]
    out_refs = refs
    layers = len(out_refs)
    rounds = layers // 2
    count, width = queries_ref.shape[1:]
    rows = count // layers
    inverse = 1.0 / HEAD**0.5
    shape = (count, 2 * count)
    query_block = lax.broadcasted_iota(jnp.int32, shape, 0) // rows
    place = lax.broadcasted_iota(jnp.int32, shape, 1)
    inside = [query_block == place // (2 * rows), query_block == place % count // rows]

    def fresh_view(pieces):
        return (pieces[1], 0) if len(pieces) == 2 else (pieces[0], layers)

    for step in range(2):
        for head in range(width // HEAD):
            lanes = slice(head * HEAD, (head + 1) * HEAD)

            def text(i):
                at = 2 * step + i
                return jnp.where(order_ref[2, 0] == 0, text_ref[at, :, lanes], text_twin_ref[at, :, lanes])

            def fresh(pieces, i):
                ref, base = fresh_view(pieces)
                half = layers // 2
                return jnp.concatenate([ref[base + half * i + j, :, lanes] for j in range(half)], 0)

            def fresh_all(pair, i):
                return jnp.concatenate([fresh(p, i) for p in pair], 0)

            def in_patches(i):
                own, twin = (fresh(p, i) for p in near_sets)
                return jnp.concatenate([x[s * rows : (s + 1) * rows] for s in range(layers) for x in (own, twin)], 0)

            def last(i):
                return jnp.concatenate([last_ref[2 + i, :, lanes], last_twin_ref[last_twin_ref.shape[0] - 2 + i, :, lanes]], 0)

            def stale_in_patches(i):
                blocks = []
                for s in range(layers):
                    at = 2 * order_ref[1, s] + i
                    blocks.append(jnp.where(order_ref[0, s] == 0, *(p[0][at, :, lanes] for p in near_sets)))
                return jnp.concatenate(blocks, 0)

            def stale_elsewhere(i):
                return jnp.concatenate([p[0][2 * k + i, :, lanes] for p in away_sets for k in range(rounds)], 0)

            if step == 0:
                own = [in_patches(i) for i in range(2)]
                near = [stale_in_patches(i) for i in range(2)]
                away = [stale_elsewhere(i) for i in range(2)]
            else:
                own = [last(i) for i in range(2)]
                near = [fresh_all(near_sets, i) for i in range(2)]
                away = [fresh_all(away_sets, i) for i in range(2)]
            result = attend(
                queries_ref[step, :, lanes],
                [text(i) for i in range(2)],
                own,
                near,
                away,
                inside[step],
                inverse if step else scale_ref[0, head] * inverse,
                1.0 if step else scale_ref[1, head],
            )
            for i, out_ref in enumerate(out_refs):
                out_ref[step, :, lanes] = result[i * rows : (i + 1) * rows].astype(BF16)


def call_both(layers, scalars, parts, *operands):
    count, width = operands[0].shape[1:]
    keys = 2 * operands[1].shape[1] + 8 * count
    in_vmem = pl.BlockSpec(memory_space=pltpu.VMEM)
    return pl.pallas_call(
        functools.partial(both_kernel, parts=parts),
        out_shape=[jax.ShapeDtypeStruct((2, count // layers, width), BF16)] * layers,
        in_specs=[pl.BlockSpec(memory_space=pltpu.SMEM)] * len(scalars) + [in_vmem] * len(operands),
        out_specs=[in_vmem] * layers,
        compiler_params=pltpu.CompilerParams(vmem_limit_bytes=32 * 1024 * 1024),
        cost_estimate=pl.CostEstimate(
            flops=4 * count * keys * width, bytes_accessed=4 * width * (keys + count), transcendentals=count * keys * width // HEAD
        ),
    )(*scalars, *operands)


def layered_shards(layers, fresh_first, fresh_second, stale_cache, stale_exponent, text_first, text_second):
    core = lax.axis_index("uly")
    layer = lax.axis_index("patch") // COLUMNS
    rows, features = fresh_first.shape[1:]
    width = features // layers
    heads = width // HEAD
    half = features // 2
    rounds = layers // 2
    count = layers * rows
    text_rows = text_first.shape[1]

    def after(x, *needed):
        return lax.optimization_barrier((x,) + needed)[0]

    def layer_swap(x, shift):
        pairs = [(z * COLUMNS + y, (z + shift) % layers * COLUMNS + y) for z in range(layers) for y in range(COLUMNS)]
        return x if shift == 0 else lax.ppermute(x, "patch", pairs)

    def stale_round(x, k):
        pairs = []
        for z in range(layers):
            for y in range(COLUMNS):
                for u in range(2):
                    to = (u * rounds + (z + k) % rounds) * COLUMNS + y
                    pairs.append(((z * COLUMNS + y) * 2 + u, to * 2 + z // rounds))
        return lax.ppermute(x, ("patch", "uly"), pairs)

    def other_column(x):
        return lax.ppermute(x, "patch", [(p, p ^ 1) for p in range(layers * COLUMNS)])

    def other_core(x):
        return lax.ppermute(x, "uly", [(0, 1), (1, 0)])

    def columns_of(x, index):
        return lax.dynamic_slice_in_dim(x, index * width, width, x.ndim - 1)

    shared = [columns_of(stale_cache, (layer + k) % rounds) for k in range(rounds)]
    shared += [columns_of(fresh_first[1:], (layer + s) % layers) for s in range(layers)]
    *owned, text = pack(
        functools.partial(pack_owned_kernel, layers=layers),
        [(4, rows, width)] * layers + [(4, text_rows, width)],
        2 * layers + 2,
        after(fresh_first, shared),
        fresh_second,
        text_first,
        text_second,
    )
    stale = [stale_round(shared[k], k) for k in range(rounds)]
    fresh = [layer_swap(shared[rounds + s], s) for s in range(layers)]
    fresh[0] = after(fresh[0], owned)
    fresh_block = jnp.concatenate(fresh, 1).reshape(layers, 2 * rows, width)
    stale_block = jnp.concatenate(stale, 0)
    near = jnp.concatenate([stale_block, fresh_block], 0)
    away = [other_column(near)]
    owned = {s: layer_swap(owned[s], s) for s in (0, 2, 1, 3)}
    owned = [owned[s] for s in range(layers)]
    away_twin = [other_core(away[0][:layers]), other_core(away[0][layers:])]
    last = jnp.concatenate(owned, 1)
    near_twin = [other_core(near)]
    last_twin = other_core(last[2:])
    text_twin = other_core(after(text, owned[1]))
    sets = [[near], near_twin, away, away_twin]

    scales = jnp.exp2(lax.dynamic_slice_in_dim(stale_exponent, layer * heads, heads, 1).astype(F32))
    source = [(layer - s) % layers for s in range(layers)]
    order = jnp.stack(
        [jnp.stack([(L // rounds != core).astype(jnp.int32) for L in source]), jnp.stack([(L - layer) % rounds for L in source]), jnp.full((layers,), (layer // rounds != core).astype(jnp.int32))]
    )
    parts = tuple(len(p) for p in sets)
    flat = [p for pieces in sets for p in pieces]
    blocks = call_both(layers, [scales, order], parts, last[:2], text, text_twin, last, last_twin, *flat)

    out = jnp.zeros((2, rows, features), BF16)
    for s in range(layers):
        out = lax.dynamic_update_slice_in_dim(out, layer_swap(blocks[s], -s), (layer + s) % layers * width, 2)
    return out[0], out[1]


def solution(mesh):
    placed = (
        P(None, ("group", "patch", "uly"), None),
        P(None, ("group", "patch", "uly"), None),
        P(None, ("group", "patch"), "uly"),
        P("group", None),
        P(None, "group", "uly"),
        P(None, "group", "uly"),
    )

    def shards(*arrays):
        layers = mesh.shape["patch"] // COLUMNS
        heads = arrays[0].shape[2] // HEAD
        if mesh.shape["uly"] == 2 and layers == 4 and heads % layers == 0:
            return layered_shards(layers, *arrays)
        return general_shards(*arrays)

    return jax.shard_map(
        shards,
        mesh=mesh,
        in_specs=placed,
        out_specs=(P(("group", "patch", "uly"), None), P(("group", "patch", "uly"), None)),
        check_vma=False,
    )
```

time: 67.1 us -> 52.3 us (0.78)
  starting transfers between devices: 31.1 us -> 21.5 us
  waiting for transfers between devices: 24.1 us -> 18.6 us
  Pallas kernels: 4.1 us -> 6.66 us
  other arithmetic: 1.92 us -> 0.41 us
  local copies, waits for them, and re-layouts: 4.45 us -> 3.77 us
    ppermute x12 -> x9, starting transfers between devices: 25 us -> 16.5 us  [layer_swap(): return x if shift == 0 else lax.ppermute(x, 'patch', pairs)]
    ppermute x2 -> x1, waiting for transfers between devices: 11.8 us -> 5.25 us  [other_column(): lax.ppermute(x, 'patch', [(p, p ^ 1) for p in range(layers * COLUMNS)])]
    pallas_call x2, Pallas kernels: 4.1 us -> 6.66 us  [the longest x1 4.06 us: call_both(): pl.pallas_call(functools.partial(both_kernel, parts=parts), out_shape=[ja...]
    dynamic_slice x3 -> x2, local copies, waits for them, and re-layouts: 1.86 us -> 0.07 us  [columns_of(): return lax.dynamic_slice_in_dim(x, index * width, width, x.ndim - 1)]
    ppermute x2, starting transfers between devices: 3.18 us -> 1.41 us  [stale_round(): return lax.ppermute(x, ('patch', 'uly'), pairs)]
    concatenate x5 -> x2, other arithmetic: 1.55 us -> 0.11 us  [the longest x1 0.08 us: layered_shards(): near = jnp.concatenate([stale_block, fresh_block], 0)]
    ppermute x6 -> x5, starting transfers between devices: 0.8 us -> 2.04 us  [other_core(): return lax.ppermute(x, 'uly', [(0, 1), (1, 0)])]
    unnamed x12 -> x13, local copies, waits for them, and re-layouts: 0.68 us -> 1.71 us
  transfers between devices with their start and end apart: 22 -> 17, of which waited for: 8 -> 7; matrix products, arithmetic and copies ran while one was open for 7% -> 3% of each run, Pallas kernels for 6% -> 5%
where the time goes in v3:
time: 52.3 us; the launch traced here: 52.1 us
  starting transfers between devices  21.5 us (41%)
  waiting for transfers between devices  18.6 us (36%)
  Pallas kernels  6.66 us (13%)
  local copies, waits for them, and re-layouts  3.77 us (7%)
  between operations  1.08 us (2%)
    ppermute x9, starting transfers between devices, layer_swap(): return x if shift == 0 else lax.ppermute(x, 'patch', pairs)  16.5 us
    ppermute x9, waiting for transfers between devices, layer_swap(): return x if shift == 0 else lax.ppermute(x, 'patch', pairs)  12.1 us
    ppermute x1, waiting for transfers between devices, other_column(): lax.ppermute(x, 'patch', [(p, p ^ 1) for p in range(layers * COLUMNS)])  5.25 us
    pallas_call x1, Pallas kernels, call_both(): pl.pallas_call(functools.partial(both_kernel, parts=parts), out_shape=[ja...  4.06 us
    pallas_call x1, Pallas kernels, pack(): pl.pallas_call(kernel, out_shape=[jax.ShapeDtypeStruct(shape, BF16) for s...  2.6 us
    ppermute x5, starting transfers between devices, other_core(): return lax.ppermute(x, 'uly', [(0, 1), (1, 0)])  2.04 us
    unnamed x13, local copies, waits for them, and re-layouts  1.71 us
    ppermute x1, starting transfers between devices, other_column(): lax.ppermute(x, 'patch', [(p, p ^ 1) for p in range(layers * COLUMNS)])  1.58 us
  transfers between devices with their start and end apart: 17, of which 7 were waited for; matrix products, arithmetic and copies ran while one was open for 3% of the time, Pallas kernels for 5%

profile of v3, /device:TPU:0, one launch (start us, length us, event | category | flops | bytes accessed | tf_op | source)
XLA Modules:
  0.0 52.1 jit_solution(12175273152212513694)
XLA Ops:
  0.7 0.9 %slice-done = bf16[2,48,1536]{2,1,0:T(8,128)(2,1)S(1)} async-done(((bf16[3,48,1536]{2,1,0:T(8,128)(2,1)}), bf16[2,48,1536]{2,1,0:T(8,128)(2,1)S(1)}, s32[]{:S(2)}) %slice-start) | async-done | bytes 294936 | tf_op jit(solution)/shard_map/slice | solution.py:282
  1.7 3.1 %collective-permute-start.7 = (bf16[2,48,384]{2,1,0:T(8,128)(2,1)S(1)}, bf16[2,48,384]{2,1,0:T(8,128)(2,1)S(1)}, u32[]{:S(2)}, u32[]{:S(2)}) collective-permute-start(bf16[2,48,384]{2,1,0:T(8,128)(2,1)S(1)} %get-tuple-element.34), channel_id=1, source_target_pairs={{0,4},{2,6},{4,8},{6,10},{8,12},{10,14},{12,0},{14,2},{1,5},{3,7},... | collective-permute-start | bytes 221192 | tf_op jit(solution)/shard_map/ppermute | solution.py:261
  4.8 2.6 %collective-permute-start.8 = (bf16[2,48,384]{2,1,0:T(8,128)(2,1)S(1)}, bf16[2,48,384]{2,1,0:T(8,128)(2,1)S(1)}, u32[]{:S(2)}, u32[]{:S(2)}) collective-permute-start(bf16[2,48,384]{2,1,0:T(8,128)(2,1)S(1)} %get-tuple-element.33), channel_id=1, source_target_pairs={{0,8},{2,10},{4,12},{6,14},{8,0},{10,2},{12,4},{14,6},{1,9},{3,11}... | collective-permute-start | bytes 221192 | tf_op jit(solution)/shard_map/ppermute | solution.py:261
  7.4 1.3 %collective-permute-start.9 = (bf16[2,48,384]{2,1,0:T(8,128)(2,1)S(1)}, bf16[2,48,384]{2,1,0:T(8,128)(2,1)S(1)}, u32[]{:S(2)}, u32[]{:S(2)}) collective-permute-start(bf16[2,48,384]{2,1,0:T(8,128)(2,1)S(1)} %get-tuple-element.32), channel_id=1, source_target_pairs={{0,12},{2,14},{4,0},{6,2},{8,4},{10,6},{12,8},{14,10},{1,13},{3,15... | collective-permute-start | bytes 221192 | tf_op jit(solution)/shard_map/ppermute | solution.py:261
  8.8 0.7 %collective-permute-start.5 = (bf16[2,96,384]{2,1,0:T(8,128)(2,1)S(1)}, bf16[2,96,384]{2,1,0:T(8,128)(2,1)S(1)}, u32[]{:S(2)}, u32[]{:S(2)}) collective-permute-start(bf16[2,96,384]{2,1,0:T(8,128)(2,1)S(1)} %get-tuple-element.37), channel_id=1, source_target_pairs={{0,0},{1,8},{2,2},{3,10},{4,4},{5,12},{6,6},{7,14},{8,1},{9,9},{10... | collective-permute-start | bytes 442376 | tf_op jit(solution)/shard_map/ppermute | solution.py:270
  9.5 0.7 %collective-permute-start.6 = (bf16[2,96,384]{2,1,0:T(8,128)(2,1)S(1)}, bf16[2,96,384]{2,1,0:T(8,128)(2,1)S(1)}, u32[]{:S(2)}, u32[]{:S(2)}) collective-permute-start(bf16[2,96,384]{2,1,0:T(8,128)(2,1)S(1)} %get-tuple-element.36), channel_id=1, source_target_pairs={{0,4},{1,12},{2,6},{3,14},{4,0},{5,8},{6,2},{7,10},{8,5},{9,13},{1... | collective-permute-start | bytes 442376 | tf_op jit(solution)/shard_map/ppermute | solution.py:270
  10.2 2.6 %shard_map.77 = (bf16[4,48,384]{2,1,0:T(8,128)(2,1)}, bf16[4,48,384]{2,1,0:T(8,128)(2,1)}, bf16[4,48,384]{2,1,0:T(8,128)(2,1)}, bf16[4,48,384]{2,1,0:T(8,128)(2,1)}, bf16[4,256,384]{2,1,0:T(8,128)(2,1)}) custom-call(bf16[3,48,1536]{2,1,0:T(8,128)(2,1)} %first_ref, bf16[3,48,1536]{2,1,0:T(8,128)(2,1)} %second_ref.1, bf16[2,256,768]{2,1,0:T(8,128)(2,1)} %text_first_ref.1, ...), custom_call_target="tpu_custom_call" | custom-call | bytes 1048576 | tf_op jit(solution)/shard_map/pallas_call | solution.py:144
  12.8 1.0 %constant_dynamic-update-slice_fusion.3 = bf16[4,192,384]{2,1,0:T(8,128)(2,1)S(1)} fusion(bf16[4,48,384]{2,1,0:T(8,128)(2,1)} %get-tuple-element.15), kind=kLoop, calls=%fused_computation.7 | loop fusion | bytes 294912
  13.9 0.7 %copy-done.2 = s32[2,12]{1,0:T(2,128)S(1)} copy-done((s32[2,12]{1,0:T(2,128)S(1)}, s32[2,12]{1,0:T(2,128)}, u32[]{:S(2)}) %copy-start.2) | copy-done | bytes 120
  14.6 0.1 fusion.2.scale_ref
  14.7 0.1 fusion.3
  14.8 0.1 pad.9.clone
  14.9 1.4 %collective-permute-start = (bf16[4,48,384]{2,1,0:T(8,128)(2,1)}, bf16[4,48,384]{2,1,0:T(8,128)(2,1)S(1)}, u32[]{:S(2)}, u32[]{:S(2)}) collective-permute-start(bf16[4,48,384]{2,1,0:T(8,128)(2,1)} %get-tuple-element.16), channel_id=1, source_target_pairs={{0,4},{2,6},{4,8},{6,10},{8,12},{10,14},{12,0},{14,2},{1,5},{3,7},... | collective-permute-start | bytes 442376 | tf_op jit(solution)/shard_map/ppermute | solution.py:261
  16.3 3.5 %collective-permute-start.1 = (bf16[4,48,384]{2,1,0:T(8,128)(2,1)S(1)}, bf16[4,48,384]{2,1,0:T(8,128)(2,1)S(1)}, u32[]{:S(2)}, u32[]{:S(2)}) collective-permute-start(bf16[4,48,384]{2,1,0:T(8,128)(2,1)S(1)} %copy-done.4), channel_id=1, source_target_pairs={{0,8},{2,10},{4,12},{6,14},{8,0},{10,2},{12,4},{14,6},{1,9},{3,11}... | collective-permute-start | bytes 442376 | tf_op jit(solution)/shard_map/ppermute | solution.py:261
  19.8 0.8 %collective-permute-start.2 = (bf16[4,48,384]{2,1,0:T(8,128)(2,1)S(1)}, bf16[4,48,384]{2,1,0:T(8,128)(2,1)S(1)}, u32[]{:S(2)}, u32[]{:S(2)}) collective-permute-start(bf16[4,48,384]{2,1,0:T(8,128)(2,1)S(1)} %copy-done.3), channel_id=1, source_target_pairs={{0,12},{2,14},{4,0},{6,2},{8,4},{10,6},{12,8},{14,10},{1,13},{3,15... | collective-permute-start | bytes 442376 | tf_op jit(solution)/shard_map/ppermute | solution.py:261
  20.7 0.1 pad_maximum_fusion.refs_0_
  20.8 1.6 %collective-permute-start.11 = (bf16[8,96,384]{2,1,0:T(8,128)(2,1)S(1)}, bf16[8,96,384]{2,1,0:T(8,128)(2,1)S(1)}, u32[]{:S(2)}, u32[]{:S(2)}) collective-permute-start(bf16[8,96,384]{2,1,0:T(8,128)(2,1)S(1)} %pad_maximum_fusion.refs_0_), channel_id=1, source_target_pairs={{0,2},{2,0},{4,6},{6,4},{8,10},{10,8},{12,14},{14,12},{1,3},{3,1},... | collective-permute-start | bytes 1769480 | tf_op jit(solution)/shard_map/ppermute | solution.py:273
  22.3 1.2 %collective-permute-done = bf16[4,48,384]{2,1,0:T(8,128)(2,1)S(1)} collective-permute-done((bf16[4,48,384]{2,1,0:T(8,128)(2,1)}, bf16[4,48,384]{2,1,0:T(8,128)(2,1)S(1)}, u32[]{:S(2)}, u32[]{:S(2)}) %collective-permute-start) | collective-permute-done | bytes 147488 | tf_op jit(solution)/shard_map/ppermute | solution.py:261
  23.5 1.4 %collective-permute-start.3 = (bf16[4,256,384]{2,1,0:T(8,128)(2,1)S(1)}, bf16[4,256,384]{2,1,0:T(8,128)(2,1)S(1)}, u32[]{:S(2)}, u32[]{:S(2)}) collective-permute-start(bf16[4,256,384]{2,1,0:T(8,128)(2,1)S(1)} %copy-done), channel_id=1, source_target_pairs={{0,1},{1,0},{2,3},{3,2},{4,5},{5,4},{6,7},{7,6},{8,9},{9,8},{10,11... | collective-permute-start | bytes 2359304 | tf_op jit(solution)/shard_map/ppermute | solution.py:276
  24.9 5.6 %collective-permute-done.1 = bf16[4,48,384]{2,1,0:T(8,128)(2,1)S(1)} collective-permute-done((bf16[4,48,384]{2,1,0:T(8,128)(2,1)S(1)}, bf16[4,48,384]{2,1,0:T(8,128)(2,1)S(1)}, u32[]{:S(2)}, u32[]{:S(2)}) %collective-permute-start.1) | collective-permute-done | bytes 147488 | tf_op jit(solution)/shard_map/ppermute | solution.py:261
  30.8 5.2 %collective-permute-done.11.refs_2_ = bf16[8,96,384]{2,1,0:T(8,128)(2,1)S(1)} collective-permute-done((bf16[8,96,384]{2,1,0:T(8,128)(2,1)S(1)}, bf16[8,96,384]{2,1,0:T(8,128)(2,1)S(1)}, u32[]{:S(2)}, u32[]{:S(2)}) %collective-permute-start.11) | collective-permute-done | bytes 589856 | tf_op jit(solution)/shard_map/ppermute | solution.py:273
  36.2 0.5 collective-permute-start.13
  36.7 0.1 add_bitcast_fusion
  36.8 0.9 %collective-permute-done.12.refs_3_ = bf16[4,96,384]{2,1,0:T(8,128)(2,1)S(1)} collective-permute-done((bf16[4,96,384]{2,1,0:T(8,128)(2,1)S(1)}, bf16[4,96,384]{2,1,0:T(8,128)(2,1)S(1)}, u32[]{:S(2)}, u32[]{:S(2)}) %collective-permute-start.12) | collective-permute-done | bytes 294944 | tf_op jit(solution)/shard_map/ppermute | solution.py:276
  37.7 0.4 collective-permute-done.13.refs_4_
  38.2 4.1 %shard_map.78 = (bf16[2,48,384]{2,1,0:T(8,128)(2,1)S(1)}, bf16[2,48,384]{2,1,0:T(8,128)(2,1)S(1)}, bf16[2,48,384]{2,1,0:T(8,128)(2,1)S(1)}, bf16[2,48,384]{2,1,0:T(8,128)(2,1)S(1)}) custom-call(f32[2,3]{1,0:T(2,128)S(1)} %fusion.2.scale_ref, s32[3,4]{1,0:T(4,128)S(1)} %add_add_fusion.order_ref, bf16[2,192,384]{2,1,0:T(8,128)(2,1)S(1)} %get-tuple-element.29.queries_ref, ...), custom_call_target="tpu_custom_call" | custom-call | flops 603979776 | bytes 3440640 | tf_op jit(solution)/shard_map/pallas_call | solution.py:233
  42.2 0.7 %collective-permute-start.14 = (bf16[2,48,384]{2,1,0:T(8,128)(2,1)S(1)}, bf16[2,48,384]{2,1,0:T(8,128)(2,1)S(1)}, u32[]{:S(2)}, u32[]{:S(2)}) collective-permute-start(bf16[2,48,384]{2,1,0:T(8,128)(2,1)S(1)} %get-tuple-element.23), channel_id=1, source_target_pairs={{0,12},{2,14},{4,0},{6,2},{8,4},{10,6},{12,8},{14,10},{1,13},{3,15... | collective-permute-start | bytes 221192 | tf_op jit(solution)/shard_map/ppermute | solution.py:261
  42.9 1.3 %collective-permute-start.15 = (bf16[2,48,384]{2,1,0:T(8,128)(2,1)S(1)}, bf16[2,48,384]{2,1,0:T(8,128)(2,1)S(1)}, u32[]{:S(2)}, u32[]{:S(2)}) collective-permute-start(bf16[2,48,384]{2,1,0:T(8,128)(2,1)S(1)} %get-tuple-element.24), channel_id=1, source_target_pairs={{0,8},{2,10},{4,12},{6,14},{8,0},{10,2},{12,4},{14,6},{1,9},{3,11}... | collective-permute-start | bytes 221192 | tf_op jit(solution)/shard_map/ppermute | solution.py:261
  44.2 1.7 %collective-permute-start.16 = (bf16[2,48,384]{2,1,0:T(8,128)(2,1)S(1)}, bf16[2,48,384]{2,1,0:T(8,128)(2,1)S(1)}, u32[]{:S(2)}, u32[]{:S(2)}) collective-permute-start(bf16[2,48,384]{2,1,0:T(8,128)(2,1)S(1)} %get-tuple-element.25), channel_id=1, source_target_pairs={{0,4},{2,6},{4,8},{6,10},{8,12},{10,14},{12,0},{14,2},{1,5},{3,7},... | collective-permute-start | bytes 221192 | tf_op jit(solution)/shard_map/ppermute | solution.py:261
  46.0 1.2 %collective-permute-done.14 = bf16[2,48,384]{2,1,0:T(8,128)(2,1)S(1)} collective-permute-done((bf16[2,48,384]{2,1,0:T(8,128)(2,1)S(1)}, bf16[2,48,384]{2,1,0:T(8,128)(2,1)S(1)}, u32[]{:S(2)}, u32[]{:S(2)}) %collective-permute-start.14) | collective-permute-done | bytes 73760 | tf_op jit(solution)/shard_map/ppermute | solution.py:261
  47.2 4.1 %collective-permute-done.15 = bf16[2,48,384]{2,1,0:T(8,128)(2,1)S(1)} collective-permute-done((bf16[2,48,384]{2,1,0:T(8,128)(2,1)S(1)}, bf16[2,48,384]{2,1,0:T(8,128)(2,1)S(1)}, u32[]{:S(2)}, u32[]{:S(2)}) %collective-permute-start.15) | collective-permute-done | bytes 73760 | tf_op jit(solution)/shard_map/ppermute | solution.py:261
  51.4 0.7 %slice_bitcast_fusion = (bf16[48,1536]{1,0:T(8,128)(2,1)}, bf16[48,1536]{1,0:T(8,128)(2,1)}) fusion(bf16[2,48,1536]{2,1,0:T(8,128)(2,1)S(1)} %constant_dynamic-update-slice_fusion.4), kind=kLoop, calls=%fused_computation.2 | loop fusion | bytes 589824 | tf_op jit(solution)/shard_map/squeeze | solution.py:320
  (37 shorter events, 0.7 us)
Async XLA Ops:
  0.7 1.0 %slice-start = ((bf16[3,48,1536]{2,1,0:T(8,128)(2,1)}), bf16[2,48,1536]{2,1,0:T(8,128)(2,1)S(1)}, s32[]{:S(2)}) async-start(bf16[3,48,1536]{2,1,0:T(8,128)(2,1)} %first_ref), calls=%async_computation | async-start | bytes 589824 | tf_op jit(solution)/shard_map/slice | solution.py:282
  1.7 7.1 %copy-start.1 = (bf16[2,96,768]{2,1,0:T(8,128)(2,1)S(1)}, bf16[2,96,768]{2,1,0:T(8,128)(2,1)}, u32[]{:S(2)}) copy-start(bf16[2,96,768]{2,1,0:T(8,128)(2,1)} %param.8) | copy-start | bytes 884740
  1.7 13.1 %collective-permute-start.7 = (bf16[2,48,384]{2,1,0:T(8,128)(2,1)S(1)}, bf16[2,48,384]{2,1,0:T(8,128)(2,1)S(1)}, u32[]{:S(2)}, u32[]{:S(2)}) collective-permute-start(bf16[2,48,384]{2,1,0:T(8,128)(2,1)S(1)} %get-tuple-element.34), channel_id=1, source_target_pairs={{0,4},{2,6},{4,8},{6,10},{8,12},{10,14},{12,0},{14,2},{1,5},{3,7},... | collective-permute-start | bytes 221192 | tf_op jit(solution)/shard_map/ppermute | solution.py:261
  4.8 11.5 %collective-permute-start.8 = (bf16[2,48,384]{2,1,0:T(8,128)(2,1)S(1)}, bf16[2,48,384]{2,1,0:T(8,128)(2,1)S(1)}, u32[]{:S(2)}, u32[]{:S(2)}) collective-permute-start(bf16[2,48,384]{2,1,0:T(8,128)(2,1)S(1)} %get-tuple-element.33), channel_id=1, source_target_pairs={{0,8},{2,10},{4,12},{6,14},{8,0},{10,2},{12,4},{14,6},{1,9},{3,11}... | collective-permute-start | bytes 221192 | tf_op jit(solution)/shard_map/ppermute | solution.py:261
  7.4 12.4 %collective-permute-start.9 = (bf16[2,48,384]{2,1,0:T(8,128)(2,1)S(1)}, bf16[2,48,384]{2,1,0:T(8,128)(2,1)S(1)}, u32[]{:S(2)}, u32[]{:S(2)}) collective-permute-start(bf16[2,48,384]{2,1,0:T(8,128)(2,1)S(1)} %get-tuple-element.32), channel_id=1, source_target_pairs={{0,12},{2,14},{4,0},{6,2},{8,4},{10,6},{12,8},{14,10},{1,13},{3,15... | collective-permute-start | bytes 221192 | tf_op jit(solution)/shard_map/ppermute | solution.py:261
  8.8 11.9 %collective-permute-start.5 = (bf16[2,96,384]{2,1,0:T(8,128)(2,1)S(1)}, bf16[2,96,384]{2,1,0:T(8,128)(2,1)S(1)}, u32[]{:S(2)}, u32[]{:S(2)}) collective-permute-start(bf16[2,96,384]{2,1,0:T(8,128)(2,1)S(1)} %get-tuple-element.37), channel_id=1, source_target_pairs={{0,0},{1,8},{2,2},{3,10},{4,4},{5,12},{6,6},{7,14},{8,1},{9,9},{10... | collective-permute-start | bytes 442376 | tf_op jit(solution)/shard_map/ppermute | solution.py:270
  9.5 11.2 %collective-permute-start.6 = (bf16[2,96,384]{2,1,0:T(8,128)(2,1)S(1)}, bf16[2,96,384]{2,1,0:T(8,128)(2,1)S(1)}, u32[]{:S(2)}, u32[]{:S(2)}) collective-permute-start(bf16[2,96,384]{2,1,0:T(8,128)(2,1)S(1)} %get-tuple-element.36), channel_id=1, source_target_pairs={{0,4},{1,12},{2,6},{3,14},{4,0},{5,8},{6,2},{7,10},{8,5},{9,13},{1... | collective-permute-start | bytes 442376 | tf_op jit(solution)/shard_map/ppermute | solution.py:270
  12.8 3.5 %copy-start.4 = (bf16[4,48,384]{2,1,0:T(8,128)(2,1)S(1)}, bf16[4,48,384]{2,1,0:T(8,128)(2,1)}, u32[]{:S(2)}) copy-start(bf16[4,48,384]{2,1,0:T(8,128)(2,1)} %get-tuple-element.17) | copy-start | bytes 442372
  12.8 7.0 %copy-start.3 = (bf16[4,48,384]{2,1,0:T(8,128)(2,1)S(1)}, bf16[4,48,384]{2,1,0:T(8,128)(2,1)}, u32[]{:S(2)}) copy-start(bf16[4,48,384]{2,1,0:T(8,128)(2,1)} %get-tuple-element.18) | copy-start | bytes 442372
  13.9 0.7 %copy-start.2 = (s32[2,12]{1,0:T(2,128)S(1)}, s32[2,12]{1,0:T(2,128)}, u32[]{:S(2)}) copy-start(s32[2,12]{1,0:T(2,128)} %param.9) | copy-start | bytes 292
  14.9 8.6 %copy-start = (bf16[4,256,384]{2,1,0:T(8,128)(2,1)S(1)}, bf16[4,256,384]{2,1,0:T(8,128)(2,1)}, u32[]{:S(2)}) copy-start(bf16[4,256,384]{2,1,0:T(8,128)(2,1)} %get-tuple-element.20.text_ref) | copy-start | bytes 2359300
  14.9 8.6 %collective-permute-start = (bf16[4,48,384]{2,1,0:T(8,128)(2,1)}, bf16[4,48,384]{2,1,0:T(8,128)(2,1)S(1)}, u32[]{:S(2)}, u32[]{:S(2)}) collective-permute-start(bf16[4,48,384]{2,1,0:T(8,128)(2,1)} %get-tuple-element.16), channel_id=1, source_target_pairs={{0,4},{2,6},{4,8},{6,10},{8,12},{10,14},{12,0},{14,2},{1,5},{3,7},... | collective-permute-start | bytes 442376 | tf_op jit(solution)/shard_map/ppermute | solution.py:261
  16.3 14.3 %collective-permute-start.1 = (bf16[4,48,384]{2,1,0:T(8,128)(2,1)S(1)}, bf16[4,48,384]{2,1,0:T(8,128)(2,1)S(1)}, u32[]{:S(2)}, u32[]{:S(2)}) collective-permute-start(bf16[4,48,384]{2,1,0:T(8,128)(2,1)S(1)} %copy-done.4), channel_id=1, source_target_pairs={{0,8},{2,10},{4,12},{6,14},{8,0},{10,2},{12,4},{14,6},{1,9},{3,11}... | collective-permute-start | bytes 442376 | tf_op jit(solution)/shard_map/ppermute | solution.py:261
  19.8 10.8 %collective-permute-start.2 = (bf16[4,48,384]{2,1,0:T(8,128)(2,1)S(1)}, bf16[4,48,384]{2,1,0:T(8,128)(2,1)S(1)}, u32[]{:S(2)}, u32[]{:S(2)}) collective-permute-start(bf16[4,48,384]{2,1,0:T(8,128)(2,1)S(1)} %copy-done.3), channel_id=1, source_target_pairs={{0,12},{2,14},{4,0},{6,2},{8,4},{10,6},{12,8},{14,10},{1,13},{3,15... | collective-permute-start | bytes 442376 | tf_op jit(solution)/shard_map/ppermute | solution.py:261
  20.8 15.3 %collective-permute-start.11 = (bf16[8,96,384]{2,1,0:T(8,128)(2,1)S(1)}, bf16[8,96,384]{2,1,0:T(8,128)(2,1)S(1)}, u32[]{:S(2)}, u32[]{:S(2)}) collective-permute-start(bf16[8,96,384]{2,1,0:T(8,128)(2,1)S(1)} %pad_maximum_fusion.refs_0_), channel_id=1, source_target_pairs={{0,2},{2,0},{4,6},{6,4},{8,10},{10,8},{12,14},{14,12},{1,3},{3,1},... | collective-permute-start | bytes 1769480 | tf_op jit(solution)/shard_map/ppermute | solution.py:273
  22.3 14.5 %collective-permute-start.10 = (bf16[8,96,384]{2,1,0:T(8,128)(2,1)S(1)}, bf16[8,96,384]{2,1,0:T(8,128)(2,1)S(1)}, u32[]{:S(2)}, u32[]{:S(2)}) collective-permute-start(bf16[8,96,384]{2,1,0:T(8,128)(2,1)S(1)} %pad_maximum_fusion.refs_0_), channel_id=1, source_target_pairs={{0,1},{1,0},{2,3},{3,2},{4,5},{5,4},{6,7},{7,6},{8,9},{9,8},{10,11... | collective-permute-start | bytes 1769480 | tf_op jit(solution)/shard_map/ppermute | solution.py:276
  23.5 13.3 %collective-permute-start.3 = (bf16[4,256,384]{2,1,0:T(8,128)(2,1)S(1)}, bf16[4,256,384]{2,1,0:T(8,128)(2,1)S(1)}, u32[]{:S(2)}, u32[]{:S(2)}) collective-permute-start(bf16[4,256,384]{2,1,0:T(8,128)(2,1)S(1)} %copy-done), channel_id=1, source_target_pairs={{0,1},{1,0},{2,3},{3,2},{4,5},{5,4},{6,7},{7,6},{8,9},{9,8},{10,11... | collective-permute-start | bytes 2359304 | tf_op jit(solution)/shard_map/ppermute | solution.py:276
  30.7 6.1 %collective-permute-start.4 = (bf16[2,192,384]{2,1,0:T(8,128)(2,1)S(1)}, bf16[2,192,384]{2,1,0:T(8,128)(2,1)S(1)}, u32[]{:S(2)}, u32[]{:S(2)}) collective-permute-start(bf16[2,192,384]{2,1,0:T(8,128)(2,1)S(1)} %get-tuple-element.28), channel_id=1, source_target_pairs={{0,1},{1,0},{2,3},{3,2},{4,5},{5,4},{6,7},{7,6},{8,9},{9,8},{10,11... | collective-permute-start | bytes 884744 | tf_op jit(solution)/shard_map/ppermute | solution.py:276
  36.1 1.6 %collective-permute-start.12 = (bf16[4,96,384]{2,1,0:T(8,128)(2,1)S(1)}, bf16[4,96,384]{2,1,0:T(8,128)(2,1)S(1)}, u32[]{:S(2)}, u32[]{:S(2)}) collective-permute-start(bf16[4,96,384]{2,1,0:T(8,128)(2,1)S(1)} %get-tuple-element.27), channel_id=1, source_target_pairs={{0,1},{1,0},{2,3},{3,2},{4,5},{5,4},{6,7},{7,6},{8,9},{9,8},{10,11... | collective-permute-start | bytes 884744 | tf_op jit(solution)/shard_map/ppermute | solution.py:276
  36.2 2.0 %collective-permute-start.13 = (bf16[4,96,384]{2,1,0:T(8,128)(2,1)S(1)}, bf16[4,96,384]{2,1,0:T(8,128)(2,1)S(1)}, u32[]{:S(2)}, u32[]{:S(2)}) collective-permute-start(bf16[4,96,384]{2,1,0:T(8,128)(2,1)S(1)} %get-tuple-element.26), channel_id=1, source_target_pairs={{0,1},{1,0},{2,3},{3,2},{4,5},{5,4},{6,7},{7,6},{8,9},{9,8},{10,11... | collective-permute-start | bytes 884744 | tf_op jit(solution)/shard_map/ppermute | solution.py:276
  42.2 5.0 %collective-permute-start.14 = (bf16[2,48,384]{2,1,0:T(8,128)(2,1)S(1)}, bf16[2,48,384]{2,1,0:T(8,128)(2,1)S(1)}, u32[]{:S(2)}, u32[]{:S(2)}) collective-permute-start(bf16[2,48,384]{2,1,0:T(8,128)(2,1)S(1)} %get-tuple-element.23), channel_id=1, source_target_pairs={{0,12},{2,14},{4,0},{6,2},{8,4},{10,6},{12,8},{14,10},{1,13},{3,15... | collective-permute-start | bytes 221192 | tf_op jit(solution)/shard_map/ppermute | solution.py:261
  42.9 8.4 %collective-permute-start.15 = (bf16[2,48,384]{2,1,0:T(8,128)(2,1)S(1)}, bf16[2,48,384]{2,1,0:T(8,128)(2,1)S(1)}, u32[]{:S(2)}, u32[]{:S(2)}) collective-permute-start(bf16[2,48,384]{2,1,0:T(8,128)(2,1)S(1)} %get-tuple-element.24), channel_id=1, source_target_pairs={{0,8},{2,10},{4,12},{6,14},{8,0},{10,2},{12,4},{14,6},{1,9},{3,11}... | collective-permute-start | bytes 221192 | tf_op jit(solution)/shard_map/ppermute | solution.py:261
  44.2 7.1 %collective-permute-start.16 = (bf16[2,48,384]{2,1,0:T(8,128)(2,1)S(1)}, bf16[2,48,384]{2,1,0:T(8,128)(2,1)S(1)}, u32[]{:S(2)}, u32[]{:S(2)}) collective-permute-start(bf16[2,48,384]{2,1,0:T(8,128)(2,1)S(1)} %get-tuple-element.25), channel_id=1, source_target_pairs={{0,4},{2,6},{4,8},{6,10},{8,12},{10,14},{12,0},{14,2},{1,5},{3,7},... | collective-permute-start | bytes 221192 | tf_op jit(solution)/shard_map/ppermute | solution.py:261

commit v4 on v3

--- a/solution.py
+++ b/solution.py
@@ -8,6 +8,7 @@
 from jax.sharding import PartitionSpec as P
 
 HEAD = 128
+LOG2E = 1.4426950408889634
 COLUMNS = 2
 BF16 = jnp.bfloat16
 F32 = jnp.float32
@@ -78,27 +79,25 @@
     return jnp.dot(a, b, preferred_element_type=F32)
 
 
-def attend(q, text, own, near, away, inside, key_factor, value_factor):
-    inverse = 1.0 / HEAD**0.5
-    scores = [
-        dot_t(q, text[0]) * inverse,
-        jnp.where(inside, dot_t(q, own[0]) * inverse, dot_t(q, near[0]) * key_factor),
-        dot_t(q, away[0]) * key_factor,
-    ]
-    top = functools.reduce(jnp.maximum, [s.max(-1, keepdims=True) for s in scores])
-    weights = [jnp.exp(s - top) for s in scores]
-    total = functools.reduce(jnp.add, [w.sum(-1, keepdims=True) for w in weights])
-    w_text, w_near, w_away = [w.astype(BF16) for w in weights]
+def scores_of(q, text, own, near, away, inside, key_factor):
+    first, second = text[0].shape[0], near[0].shape[0]
+    fixed = dot_t(q, jnp.concatenate([text[0], own[0]], 0)) * (LOG2E / HEAD**0.5)
+    far = dot_t(q, jnp.concatenate([near[0], away[0]], 0)) * (key_factor * LOG2E)
+    return jnp.concatenate([fixed[:, :first], jnp.where(inside, fixed[:, first:], far[:, :second]), far[:, second:]], 1)
+
+
+def weights_of(score):
+    weight = jnp.exp2(score - score.max(-1, keepdims=True))
+    return weight.astype(BF16), weight.sum(-1, keepdims=True)
+
+
+def mix(rounded, total, text, own, near, away, inside, value_factor):
+    first, second = text[0].shape[0], near[0].shape[0]
+    w_text, w_near, w_away = rounded[:, :first], rounded[:, first : first + second], rounded[:, first + second :]
     zero = jnp.zeros((), BF16)
-    kept = dot(w_text, text[1]) + dot(jnp.where(inside, w_near, zero), own[1])
-    far = dot(jnp.where(inside, zero, w_near), near[1]) + dot(w_away, away[1])
+    kept = dot(jnp.concatenate([w_text, jnp.where(inside, w_near, zero)], 1), jnp.concatenate([text[1], own[1]], 0))
+    far = dot(jnp.concatenate([jnp.where(inside, zero, w_near), w_away], 1), jnp.concatenate([near[1], away[1]], 0))
     return (kept + value_factor * far) / total
-
-
-def store_blocks(out_refs, result, lanes):
-    rows = out_refs[0].shape[0]
-    for i, out_ref in enumerate(out_refs):
-        out_ref[:, lanes] = result[i * rows : (i + 1) * rows].astype(BF16)
 
 
 def kernel_columns(ref, index):
@@ -151,26 +150,27 @@
     )(*operands)
 
 
-def both_kernel(scale_ref, order_ref, queries_ref, text_ref, text_twin_ref, last_ref, last_twin_ref, *refs, parts):
+def both_kernel(scale_ref, order_ref, queries_ref, text_ref, text_twin_ref, last_ref, last_twin_ref, *refs, parts, blocks, layers):
     sets, refs = [], list(refs)
     for p in parts:
         sets.append(refs[:p])
         refs = refs[p:]
     near_sets, away_sets = sets[:2], sets[2:]
     out_refs = refs
-    layers = len(out_refs)
     rounds = layers // 2
     count, width = queries_ref.shape[1:]
     rows = count // layers
+    first_row, last_row = blocks[0] * rows, (blocks[-1] + 1) * rows
     inverse = 1.0 / HEAD**0.5
-    shape = (count, 2 * count)
-    query_block = lax.broadcasted_iota(jnp.int32, shape, 0) // rows
+    shape = (last_row - first_row, 2 * count)
+    query_block = lax.broadcasted_iota(jnp.int32, shape, 0) // rows + blocks[0]
     place = lax.broadcasted_iota(jnp.int32, shape, 1)
     inside = [query_block == place // (2 * rows), query_block == place % count // rows]
 
     def fresh_view(pieces):
         return (pieces[1], 0) if len(pieces) == 2 else (pieces[0], layers)
 
+    work = []
     for step in range(2):
         for head in range(width // HEAD):
             lanes = slice(head * HEAD, (head + 1) * HEAD)
@@ -212,32 +212,34 @@
                 own = [last(i) for i in range(2)]
                 near = [fresh_all(near_sets, i) for i in range(2)]
                 away = [fresh_all(away_sets, i) for i in range(2)]
-            result = attend(
-                queries_ref[step, :, lanes],
-                [text(i) for i in range(2)],
-                own,
-                near,
-                away,
-                inside[step],
-                inverse if step else scale_ref[0, head] * inverse,
-                1.0 if step else scale_ref[1, head],
-            )
-            for i, out_ref in enumerate(out_refs):
-                out_ref[step, :, lanes] = result[i * rows : (i + 1) * rows].astype(BF16)
-
-
-def call_both(layers, scalars, parts, *operands):
+            parts_of = ([text(i) for i in range(2)], own, near, away)
+            work.append((step, head, lanes, parts_of))
+    scores = [
+        scores_of(queries_ref[step, first_row:last_row, lanes], *p, inside[step], inverse if step else scale_ref[0, head] * inverse)
+        for step, head, lanes, p in work
+    ]
+    weights = [weights_of(s) for s in scores]
+    for (step, head, lanes, p), (rounded, total) in zip(work, weights):
+        result = mix(rounded, total, *p, inside[step], 1.0 if step else scale_ref[1, head])
+        for i, out_ref in enumerate(out_refs):
+            out_ref[step, :, lanes] = result[i * rows : (i + 1) * rows].astype(BF16)
+
+
+def call_both(layers, scalars, parts, blocks, *operands):
     count, width = operands[0].shape[1:]
+    rows = count // layers
     keys = 2 * operands[1].shape[1] + 8 * count
     in_vmem = pl.BlockSpec(memory_space=pltpu.VMEM)
     return pl.pallas_call(
-        functools.partial(both_kernel, parts=parts),
-        out_shape=[jax.ShapeDtypeStruct((2, count // layers, width), BF16)] * layers,
+        functools.partial(both_kernel, parts=parts, blocks=blocks, layers=layers),
+        out_shape=[jax.ShapeDtypeStruct((2, rows, width), BF16)] * len(blocks),
         in_specs=[pl.BlockSpec(memory_space=pltpu.SMEM)] * len(scalars) + [in_vmem] * len(operands),
-        out_specs=[in_vmem] * layers,
+        out_specs=[in_vmem] * len(blocks),
         compiler_params=pltpu.CompilerParams(vmem_limit_bytes=32 * 1024 * 1024),
         cost_estimate=pl.CostEstimate(
-            flops=4 * count * keys * width, bytes_accessed=4 * width * (keys + count), transcendentals=count * keys * width // HEAD
+            flops=4 * rows * len(blocks) * keys * width,
+            bytes_accessed=4 * width * (keys + count),
+            transcendentals=rows * len(blocks) * keys * width // HEAD,
         ),
     )(*scalars, *operands)
 
@@ -296,12 +298,13 @@
     stale_block = jnp.concatenate(stale, 0)
     near = jnp.concatenate([stale_block, fresh_block], 0)
     away = [other_column(near)]
+    owned = [owned[0], owned[1], after(owned[2], near), after(owned[3], near)]
     owned = {s: layer_swap(owned[s], s) for s in (0, 2, 1, 3)}
     owned = [owned[s] for s in range(layers)]
     away_twin = [other_core(away[0][:layers]), other_core(away[0][layers:])]
     last = jnp.concatenate(owned, 1)
     near_twin = [other_core(near)]
-    last_twin = other_core(last[2:])
+    last_twin = other_core(last)
     text_twin = other_core(after(text, owned[1]))
     sets = [[near], near_twin, away, away_twin]
 
@@ -312,7 +315,10 @@
     )
     parts = tuple(len(p) for p in sets)
     flat = [p for pieces in sets for p in pieces]
-    blocks = call_both(layers, [scales, order], parts, last[:2], text, text_twin, last, last_twin, *flat)
+    operands = [last[:2], text, text_twin, last, last_twin, *flat]
+    sent = call_both(layers, [scales, order], parts, tuple(range(1, layers)), *operands)
+    (kept,) = call_both(layers, [scales, order], parts, (0,), *operands)
+    blocks = [kept, *sent]
 
     out = jnp.zeros((2, rows, features), BF16)
     for s in range(layers):

time: 52.3 us -> 50.4 us (0.964)
  waiting for transfers between devices: 18.6 us -> 9.02 us
  starting transfers between devices: 21.5 us -> 28.2 us
  Pallas kernels: 6.66 us -> 8.44 us
  local copies, waits for them, and re-layouts: 3.77 us -> 3.03 us
    ppermute x9, starting transfers between devices: 16.5 us -> 24.2 us  [layer_swap(): return x if shift == 0 else lax.ppermute(x, 'patch', pairs)]
    ppermute x9, waiting for transfers between devices: 12.1 us -> 6.7 us  [layer_swap(): return x if shift == 0 else lax.ppermute(x, 'patch', pairs)]
    ppermute x1, waiting for transfers between devices: 5.25 us -> 0.01 us  [other_column(): lax.ppermute(x, 'patch', [(p, p ^ 1) for p in range(layers * COLUMNS)])]
    pallas_call x1 -> x2, Pallas kernels: 4.06 us -> 5.85 us  [call_both(): pl.pallas_call(functools.partial(both_kernel, parts=parts, blocks=blocks,...]
    ppermute x5, starting transfers between devices: 2.04 us -> 0.78 us  [other_core(): return lax.ppermute(x, 'uly', [(0, 1), (1, 0)])]
    unnamed x13 -> x11, local copies, waits for them, and re-layouts: 1.71 us -> 0.99 us
    ppermute x2, waiting for transfers between devices: 0.01 us -> 0.57 us  [stale_round(): return lax.ppermute(x, ('patch', 'uly'), pairs)]
  transfers between devices with their start and end apart: 17 -> 17, of which waited for: 7 -> 7; matrix products, arithmetic and copies ran while one was open for 3% -> 3% of each run, Pallas kernels for 5% -> 10%
where the time goes in v4:
time: 50.4 us; the launch traced here: 50.2 us
  starting transfers between devices  28.2 us (56%)
  waiting for transfers between devices  9.02 us (18%)
  Pallas kernels  8.44 us (17%)
  local copies, waits for them, and re-layouts  3.03 us (6%)
  between operations  1.06 us (2%)
    ppermute x9, starting transfers between devices, layer_swap(): return x if shift == 0 else lax.ppermute(x, 'patch', pairs)  24.2 us
    ppermute x9, waiting for transfers between devices, layer_swap(): return x if shift == 0 else lax.ppermute(x, 'patch', pairs)  6.7 us
    pallas_call x2, Pallas kernels, call_both(): pl.pallas_call(functools.partial(both_kernel, parts=parts, blocks=blocks,...  5.85 us
    pallas_call x1, Pallas kernels, pack(): pl.pallas_call(kernel, out_shape=[jax.ShapeDtypeStruct(shape, BF16) for s...  2.59 us
    ppermute x1, starting transfers between devices, other_column(): lax.ppermute(x, 'patch', [(p, p ^ 1) for p in range(layers * COLUMNS)])  1.8 us
    ppermute x5, waiting for transfers between devices, other_core(): return lax.ppermute(x, 'uly', [(0, 1), (1, 0)])  1.75 us
    ppermute x2, starting transfers between devices, stale_round(): return lax.ppermute(x, ('patch', 'uly'), pairs)  1.41 us
  transfers between devices with their start and end apart: 17, of which 7 were waited for; matrix products, arithmetic and copies ran while one was open for 3% of the time, Pallas kernels for 10%

profile of v4, /device:TPU:0, one launch (start us, length us, event | category | flops | bytes accessed | tf_op | source)
XLA Modules:
  0.0 50.2 jit_solution(16346809868630400723)
XLA Ops:
  0.7 0.9 %slice-done = bf16[2,48,1536]{2,1,0:T(8,128)(2,1)S(1)} async-done(((bf16[3,48,1536]{2,1,0:T(8,128)(2,1)}), bf16[2,48,1536]{2,1,0:T(8,128)(2,1)S(1)}, s32[]{:S(2)}) %slice-start) | async-done | bytes 294936 | tf_op jit(solution)/shard_map/slice | solution.py:284
  1.7 3.1 %collective-permute-start.3 = (bf16[2,48,384]{2,1,0:T(8,128)(2,1)S(1)}, bf16[2,48,384]{2,1,0:T(8,128)(2,1)S(1)}, u32[]{:S(2)}, u32[]{:S(2)}) collective-permute-start(bf16[2,48,384]{2,1,0:T(8,128)(2,1)S(1)} %get-tuple-element.34), channel_id=1, source_target_pairs={{0,4},{2,6},{4,8},{6,10},{8,12},{10,14},{12,0},{14,2},{1,5},{3,7},... | collective-permute-start | bytes 221192 | tf_op jit(solution)/shard_map/ppermute | solution.py:263
  4.8 2.6 %collective-permute-start.4 = (bf16[2,48,384]{2,1,0:T(8,128)(2,1)S(1)}, bf16[2,48,384]{2,1,0:T(8,128)(2,1)S(1)}, u32[]{:S(2)}, u32[]{:S(2)}) collective-permute-start(bf16[2,48,384]{2,1,0:T(8,128)(2,1)S(1)} %get-tuple-element.33), channel_id=1, source_target_pairs={{0,8},{2,10},{4,12},{6,14},{8,0},{10,2},{12,4},{14,6},{1,9},{3,11}... | collective-permute-start | bytes 221192 | tf_op jit(solution)/shard_map/ppermute | solution.py:263
  7.4 1.3 %collective-permute-start.5 = (bf16[2,48,384]{2,1,0:T(8,128)(2,1)S(1)}, bf16[2,48,384]{2,1,0:T(8,128)(2,1)S(1)}, u32[]{:S(2)}, u32[]{:S(2)}) collective-permute-start(bf16[2,48,384]{2,1,0:T(8,128)(2,1)S(1)} %get-tuple-element.32), channel_id=1, source_target_pairs={{0,12},{2,14},{4,0},{6,2},{8,4},{10,6},{12,8},{14,10},{1,13},{3,15... | collective-permute-start | bytes 221192 | tf_op jit(solution)/shard_map/ppermute | solution.py:263
  8.8 0.7 %collective-permute-start.1 = (bf16[2,96,384]{2,1,0:T(8,128)(2,1)S(1)}, bf16[2,96,384]{2,1,0:T(8,128)(2,1)S(1)}, u32[]{:S(2)}, u32[]{:S(2)}) collective-permute-start(bf16[2,96,384]{2,1,0:T(8,128)(2,1)S(1)} %get-tuple-element.37), channel_id=1, source_target_pairs={{0,0},{1,8},{2,2},{3,10},{4,4},{5,12},{6,6},{7,14},{8,1},{9,9},{10... | collective-permute-start | bytes 442376 | tf_op jit(solution)/shard_map/ppermute | solution.py:272
  9.5 0.7 %collective-permute-start.2 = (bf16[2,96,384]{2,1,0:T(8,128)(2,1)S(1)}, bf16[2,96,384]{2,1,0:T(8,128)(2,1)S(1)}, u32[]{:S(2)}, u32[]{:S(2)}) collective-permute-start(bf16[2,96,384]{2,1,0:T(8,128)(2,1)S(1)} %get-tuple-element.36), channel_id=1, source_target_pairs={{0,4},{1,12},{2,6},{3,14},{4,0},{5,8},{6,2},{7,10},{8,5},{9,13},{1... | collective-permute-start | bytes 442376 | tf_op jit(solution)/shard_map/ppermute | solution.py:272
  10.2 2.6 %shard_map.77 = (bf16[4,48,384]{2,1,0:T(8,128)(2,1)}, bf16[4,48,384]{2,1,0:T(8,128)(2,1)}, bf16[4,48,384]{2,1,0:T(8,128)(2,1)}, bf16[4,48,384]{2,1,0:T(8,128)(2,1)}, bf16[4,256,384]{2,1,0:T(8,128)(2,1)}) custom-call(bf16[3,48,1536]{2,1,0:T(8,128)(2,1)} %first_ref, bf16[3,48,1536]{2,1,0:T(8,128)(2,1)} %second_ref.1, bf16[2,256,768]{2,1,0:T(8,128)(2,1)} %text_first_ref.1, ...), custom_call_target="tpu_custom_call" | custom-call | bytes 1048576 | tf_op jit(solution)/shard_map/pallas_call | solution.py:143
  12.8 1.4 %collective-permute-start = (bf16[4,48,384]{2,1,0:T(8,128)(2,1)}, bf16[4,48,384]{2,1,0:T(8,128)(2,1)S(1)}, u32[]{:S(2)}, u32[]{:S(2)}) collective-permute-start(bf16[4,48,384]{2,1,0:T(8,128)(2,1)} %get-tuple-element.17), channel_id=1, source_target_pairs={{0,4},{2,6},{4,8},{6,10},{8,12},{10,14},{12,0},{14,2},{1,5},{3,7},... | collective-permute-start | bytes 442376 | tf_op jit(solution)/shard_map/ppermute | solution.py:263
  14.3 0.6 %collective-permute-done.2 = bf16[2,96,384]{2,1,0:T(8,128)(2,1)S(1)} collective-permute-done((bf16[2,96,384]{2,1,0:T(8,128)(2,1)S(1)}, bf16[2,96,384]{2,1,0:T(8,128)(2,1)S(1)}, u32[]{:S(2)}, u32[]{:S(2)}) %collective-permute-start.2) | collective-permute-done | bytes 147488 | tf_op jit(solution)/shard_map/ppermute | solution.py:272
  14.8 0.1 pad_maximum_fusion.refs_0_
  14.9 1.8 %collective-permute-start.11 = (bf16[8,96,384]{2,1,0:T(8,128)(2,1)S(1)}, bf16[8,96,384]{2,1,0:T(8,128)(2,1)S(1)}, u32[]{:S(2)}, u32[]{:S(2)}) collective-permute-start(bf16[8,96,384]{2,1,0:T(8,128)(2,1)S(1)} %pad_maximum_fusion.refs_0_), channel_id=1, source_target_pairs={{0,2},{2,0},{4,6},{6,4},{8,10},{10,8},{12,14},{14,12},{1,3},{3,1},... | collective-permute-start | bytes 1769480 | tf_op jit(solution)/shard_map/ppermute | solution.py:275
  16.8 8.0 %collective-permute-start.6 = (bf16[4,48,384]{2,1,0:T(8,128)(2,1)}, bf16[4,48,384]{2,1,0:T(8,128)(2,1)}, u32[]{:S(2)}, u32[]{:S(2)}) collective-permute-start(bf16[4,48,384]{2,1,0:T(8,128)(2,1)} %get-tuple-element.21), channel_id=1, source_target_pairs={{0,8},{2,10},{4,12},{6,14},{8,0},{10,2},{12,4},{14,6},{1,9},{3,11}... | collective-permute-start | bytes 442376 | tf_op jit(solution)/shard_map/ppermute | solution.py:263
  24.8 0.1 fusion.2.scale_ref
  25.0 2.9 %collective-permute-start.7 = (bf16[4,48,384]{2,1,0:T(8,128)(2,1)}, bf16[4,48,384]{2,1,0:T(8,128)(2,1)S(1)}, u32[]{:S(2)}, u32[]{:S(2)}) collective-permute-start(bf16[4,48,384]{2,1,0:T(8,128)(2,1)} %get-tuple-element.22), channel_id=1, source_target_pairs={{0,12},{2,14},{4,0},{6,2},{8,4},{10,6},{12,8},{14,10},{1,13},{3,15... | collective-permute-start | bytes 442376 | tf_op jit(solution)/shard_map/ppermute | solution.py:263
  28.0 0.5 collective-permute-done.6
  28.4 0.9 %constant_dynamic-update-slice_fusion.1 = bf16[4,192,384]{2,1,0:T(8,128)(2,1)S(1)} fusion(bf16[4,192,384]{2,1,0:T(8,128)(2,1)S(1)} %constant_dynamic-update-slice_fusion.2, bf16[4,48,384]{2,1,0:T(8,128)(2,1)} %collective-permute-done.6), kind=kLoop, calls=%fused_computation.5 | loop fusion | bytes 294912
  29.4 2.2 %collective-permute-done.7 = bf16[4,48,384]{2,1,0:T(8,128)(2,1)S(1)} collective-permute-done((bf16[4,48,384]{2,1,0:T(8,128)(2,1)}, bf16[4,48,384]{2,1,0:T(8,128)(2,1)S(1)}, u32[]{:S(2)}, u32[]{:S(2)}) %collective-permute-start.7) | collective-permute-done | bytes 147488 | tf_op jit(solution)/shard_map/ppermute | solution.py:263
  31.7 0.1 fusion.3
  31.8 0.1 pad.9.clone
  32.0 0.6 %collective-permute-start.12 = (bf16[4,96,384]{2,1,0:T(8,128)(2,1)S(1)}, bf16[4,96,384]{2,1,0:T(8,128)(2,1)S(1)}, u32[]{:S(2)}, u32[]{:S(2)}) collective-permute-start(bf16[4,96,384]{2,1,0:T(8,128)(2,1)S(1)} %get-tuple-element.29), channel_id=1, source_target_pairs={{0,1},{1,0},{2,3},{3,2},{4,5},{5,4},{6,7},{7,6},{8,9},{9,8},{10,11... | collective-permute-start | bytes 884744 | tf_op jit(solution)/shard_map/ppermute | solution.py:278
  32.5 0.1 collective-permute-start.13
  32.6 0.1 add_bitcast_fusion
  32.7 0.1 add_add_fusion.order_ref
  32.8 1.0 %collective-permute-done.9.last_twin_ref = bf16[4,192,384]{2,1,0:T(8,128)(2,1)} collective-permute-done((bf16[4,192,384]{2,1,0:T(8,128)(2,1)S(1)}, bf16[4,192,384]{2,1,0:T(8,128)(2,1)}, u32[]{:S(2)}, u32[]{:S(2)}) %collective-permute-start.9) | collective-permute-done | bytes 589856 | tf_op jit(solution)/shard_map/ppermute | solution.py:278
  33.8 0.3 collective-permute-done.12.refs_3_
  34.1 0.4 collective-permute-done.13.refs_4_
  34.5 3.3 %shard_map.79 = (bf16[2,48,384]{2,1,0:T(8,128)(2,1)S(1)}, bf16[2,48,384]{2,1,0:T(8,128)(2,1)S(1)}, bf16[2,48,384]{2,1,0:T(8,128)(2,1)S(1)}) custom-call(f32[2,3]{1,0:T(2,128)S(1)} %fusion.2.scale_ref, s32[3,4]{1,0:T(4,128)S(1)} %add_add_fusion.order_ref, bf16[2,192,384]{2,1,0:T(8,128)(2,1)S(1)} %slice.27.queries_ref, bf16[4,256,384]{2,1,0:T(8,128)(2,1)S(1)} %copy-done, ...), custom_call_target="tpu_custom_call" | custom-call | flops 452984832 | bytes 3440640 | tf_op jit(solution)/shard_map/pallas_call | solution.py:233
  37.8 4.2 %collective-permute-start.14 = (bf16[2,48,384]{2,1,0:T(8,128)(2,1)S(1)}, bf16[2,48,384]{2,1,0:T(8,128)(2,1)S(1)}, u32[]{:S(2)}, u32[]{:S(2)}) collective-permute-start(bf16[2,48,384]{2,1,0:T(8,128)(2,1)S(1)} %get-tuple-element.25), channel_id=1, source_target_pairs={{0,12},{2,14},{4,0},{6,2},{8,4},{10,6},{12,8},{14,10},{1,13},{3,15... | collective-permute-start | bytes 221192 | tf_op jit(solution)/shard_map/ppermute | solution.py:263
  42.1 0.6 %collective-permute-start.16 = (bf16[2,48,384]{2,1,0:T(8,128)(2,1)S(1)}, bf16[2,48,384]{2,1,0:T(8,128)(2,1)S(1)}, u32[]{:S(2)}, u32[]{:S(2)}) collective-permute-start(bf16[2,48,384]{2,1,0:T(8,128)(2,1)S(1)} %get-tuple-element.27), channel_id=1, source_target_pairs={{0,4},{2,6},{4,8},{6,10},{8,12},{10,14},{12,0},{14,2},{1,5},{3,7},... | collective-permute-start | bytes 221192 | tf_op jit(solution)/shard_map/ppermute | solution.py:263
  42.7 2.6 %shard_map.78 = bf16[2,48,384]{2,1,0:T(8,128)(2,1)S(1)} custom-call(f32[2,3]{1,0:T(2,128)S(1)} %fusion.2.scale_ref, s32[3,4]{1,0:T(4,128)S(1)} %add_add_fusion.order_ref, bf16[2,192,384]{2,1,0:T(8,128)(2,1)S(1)} %slice.27.queries_ref, bf16[4,256,384]{2,1,0:T(8,128)(2,1)S(1)} %copy-done, bf16[4,256,384]{2,1,0:T(8,128)(2,1)S(1)} %collective-permute-done.8.text_twin_ref, ...), custom_call_target="tpu_custom_call" | custom-call | flops 150994944 | bytes 3440640 | tf_op jit(solution)/shard_map/pallas_call | solution.py:233
  45.4 4.0 %collective-permute-done.15 = bf16[2,48,384]{2,1,0:T(8,128)(2,1)S(1)} collective-permute-done((bf16[2,48,384]{2,1,0:T(8,128)(2,1)S(1)}, bf16[2,48,384]{2,1,0:T(8,128)(2,1)S(1)}, u32[]{:S(2)}, u32[]{:S(2)}) %collective-permute-start.15) | collective-permute-done | bytes 73760 | tf_op jit(solution)/shard_map/ppermute | solution.py:263
  49.4 0.7 %slice_bitcast_fusion = (bf16[48,1536]{1,0:T(8,128)(2,1)}, bf16[48,1536]{1,0:T(8,128)(2,1)}) fusion(bf16[2,48,1536]{2,1,0:T(8,128)(2,1)S(1)} %constant_dynamic-update-slice_fusion.4), kind=kLoop, calls=%fused_computation.2 | loop fusion | bytes 589824 | tf_op jit(solution)/shard_map/squeeze | solution.py:326
  (36 shorter events, 0.6 us)
Async XLA Ops:
  0.7 1.0 %slice-start = ((bf16[3,48,1536]{2,1,0:T(8,128)(2,1)}), bf16[2,48,1536]{2,1,0:T(8,128)(2,1)S(1)}, s32[]{:S(2)}) async-start(bf16[3,48,1536]{2,1,0:T(8,128)(2,1)} %first_ref), calls=%async_computation | async-start | bytes 589824 | tf_op jit(solution)/shard_map/slice | solution.py:284
  1.7 7.1 %copy-start.1 = (bf16[2,96,768]{2,1,0:T(8,128)(2,1)S(1)}, bf16[2,96,768]{2,1,0:T(8,128)(2,1)}, u32[]{:S(2)}) copy-start(bf16[2,96,768]{2,1,0:T(8,128)(2,1)} %param.8) | copy-start | bytes 884740
  1.7 11.1 %collective-permute-start.3 = (bf16[2,48,384]{2,1,0:T(8,128)(2,1)S(1)}, bf16[2,48,384]{2,1,0:T(8,128)(2,1)S(1)}, u32[]{:S(2)}, u32[]{:S(2)}) collective-permute-start(bf16[2,48,384]{2,1,0:T(8,128)(2,1)S(1)} %get-tuple-element.34), channel_id=1, source_target_pairs={{0,4},{2,6},{4,8},{6,10},{8,12},{10,14},{12,0},{14,2},{1,5},{3,7},... | collective-permute-start | bytes 221192 | tf_op jit(solution)/shard_map/ppermute | solution.py:263
  4.8 9.4 %collective-permute-start.4 = (bf16[2,48,384]{2,1,0:T(8,128)(2,1)S(1)}, bf16[2,48,384]{2,1,0:T(8,128)(2,1)S(1)}, u32[]{:S(2)}, u32[]{:S(2)}) collective-permute-start(bf16[2,48,384]{2,1,0:T(8,128)(2,1)S(1)} %get-tuple-element.33), channel_id=1, source_target_pairs={{0,8},{2,10},{4,12},{6,14},{8,0},{10,2},{12,4},{14,6},{1,9},{3,11}... | collective-permute-start | bytes 221192 | tf_op jit(solution)/shard_map/ppermute | solution.py:263
  7.4 6.8 %collective-permute-start.5 = (bf16[2,48,384]{2,1,0:T(8,128)(2,1)S(1)}, bf16[2,48,384]{2,1,0:T(8,128)(2,1)S(1)}, u32[]{:S(2)}, u32[]{:S(2)}) collective-permute-start(bf16[2,48,384]{2,1,0:T(8,128)(2,1)S(1)} %get-tuple-element.32), channel_id=1, source_target_pairs={{0,12},{2,14},{4,0},{6,2},{8,4},{10,6},{12,8},{14,10},{1,13},{3,15... | collective-permute-start | bytes 221192 | tf_op jit(solution)/shard_map/ppermute | solution.py:263
  8.8 5.5 %collective-permute-start.1 = (bf16[2,96,384]{2,1,0:T(8,128)(2,1)S(1)}, bf16[2,96,384]{2,1,0:T(8,128)(2,1)S(1)}, u32[]{:S(2)}, u32[]{:S(2)}) collective-permute-start(bf16[2,96,384]{2,1,0:T(8,128)(2,1)S(1)} %get-tuple-element.37), channel_id=1, source_target_pairs={{0,0},{1,8},{2,2},{3,10},{4,4},{5,12},{6,6},{7,14},{8,1},{9,9},{10... | collective-permute-start | bytes 442376 | tf_op jit(solution)/shard_map/ppermute | solution.py:272
  9.5 5.4 %collective-permute-start.2 = (bf16[2,96,384]{2,1,0:T(8,128)(2,1)S(1)}, bf16[2,96,384]{2,1,0:T(8,128)(2,1)S(1)}, u32[]{:S(2)}, u32[]{:S(2)}) collective-permute-start(bf16[2,96,384]{2,1,0:T(8,128)(2,1)S(1)} %get-tuple-element.36), channel_id=1, source_target_pairs={{0,4},{1,12},{2,6},{3,14},{4,0},{5,8},{6,2},{7,10},{8,5},{9,13},{1... | collective-permute-start | bytes 442376 | tf_op jit(solution)/shard_map/ppermute | solution.py:272
  12.8 15.1 %collective-permute-start = (bf16[4,48,384]{2,1,0:T(8,128)(2,1)}, bf16[4,48,384]{2,1,0:T(8,128)(2,1)S(1)}, u32[]{:S(2)}, u32[]{:S(2)}) collective-permute-start(bf16[4,48,384]{2,1,0:T(8,128)(2,1)} %get-tuple-element.17), channel_id=1, source_target_pairs={{0,4},{2,6},{4,8},{6,10},{8,12},{10,14},{12,0},{14,2},{1,5},{3,7},... | collective-permute-start | bytes 442376 | tf_op jit(solution)/shard_map/ppermute | solution.py:263
  14.8 1.9 %copy-start.2 = (bf16[4,48,384]{2,1,0:T(8,128)(2,1)S(1)}, bf16[4,48,384]{2,1,0:T(8,128)(2,1)}, u32[]{:S(2)}) copy-start(bf16[4,48,384]{2,1,0:T(8,128)(2,1)} %get-tuple-element.16) | copy-start | bytes 442372
  14.8 13.1 %copy-start = (bf16[4,256,384]{2,1,0:T(8,128)(2,1)S(1)}, bf16[4,256,384]{2,1,0:T(8,128)(2,1)}, u32[]{:S(2)}) copy-start(bf16[4,256,384]{2,1,0:T(8,128)(2,1)} %get-tuple-element.24.text_ref) | copy-start | bytes 2359300
  14.9 17.0 %collective-permute-start.11 = (bf16[8,96,384]{2,1,0:T(8,128)(2,1)S(1)}, bf16[8,96,384]{2,1,0:T(8,128)(2,1)S(1)}, u32[]{:S(2)}, u32[]{:S(2)}) collective-permute-start(bf16[8,96,384]{2,1,0:T(8,128)(2,1)S(1)} %pad_maximum_fusion.refs_0_), channel_id=1, source_target_pairs={{0,2},{2,0},{4,6},{6,4},{8,10},{10,8},{12,14},{14,12},{1,3},{3,1},... | collective-permute-start | bytes 1769480 | tf_op jit(solution)/shard_map/ppermute | solution.py:275
  16.8 8.0 %copy-start.3 = (s32[2,12]{1,0:T(2,128)S(1)}, s32[2,12]{1,0:T(2,128)}, u32[]{:S(2)}) copy-start(s32[2,12]{1,0:T(2,128)} %param.9) | copy-start | bytes 292
  16.8 11.7 %collective-permute-start.6 = (bf16[4,48,384]{2,1,0:T(8,128)(2,1)}, bf16[4,48,384]{2,1,0:T(8,128)(2,1)}, u32[]{:S(2)}, u32[]{:S(2)}) collective-permute-start(bf16[4,48,384]{2,1,0:T(8,128)(2,1)} %get-tuple-element.21), channel_id=1, source_target_pairs={{0,8},{2,10},{4,12},{6,14},{8,0},{10,2},{12,4},{14,6},{1,9},{3,11}... | collective-permute-start | bytes 442376 | tf_op jit(solution)/shard_map/ppermute | solution.py:263
  24.9 7.8 %collective-permute-start.10 = (bf16[8,96,384]{2,1,0:T(8,128)(2,1)S(1)}, bf16[8,96,384]{2,1,0:T(8,128)(2,1)}, u32[]{:S(2)}, u32[]{:S(2)}) collective-permute-start(bf16[8,96,384]{2,1,0:T(8,128)(2,1)S(1)} %pad_maximum_fusion.refs_0_), channel_id=1, source_target_pairs={{0,1},{1,0},{2,3},{3,2},{4,5},{5,4},{6,7},{7,6},{8,9},{9,8},{10,11... | collective-permute-start | bytes 1769480 | tf_op jit(solution)/shard_map/ppermute | solution.py:278
  25.0 6.6 %collective-permute-start.7 = (bf16[4,48,384]{2,1,0:T(8,128)(2,1)}, bf16[4,48,384]{2,1,0:T(8,128)(2,1)S(1)}, u32[]{:S(2)}, u32[]{:S(2)}) collective-permute-start(bf16[4,48,384]{2,1,0:T(8,128)(2,1)} %get-tuple-element.22), channel_id=1, source_target_pairs={{0,12},{2,14},{4,0},{6,2},{8,4},{10,6},{12,8},{14,10},{1,13},{3,15... | collective-permute-start | bytes 442376 | tf_op jit(solution)/shard_map/ppermute | solution.py:263
  27.9 5.9 %collective-permute-start.8 = (bf16[4,256,384]{2,1,0:T(8,128)(2,1)S(1)}, bf16[4,256,384]{2,1,0:T(8,128)(2,1)S(1)}, u32[]{:S(2)}, u32[]{:S(2)}) collective-permute-start(bf16[4,256,384]{2,1,0:T(8,128)(2,1)S(1)} %copy-done), channel_id=1, source_target_pairs={{0,1},{1,0},{2,3},{3,2},{4,5},{5,4},{6,7},{7,6},{8,9},{9,8},{10,11... | collective-permute-start | bytes 2359304 | tf_op jit(solution)/shard_map/ppermute | solution.py:278
  31.6 2.2 %collective-permute-start.9 = (bf16[4,192,384]{2,1,0:T(8,128)(2,1)S(1)}, bf16[4,192,384]{2,1,0:T(8,128)(2,1)}, u32[]{:S(2)}, u32[]{:S(2)}) collective-permute-start(bf16[4,192,384]{2,1,0:T(8,128)(2,1)S(1)} %constant_dynamic-update-slice_fusion.last_ref), channel_id=1, source_target_pairs={{0,1},{1,0},{2,3},{3,2},{4,5},{5,4},{6,7},{7,6},{8,9},{9,8},{10,11... | collective-permute-start | bytes 1769480 | tf_op jit(solution)/shard_map/ppermute | solution.py:278
  32.0 2.2 %collective-permute-start.12 = (bf16[4,96,384]{2,1,0:T(8,128)(2,1)S(1)}, bf16[4,96,384]{2,1,0:T(8,128)(2,1)S(1)}, u32[]{:S(2)}, u32[]{:S(2)}) collective-permute-start(bf16[4,96,384]{2,1,0:T(8,128)(2,1)S(1)} %get-tuple-element.29), channel_id=1, source_target_pairs={{0,1},{1,0},{2,3},{3,2},{4,5},{5,4},{6,7},{7,6},{8,9},{9,8},{10,11... | collective-permute-start | bytes 884744 | tf_op jit(solution)/shard_map/ppermute | solution.py:278
  32.5 2.0 %collective-permute-start.13 = (bf16[4,96,384]{2,1,0:T(8,128)(2,1)S(1)}, bf16[4,96,384]{2,1,0:T(8,128)(2,1)S(1)}, u32[]{:S(2)}, u32[]{:S(2)}) collective-permute-start(bf16[4,96,384]{2,1,0:T(8,128)(2,1)S(1)} %get-tuple-element.28), channel_id=1, source_target_pairs={{0,1},{1,0},{2,3},{3,2},{4,5},{5,4},{6,7},{7,6},{8,9},{9,8},{10,11... | collective-permute-start | bytes 884744 | tf_op jit(solution)/shard_map/ppermute | solution.py:278
  37.8 7.5 %collective-permute-start.14 = (bf16[2,48,384]{2,1,0:T(8,128)(2,1)S(1)}, bf16[2,48,384]{2,1,0:T(8,128)(2,1)S(1)}, u32[]{:S(2)}, u32[]{:S(2)}) collective-permute-start(bf16[2,48,384]{2,1,0:T(8,128)(2,1)S(1)} %get-tuple-element.25), channel_id=1, source_target_pairs={{0,12},{2,14},{4,0},{6,2},{8,4},{10,6},{12,8},{14,10},{1,13},{3,15... | collective-permute-start | bytes 221192 | tf_op jit(solution)/shard_map/ppermute | solution.py:263
  42.1 7.3 %collective-permute-start.15 = (bf16[2,48,384]{2,1,0:T(8,128)(2,1)S(1)}, bf16[2,48,384]{2,1,0:T(8,128)(2,1)S(1)}, u32[]{:S(2)}, u32[]{:S(2)}) collective-permute-start(bf16[2,48,384]{2,1,0:T(8,128)(2,1)S(1)} %get-tuple-element.26), channel_id=1, source_target_pairs={{0,8},{2,10},{4,12},{6,14},{8,0},{10,2},{12,4},{14,6},{1,9},{3,11}... | collective-permute-start | bytes 221192 | tf_op jit(solution)/shard_map/ppermute | solution.py:263
  42.1 7.3 %collective-permute-start.16 = (bf16[2,48,384]{2,1,0:T(8,128)(2,1)S(1)}, bf16[2,48,384]{2,1,0:T(8,128)(2,1)S(1)}, u32[]{:S(2)}, u32[]{:S(2)}) collective-permute-start(bf16[2,48,384]{2,1,0:T(8,128)(2,1)S(1)} %get-tuple-element.27), channel_id=1, source_target_pairs={{0,4},{2,6},{4,8},{6,10},{8,12},{10,14},{12,0},{14,2},{1,5},{3,7},... | collective-permute-start | bytes 221192 | tf_op jit(solution)/shard_map/ppermute | solution.py:263

commit v5 on v4

--- a/solution.py
+++ b/solution.py
@@ -299,7 +299,7 @@
     near = jnp.concatenate([stale_block, fresh_block], 0)
     away = [other_column(near)]
     owned = [owned[0], owned[1], after(owned[2], near), after(owned[3], near)]
-    owned = {s: layer_swap(owned[s], s) for s in (0, 2, 1, 3)}
+    owned = {s: layer_swap(owned[s], s) for s in (0, 3, 2, 1)}
     owned = [owned[s] for s in range(layers)]
     away_twin = [other_core(away[0][:layers]), other_core(away[0][layers:])]
     last = jnp.concatenate(owned, 1)
@@ -321,7 +321,7 @@
     blocks = [kept, *sent]
 
     out = jnp.zeros((2, rows, features), BF16)
-    for s in range(layers):
+    for s in (0, 2, 3, 1):
         out = lax.dynamic_update_slice_in_dim(out, layer_swap(blocks[s], -s), (layer + s) % layers * width, 2)
     return out[0], out[1]
 

time: 50.4 us -> 48.7 us (0.966)
  waiting for transfers between devices: 9.02 us -> 6.41 us
  starting transfers between devices: 28.2 us -> 29.2 us
    ppermute x9, waiting for transfers between devices: 6.7 us -> 4.09 us  [layer_swap(): return x if shift == 0 else lax.ppermute(x, 'patch', pairs)]
    ppermute x9, starting transfers between devices: 24.2 us -> 25.2 us  [layer_swap(): return x if shift == 0 else lax.ppermute(x, 'patch', pairs)]
  transfers between devices with their start and end apart: 17 -> 17, of which waited for: 7 -> 8; matrix products, arithmetic and copies ran while one was open for 3% -> 3% of each run, Pallas kernels for 10% -> 11%
where the time goes in v5:
time: 48.7 us; the launch traced here: 48.5 us
  starting transfers between devices  29.2 us (60%)
  Pallas kernels  8.44 us (17%)
  waiting for transfers between devices  6.41 us (13%)
  local copies, waits for them, and re-layouts  3.02 us (6%)
  between operations  1.05 us (2%)
    ppermute x9, starting transfers between devices, layer_swap(): return x if shift == 0 else lax.ppermute(x, 'patch', pairs)  25.2 us
    pallas_call x2, Pallas kernels, call_both(): pl.pallas_call(functools.partial(both_kernel, parts=parts, blocks=blocks,...  5.85 us
    ppermute x9, waiting for transfers between devices, layer_swap(): return x if shift == 0 else lax.ppermute(x, 'patch', pairs)  4.09 us
    pallas_call x1, Pallas kernels, pack(): pl.pallas_call(kernel, out_shape=[jax.ShapeDtypeStruct(shape, BF16) for s...  2.59 us
    ppermute x1, starting transfers between devices, other_column(): lax.ppermute(x, 'patch', [(p, p ^ 1) for p in range(layers * COLUMNS)])  1.8 us
    ppermute x5, waiting for transfers between devices, other_core(): return lax.ppermute(x, 'uly', [(0, 1), (1, 0)])  1.75 us
    ppermute x2, starting transfers between devices, stale_round(): return lax.ppermute(x, ('patch', 'uly'), pairs)  1.41 us
    unnamed x11, local copies, waits for them, and re-layouts  0.99 us
  transfers between devices with their start and end apart: 17, of which 8 were waited for; matrix products, arithmetic and copies ran while one was open for 3% of the time, Pallas kernels for 11%

profile of v5, /device:TPU:0, one launch (start us, length us, event | category | flops | bytes accessed | tf_op | source)
XLA Modules:
  0.0 48.5 jit_solution(11996198681071364539)
XLA Ops:
  0.7 0.9 %slice-done = bf16[2,48,1536]{2,1,0:T(8,128)(2,1)S(1)} async-done(((bf16[3,48,1536]{2,1,0:T(8,128)(2,1)}), bf16[2,48,1536]{2,1,0:T(8,128)(2,1)S(1)}, s32[]{:S(2)}) %slice-start) | async-done | bytes 294936 | tf_op jit(solution)/shard_map/slice | solution.py:284
  1.7 3.1 %collective-permute-start.3 = (bf16[2,48,384]{2,1,0:T(8,128)(2,1)S(1)}, bf16[2,48,384]{2,1,0:T(8,128)(2,1)S(1)}, u32[]{:S(2)}, u32[]{:S(2)}) collective-permute-start(bf16[2,48,384]{2,1,0:T(8,128)(2,1)S(1)} %get-tuple-element.34), channel_id=1, source_target_pairs={{0,4},{2,6},{4,8},{6,10},{8,12},{10,14},{12,0},{14,2},{1,5},{3,7},... | collective-permute-start | bytes 221192 | tf_op jit(solution)/shard_map/ppermute | solution.py:263
  4.8 2.6 %collective-permute-start.4 = (bf16[2,48,384]{2,1,0:T(8,128)(2,1)S(1)}, bf16[2,48,384]{2,1,0:T(8,128)(2,1)S(1)}, u32[]{:S(2)}, u32[]{:S(2)}) collective-permute-start(bf16[2,48,384]{2,1,0:T(8,128)(2,1)S(1)} %get-tuple-element.33), channel_id=1, source_target_pairs={{0,8},{2,10},{4,12},{6,14},{8,0},{10,2},{12,4},{14,6},{1,9},{3,11}... | collective-permute-start | bytes 221192 | tf_op jit(solution)/shard_map/ppermute | solution.py:263
  7.4 1.3 %collective-permute-start.5 = (bf16[2,48,384]{2,1,0:T(8,128)(2,1)S(1)}, bf16[2,48,384]{2,1,0:T(8,128)(2,1)S(1)}, u32[]{:S(2)}, u32[]{:S(2)}) collective-permute-start(bf16[2,48,384]{2,1,0:T(8,128)(2,1)S(1)} %get-tuple-element.32), channel_id=1, source_target_pairs={{0,12},{2,14},{4,0},{6,2},{8,4},{10,6},{12,8},{14,10},{1,13},{3,15... | collective-permute-start | bytes 221192 | tf_op jit(solution)/shard_map/ppermute | solution.py:263
  8.8 0.7 %collective-permute-start.1 = (bf16[2,96,384]{2,1,0:T(8,128)(2,1)S(1)}, bf16[2,96,384]{2,1,0:T(8,128)(2,1)S(1)}, u32[]{:S(2)}, u32[]{:S(2)}) collective-permute-start(bf16[2,96,384]{2,1,0:T(8,128)(2,1)S(1)} %get-tuple-element.37), channel_id=1, source_target_pairs={{0,0},{1,8},{2,2},{3,10},{4,4},{5,12},{6,6},{7,14},{8,1},{9,9},{10... | collective-permute-start | bytes 442376 | tf_op jit(solution)/shard_map/ppermute | solution.py:272
  9.5 0.7 %collective-permute-start.2 = (bf16[2,96,384]{2,1,0:T(8,128)(2,1)S(1)}, bf16[2,96,384]{2,1,0:T(8,128)(2,1)S(1)}, u32[]{:S(2)}, u32[]{:S(2)}) collective-permute-start(bf16[2,96,384]{2,1,0:T(8,128)(2,1)S(1)} %get-tuple-element.36), channel_id=1, source_target_pairs={{0,4},{1,12},{2,6},{3,14},{4,0},{5,8},{6,2},{7,10},{8,5},{9,13},{1... | collective-permute-start | bytes 442376 | tf_op jit(solution)/shard_map/ppermute | solution.py:272
  10.2 2.6 %shard_map.77 = (bf16[4,48,384]{2,1,0:T(8,128)(2,1)}, bf16[4,48,384]{2,1,0:T(8,128)(2,1)}, bf16[4,48,384]{2,1,0:T(8,128)(2,1)}, bf16[4,48,384]{2,1,0:T(8,128)(2,1)}, bf16[4,256,384]{2,1,0:T(8,128)(2,1)}) custom-call(bf16[3,48,1536]{2,1,0:T(8,128)(2,1)} %first_ref, bf16[3,48,1536]{2,1,0:T(8,128)(2,1)} %second_ref.1, bf16[2,256,768]{2,1,0:T(8,128)(2,1)} %text_first_ref.1, ...), custom_call_target="tpu_custom_call" | custom-call | bytes 1048576 | tf_op jit(solution)/shard_map/pallas_call | solution.py:143
  12.8 1.4 %collective-permute-start = (bf16[4,48,384]{2,1,0:T(8,128)(2,1)}, bf16[4,48,384]{2,1,0:T(8,128)(2,1)S(1)}, u32[]{:S(2)}, u32[]{:S(2)}) collective-permute-start(bf16[4,48,384]{2,1,0:T(8,128)(2,1)} %get-tuple-element.17), channel_id=1, source_target_pairs={{0,4},{2,6},{4,8},{6,10},{8,12},{10,14},{12,0},{14,2},{1,5},{3,7},... | collective-permute-start | bytes 442376 | tf_op jit(solution)/shard_map/ppermute | solution.py:263
  14.3 0.6 %collective-permute-done.2 = bf16[2,96,384]{2,1,0:T(8,128)(2,1)S(1)} collective-permute-done((bf16[2,96,384]{2,1,0:T(8,128)(2,1)S(1)}, bf16[2,96,384]{2,1,0:T(8,128)(2,1)S(1)}, u32[]{:S(2)}, u32[]{:S(2)}) %collective-permute-start.2) | collective-permute-done | bytes 147488 | tf_op jit(solution)/shard_map/ppermute | solution.py:272
  14.8 0.1 pad_maximum_fusion.refs_0_
  14.9 1.8 %collective-permute-start.11 = (bf16[8,96,384]{2,1,0:T(8,128)(2,1)S(1)}, bf16[8,96,384]{2,1,0:T(8,128)(2,1)S(1)}, u32[]{:S(2)}, u32[]{:S(2)}) collective-permute-start(bf16[8,96,384]{2,1,0:T(8,128)(2,1)S(1)} %pad_maximum_fusion.refs_0_), channel_id=1, source_target_pairs={{0,2},{2,0},{4,6},{6,4},{8,10},{10,8},{12,14},{14,12},{1,3},{3,1},... | collective-permute-start | bytes 1769480 | tf_op jit(solution)/shard_map/ppermute | solution.py:275
  16.8 8.0 %collective-permute-start.6 = (bf16[4,48,384]{2,1,0:T(8,128)(2,1)}, bf16[4,48,384]{2,1,0:T(8,128)(2,1)}, u32[]{:S(2)}, u32[]{:S(2)}) collective-permute-start(bf16[4,48,384]{2,1,0:T(8,128)(2,1)} %get-tuple-element.21), channel_id=1, source_target_pairs={{0,8},{2,10},{4,12},{6,14},{8,0},{10,2},{12,4},{14,6},{1,9},{3,11}... | collective-permute-start | bytes 442376 | tf_op jit(solution)/shard_map/ppermute | solution.py:263
  24.8 0.1 fusion.2.scale_ref
  25.0 2.9 %collective-permute-start.7 = (bf16[4,48,384]{2,1,0:T(8,128)(2,1)}, bf16[4,48,384]{2,1,0:T(8,128)(2,1)S(1)}, u32[]{:S(2)}, u32[]{:S(2)}) collective-permute-start(bf16[4,48,384]{2,1,0:T(8,128)(2,1)} %get-tuple-element.22), channel_id=1, source_target_pairs={{0,12},{2,14},{4,0},{6,2},{8,4},{10,6},{12,8},{14,10},{1,13},{3,15... | collective-permute-start | bytes 442376 | tf_op jit(solution)/shard_map/ppermute | solution.py:263
  28.0 0.5 collective-permute-done.6
  28.4 0.9 %constant_dynamic-update-slice_fusion.1 = bf16[4,192,384]{2,1,0:T(8,128)(2,1)S(1)} fusion(bf16[4,192,384]{2,1,0:T(8,128)(2,1)S(1)} %constant_dynamic-update-slice_fusion.2, bf16[4,48,384]{2,1,0:T(8,128)(2,1)} %collective-permute-done.6), kind=kLoop, calls=%fused_computation.5 | loop fusion | bytes 294912
  29.4 2.2 %collective-permute-done.7 = bf16[4,48,384]{2,1,0:T(8,128)(2,1)S(1)} collective-permute-done((bf16[4,48,384]{2,1,0:T(8,128)(2,1)}, bf16[4,48,384]{2,1,0:T(8,128)(2,1)S(1)}, u32[]{:S(2)}, u32[]{:S(2)}) %collective-permute-start.7) | collective-permute-done | bytes 147488 | tf_op jit(solution)/shard_map/ppermute | solution.py:263
  31.7 0.1 fusion.3
  32.0 0.6 %collective-permute-start.12 = (bf16[4,96,384]{2,1,0:T(8,128)(2,1)S(1)}, bf16[4,96,384]{2,1,0:T(8,128)(2,1)S(1)}, u32[]{:S(2)}, u32[]{:S(2)}) collective-permute-start(bf16[4,96,384]{2,1,0:T(8,128)(2,1)S(1)} %get-tuple-element.29), channel_id=1, source_target_pairs={{0,1},{1,0},{2,3},{3,2},{4,5},{5,4},{6,7},{7,6},{8,9},{9,8},{10,11... | collective-permute-start | bytes 884744 | tf_op jit(solution)/shard_map/ppermute | solution.py:278
  32.5 0.1 collective-permute-start.13
  32.6 0.1 add_bitcast_fusion
  32.8 1.0 %collective-permute-done.9.last_twin_ref = bf16[4,192,384]{2,1,0:T(8,128)(2,1)} collective-permute-done((bf16[4,192,384]{2,1,0:T(8,128)(2,1)S(1)}, bf16[4,192,384]{2,1,0:T(8,128)(2,1)}, u32[]{:S(2)}, u32[]{:S(2)}) %collective-permute-start.9) | collective-permute-done | bytes 589856 | tf_op jit(solution)/shard_map/ppermute | solution.py:278
  33.8 0.3 collective-permute-done.12.refs_3_
  34.1 0.4 collective-permute-done.13.refs_4_
  34.5 3.3 %shard_map.79 = (bf16[2,48,384]{2,1,0:T(8,128)(2,1)S(1)}, bf16[2,48,384]{2,1,0:T(8,128)(2,1)S(1)}, bf16[2,48,384]{2,1,0:T(8,128)(2,1)S(1)}) custom-call(f32[2,3]{1,0:T(2,128)S(1)} %fusion.2.scale_ref, s32[3,4]{1,0:T(4,128)S(1)} %add_add_fusion.order_ref, bf16[2,192,384]{2,1,0:T(8,128)(2,1)S(1)} %slice.27.queries_ref, bf16[4,256,384]{2,1,0:T(8,128)(2,1)S(1)} %copy-done, ...), custom_call_target="tpu_custom_call" | custom-call | flops 452984832 | bytes 3440640 | tf_op jit(solution)/shard_map/pallas_call | solution.py:233
  37.8 2.0 %collective-permute-start.14 = (bf16[2,48,384]{2,1,0:T(8,128)(2,1)S(1)}, bf16[2,48,384]{2,1,0:T(8,128)(2,1)S(1)}, u32[]{:S(2)}, u32[]{:S(2)}) collective-permute-start(bf16[2,48,384]{2,1,0:T(8,128)(2,1)S(1)} %get-tuple-element.25), channel_id=1, source_target_pairs={{0,8},{2,10},{4,12},{6,14},{8,0},{10,2},{12,4},{14,6},{1,9},{3,11}... | collective-permute-start | bytes 221192 | tf_op jit(solution)/shard_map/ppermute | solution.py:263
  39.8 2.8 %collective-permute-start.15 = (bf16[2,48,384]{2,1,0:T(8,128)(2,1)S(1)}, bf16[2,48,384]{2,1,0:T(8,128)(2,1)S(1)}, u32[]{:S(2)}, u32[]{:S(2)}) collective-permute-start(bf16[2,48,384]{2,1,0:T(8,128)(2,1)S(1)} %get-tuple-element.26), channel_id=1, source_target_pairs={{0,4},{2,6},{4,8},{6,10},{8,12},{10,14},{12,0},{14,2},{1,5},{3,7},... | collective-permute-start | bytes 221192 | tf_op jit(solution)/shard_map/ppermute | solution.py:263
  42.6 1.0 %collective-permute-start.16 = (bf16[2,48,384]{2,1,0:T(8,128)(2,1)S(1)}, bf16[2,48,384]{2,1,0:T(8,128)(2,1)S(1)}, u32[]{:S(2)}, u32[]{:S(2)}) collective-permute-start(bf16[2,48,384]{2,1,0:T(8,128)(2,1)S(1)} %get-tuple-element.27), channel_id=1, source_target_pairs={{0,12},{2,14},{4,0},{6,2},{8,4},{10,6},{12,8},{14,10},{1,13},{3,15... | collective-permute-start | bytes 221192 | tf_op jit(solution)/shard_map/ppermute | solution.py:263
  43.7 2.5 %shard_map.78 = bf16[2,48,384]{2,1,0:T(8,128)(2,1)S(1)} custom-call(f32[2,3]{1,0:T(2,128)S(1)} %fusion.2.scale_ref, s32[3,4]{1,0:T(4,128)S(1)} %add_add_fusion.order_ref, bf16[2,192,384]{2,1,0:T(8,128)(2,1)S(1)} %slice.27.queries_ref, bf16[4,256,384]{2,1,0:T(8,128)(2,1)S(1)} %copy-done, bf16[4,256,384]{2,1,0:T(8,128)(2,1)S(1)} %collective-permute-done.8.text_twin_ref, ...), custom_call_target="tpu_custom_call" | custom-call | flops 150994944 | bytes 3440640 | tf_op jit(solution)/shard_map/pallas_call | solution.py:233
  46.3 1.1 %collective-permute-done.15 = bf16[2,48,384]{2,1,0:T(8,128)(2,1)S(1)} collective-permute-done((bf16[2,48,384]{2,1,0:T(8,128)(2,1)S(1)}, bf16[2,48,384]{2,1,0:T(8,128)(2,1)S(1)}, u32[]{:S(2)}, u32[]{:S(2)}) %collective-permute-start.15) | collective-permute-done | bytes 73760 | tf_op jit(solution)/shard_map/ppermute | solution.py:263
  47.4 0.3 collective-permute-done.16
  47.7 0.7 %slice_bitcast_fusion = (bf16[48,1536]{1,0:T(8,128)(2,1)}, bf16[48,1536]{1,0:T(8,128)(2,1)}) fusion(bf16[2,48,1536]{2,1,0:T(8,128)(2,1)S(1)} %constant_dynamic-update-slice_fusion.4), kind=kLoop, calls=%fused_computation.2 | loop fusion | bytes 589824 | tf_op jit(solution)/shard_map/squeeze | solution.py:326
  (36 shorter events, 0.7 us)
Async XLA Ops:
  0.7 1.0 %slice-start = ((bf16[3,48,1536]{2,1,0:T(8,128)(2,1)}), bf16[2,48,1536]{2,1,0:T(8,128)(2,1)S(1)}, s32[]{:S(2)}) async-start(bf16[3,48,1536]{2,1,0:T(8,128)(2,1)} %first_ref), calls=%async_computation | async-start | bytes 589824 | tf_op jit(solution)/shard_map/slice | solution.py:284
  1.7 7.1 %copy-start.1 = (bf16[2,96,768]{2,1,0:T(8,128)(2,1)S(1)}, bf16[2,96,768]{2,1,0:T(8,128)(2,1)}, u32[]{:S(2)}) copy-start(bf16[2,96,768]{2,1,0:T(8,128)(2,1)} %param.8) | copy-start | bytes 884740
  1.7 11.1 %collective-permute-start.3 = (bf16[2,48,384]{2,1,0:T(8,128)(2,1)S(1)}, bf16[2,48,384]{2,1,0:T(8,128)(2,1)S(1)}, u32[]{:S(2)}, u32[]{:S(2)}) collective-permute-start(bf16[2,48,384]{2,1,0:T(8,128)(2,1)S(1)} %get-tuple-element.34), channel_id=1, source_target_pairs={{0,4},{2,6},{4,8},{6,10},{8,12},{10,14},{12,0},{14,2},{1,5},{3,7},... | collective-permute-start | bytes 221192 | tf_op jit(solution)/shard_map/ppermute | solution.py:263
  4.8 9.4 %collective-permute-start.4 = (bf16[2,48,384]{2,1,0:T(8,128)(2,1)S(1)}, bf16[2,48,384]{2,1,0:T(8,128)(2,1)S(1)}, u32[]{:S(2)}, u32[]{:S(2)}) collective-permute-start(bf16[2,48,384]{2,1,0:T(8,128)(2,1)S(1)} %get-tuple-element.33), channel_id=1, source_target_pairs={{0,8},{2,10},{4,12},{6,14},{8,0},{10,2},{12,4},{14,6},{1,9},{3,11}... | collective-permute-start | bytes 221192 | tf_op jit(solution)/shard_map/ppermute | solution.py:263
  7.4 6.8 %collective-permute-start.5 = (bf16[2,48,384]{2,1,0:T(8,128)(2,1)S(1)}, bf16[2,48,384]{2,1,0:T(8,128)(2,1)S(1)}, u32[]{:S(2)}, u32[]{:S(2)}) collective-permute-start(bf16[2,48,384]{2,1,0:T(8,128)(2,1)S(1)} %get-tuple-element.32), channel_id=1, source_target_pairs={{0,12},{2,14},{4,0},{6,2},{8,4},{10,6},{12,8},{14,10},{1,13},{3,15... | collective-permute-start | bytes 221192 | tf_op jit(solution)/shard_map/ppermute | solution.py:263
  8.8 5.5 %collective-permute-start.1 = (bf16[2,96,384]{2,1,0:T(8,128)(2,1)S(1)}, bf16[2,96,384]{2,1,0:T(8,128)(2,1)S(1)}, u32[]{:S(2)}, u32[]{:S(2)}) collective-permute-start(bf16[2,96,384]{2,1,0:T(8,128)(2,1)S(1)} %get-tuple-element.37), channel_id=1, source_target_pairs={{0,0},{1,8},{2,2},{3,10},{4,4},{5,12},{6,6},{7,14},{8,1},{9,9},{10... | collective-permute-start | bytes 442376 | tf_op jit(solution)/shard_map/ppermute | solution.py:272
  9.5 5.4 %collective-permute-start.2 = (bf16[2,96,384]{2,1,0:T(8,128)(2,1)S(1)}, bf16[2,96,384]{2,1,0:T(8,128)(2,1)S(1)}, u32[]{:S(2)}, u32[]{:S(2)}) collective-permute-start(bf16[2,96,384]{2,1,0:T(8,128)(2,1)S(1)} %get-tuple-element.36), channel_id=1, source_target_pairs={{0,4},{1,12},{2,6},{3,14},{4,0},{5,8},{6,2},{7,10},{8,5},{9,13},{1... | collective-permute-start | bytes 442376 | tf_op jit(solution)/shard_map/ppermute | solution.py:272
  12.8 15.1 %collective-permute-start = (bf16[4,48,384]{2,1,0:T(8,128)(2,1)}, bf16[4,48,384]{2,1,0:T(8,128)(2,1)S(1)}, u32[]{:S(2)}, u32[]{:S(2)}) collective-permute-start(bf16[4,48,384]{2,1,0:T(8,128)(2,1)} %get-tuple-element.17), channel_id=1, source_target_pairs={{0,4},{2,6},{4,8},{6,10},{8,12},{10,14},{12,0},{14,2},{1,5},{3,7},... | collective-permute-start | bytes 442376 | tf_op jit(solution)/shard_map/ppermute | solution.py:263
  14.8 1.9 %copy-start.2 = (bf16[4,48,384]{2,1,0:T(8,128)(2,1)S(1)}, bf16[4,48,384]{2,1,0:T(8,128)(2,1)}, u32[]{:S(2)}) copy-start(bf16[4,48,384]{2,1,0:T(8,128)(2,1)} %get-tuple-element.16) | copy-start | bytes 442372
  14.8 13.1 %copy-start = (bf16[4,256,384]{2,1,0:T(8,128)(2,1)S(1)}, bf16[4,256,384]{2,1,0:T(8,128)(2,1)}, u32[]{:S(2)}) copy-start(bf16[4,256,384]{2,1,0:T(8,128)(2,1)} %get-tuple-element.24.text_ref) | copy-start | bytes 2359300
  14.9 17.0 %collective-permute-start.11 = (bf16[8,96,384]{2,1,0:T(8,128)(2,1)S(1)}, bf16[8,96,384]{2,1,0:T(8,128)(2,1)S(1)}, u32[]{:S(2)}, u32[]{:S(2)}) collective-permute-start(bf16[8,96,384]{2,1,0:T(8,128)(2,1)S(1)} %pad_maximum_fusion.refs_0_), channel_id=1, source_target_pairs={{0,2},{2,0},{4,6},{6,4},{8,10},{10,8},{12,14},{14,12},{1,3},{3,1},... | collective-permute-start | bytes 1769480 | tf_op jit(solution)/shard_map/ppermute | solution.py:275
  16.8 8.0 %copy-start.3 = (s32[2,12]{1,0:T(2,128)S(1)}, s32[2,12]{1,0:T(2,128)}, u32[]{:S(2)}) copy-start(s32[2,12]{1,0:T(2,128)} %param.9) | copy-start | bytes 292
  16.8 11.7 %collective-permute-start.6 = (bf16[4,48,384]{2,1,0:T(8,128)(2,1)}, bf16[4,48,384]{2,1,0:T(8,128)(2,1)}, u32[]{:S(2)}, u32[]{:S(2)}) collective-permute-start(bf16[4,48,384]{2,1,0:T(8,128)(2,1)} %get-tuple-element.21), channel_id=1, source_target_pairs={{0,8},{2,10},{4,12},{6,14},{8,0},{10,2},{12,4},{14,6},{1,9},{3,11}... | collective-permute-start | bytes 442376 | tf_op jit(solution)/shard_map/ppermute | solution.py:263
  24.9 7.8 %collective-permute-start.10 = (bf16[8,96,384]{2,1,0:T(8,128)(2,1)S(1)}, bf16[8,96,384]{2,1,0:T(8,128)(2,1)}, u32[]{:S(2)}, u32[]{:S(2)}) collective-permute-start(bf16[8,96,384]{2,1,0:T(8,128)(2,1)S(1)} %pad_maximum_fusion.refs_0_), channel_id=1, source_target_pairs={{0,1},{1,0},{2,3},{3,2},{4,5},{5,4},{6,7},{7,6},{8,9},{9,8},{10,11... | collective-permute-start | bytes 1769480 | tf_op jit(solution)/shard_map/ppermute | solution.py:278
  25.0 6.6 %collective-permute-start.7 = (bf16[4,48,384]{2,1,0:T(8,128)(2,1)}, bf16[4,48,384]{2,1,0:T(8,128)(2,1)S(1)}, u32[]{:S(2)}, u32[]{:S(2)}) collective-permute-start(bf16[4,48,384]{2,1,0:T(8,128)(2,1)} %get-tuple-element.22), channel_id=1, source_target_pairs={{0,12},{2,14},{4,0},{6,2},{8,4},{10,6},{12,8},{14,10},{1,13},{3,15... | collective-permute-start | bytes 442376 | tf_op jit(solution)/shard_map/ppermute | solution.py:263
  27.9 5.9 %collective-permute-start.8 = (bf16[4,256,384]{2,1,0:T(8,128)(2,1)S(1)}, bf16[4,256,384]{2,1,0:T(8,128)(2,1)S(1)}, u32[]{:S(2)}, u32[]{:S(2)}) collective-permute-start(bf16[4,256,384]{2,1,0:T(8,128)(2,1)S(1)} %copy-done), channel_id=1, source_target_pairs={{0,1},{1,0},{2,3},{3,2},{4,5},{5,4},{6,7},{7,6},{8,9},{9,8},{10,11... | collective-permute-start | bytes 2359304 | tf_op jit(solution)/shard_map/ppermute | solution.py:278
  31.6 2.2 %collective-permute-start.9 = (bf16[4,192,384]{2,1,0:T(8,128)(2,1)S(1)}, bf16[4,192,384]{2,1,0:T(8,128)(2,1)}, u32[]{:S(2)}, u32[]{:S(2)}) collective-permute-start(bf16[4,192,384]{2,1,0:T(8,128)(2,1)S(1)} %constant_dynamic-update-slice_fusion.last_ref), channel_id=1, source_target_pairs={{0,1},{1,0},{2,3},{3,2},{4,5},{5,4},{6,7},{7,6},{8,9},{9,8},{10,11... | collective-permute-start | bytes 1769480 | tf_op jit(solution)/shard_map/ppermute | solution.py:278
  32.0 2.2 %collective-permute-start.12 = (bf16[4,96,384]{2,1,0:T(8,128)(2,1)S(1)}, bf16[4,96,384]{2,1,0:T(8,128)(2,1)S(1)}, u32[]{:S(2)}, u32[]{:S(2)}) collective-permute-start(bf16[4,96,384]{2,1,0:T(8,128)(2,1)S(1)} %get-tuple-element.29), channel_id=1, source_target_pairs={{0,1},{1,0},{2,3},{3,2},{4,5},{5,4},{6,7},{7,6},{8,9},{9,8},{10,11... | collective-permute-start | bytes 884744 | tf_op jit(solution)/shard_map/ppermute | solution.py:278
  32.5 2.0 %collective-permute-start.13 = (bf16[4,96,384]{2,1,0:T(8,128)(2,1)S(1)}, bf16[4,96,384]{2,1,0:T(8,128)(2,1)S(1)}, u32[]{:S(2)}, u32[]{:S(2)}) collective-permute-start(bf16[4,96,384]{2,1,0:T(8,128)(2,1)S(1)} %get-tuple-element.28), channel_id=1, source_target_pairs={{0,1},{1,0},{2,3},{3,2},{4,5},{5,4},{6,7},{7,6},{8,9},{9,8},{10,11... | collective-permute-start | bytes 884744 | tf_op jit(solution)/shard_map/ppermute | solution.py:278
  37.8 8.4 %collective-permute-start.14 = (bf16[2,48,384]{2,1,0:T(8,128)(2,1)S(1)}, bf16[2,48,384]{2,1,0:T(8,128)(2,1)S(1)}, u32[]{:S(2)}, u32[]{:S(2)}) collective-permute-start(bf16[2,48,384]{2,1,0:T(8,128)(2,1)S(1)} %get-tuple-element.25), channel_id=1, source_target_pairs={{0,8},{2,10},{4,12},{6,14},{8,0},{10,2},{12,4},{14,6},{1,9},{3,11}... | collective-permute-start | bytes 221192 | tf_op jit(solution)/shard_map/ppermute | solution.py:263
  39.8 7.6 %collective-permute-start.15 = (bf16[2,48,384]{2,1,0:T(8,128)(2,1)S(1)}, bf16[2,48,384]{2,1,0:T(8,128)(2,1)S(1)}, u32[]{:S(2)}, u32[]{:S(2)}) collective-permute-start(bf16[2,48,384]{2,1,0:T(8,128)(2,1)S(1)} %get-tuple-element.26), channel_id=1, source_target_pairs={{0,4},{2,6},{4,8},{6,10},{8,12},{10,14},{12,0},{14,2},{1,5},{3,7},... | collective-permute-start | bytes 221192 | tf_op jit(solution)/shard_map/ppermute | solution.py:263
  42.6 5.1 %collective-permute-start.16 = (bf16[2,48,384]{2,1,0:T(8,128)(2,1)S(1)}, bf16[2,48,384]{2,1,0:T(8,128)(2,1)S(1)}, u32[]{:S(2)}, u32[]{:S(2)}) collective-permute-start(bf16[2,48,384]{2,1,0:T(8,128)(2,1)S(1)} %get-tuple-element.27), channel_id=1, source_target_pairs={{0,12},{2,14},{4,0},{6,2},{8,4},{10,6},{12,8},{14,10},{1,13},{3,15... | collective-permute-start | bytes 221192 | tf_op jit(solution)/shard_map/ppermute | solution.py:263

commit v6 on v5

--- a/solution.py
+++ b/solution.py
@@ -281,7 +281,8 @@
         return lax.dynamic_slice_in_dim(x, index * width, width, x.ndim - 1)
 
     shared = [columns_of(stale_cache, (layer + k) % rounds) for k in range(rounds)]
-    shared += [columns_of(fresh_first[1:], (layer + s) % layers) for s in range(layers)]
+    away_parts = [columns_of(fresh_first[1:], (layer + s) % layers) for s in range(1, layers)]
+    shared += [columns_of(after(fresh_first, *away_parts)[1:], layer), *away_parts]
     *owned, text = pack(
         functools.partial(pack_owned_kernel, layers=layers),
         [(4, rows, width)] * layers + [(4, text_rows, width)],

time: 48.7 us -> 48.4 us (level)
  starting transfers between devices: 29.2 us -> 27.6 us
  local copies, waits for them, and re-layouts: 3.02 us -> 3.98 us
    ppermute x9, starting transfers between devices: 25.2 us -> 23.8 us  [layer_swap(): return x if shift == 0 else lax.ppermute(x, 'patch', pairs)]
    slice x0 -> x2, local copies, waits for them, and re-layouts: none -> 0.96 us  [layered_shards(): after(fresh_first, *away_parts)[1:]]
    ppermute x9, waiting for transfers between devices: 4.09 us -> 4.66 us  [layer_swap(): return x if shift == 0 else lax.ppermute(x, 'patch', pairs)]
    ppermute x2, waiting for transfers between devices: 0.57 us -> 0.01 us  [stale_round(): return lax.ppermute(x, ('patch', 'uly'), pairs)]
  transfers between devices with their start and end apart: 17 -> 17, of which waited for: 8 -> 7; matrix products, arithmetic and copies ran while one was open for 3% -> 4% of each run, Pallas kernels for 11% -> 11%
where the time goes in v6:
time: 48.4 us; the launch traced here: 47.9 us
  starting transfers between devices  27.6 us (57%)
  Pallas kernels  8.49 us (18%)
  waiting for transfers between devices  6.41 us (13%)
  local copies, waits for them, and re-layouts  3.98 us (8%)
  between operations  1.07 us (2%)
    ppermute x9, starting transfers between devices, layer_swap(): return x if shift == 0 else lax.ppermute(x, 'patch', pairs)  23.8 us
    pallas_call x2, Pallas kernels, call_both(): pl.pallas_call(functools.partial(both_kernel, parts=parts, blocks=blocks,...  5.85 us
    ppermute x9, waiting for transfers between devices, layer_swap(): return x if shift == 0 else lax.ppermute(x, 'patch', pairs)  4.66 us
    pallas_call x1, Pallas kernels, pack(): pl.pallas_call(kernel, out_shape=[jax.ShapeDtypeStruct(shape, BF16) for s...  2.63 us
    ppermute x5, waiting for transfers between devices, other_core(): return lax.ppermute(x, 'uly', [(0, 1), (1, 0)])  1.74 us
    ppermute x1, starting transfers between devices, other_column(): lax.ppermute(x, 'patch', [(p, p ^ 1) for p in range(layers * COLUMNS)])  1.58 us
    ppermute x2, starting transfers between devices, stale_round(): return lax.ppermute(x, ('patch', 'uly'), pairs)  1.41 us
    unnamed x11, local copies, waits for them, and re-layouts  1 us
  transfers between devices with their start and end apart: 17, of which 7 were waited for; matrix products, arithmetic and copies ran while one was open for 4% of the time, Pallas kernels for 11%

profile of v6, /device:TPU:0, one launch (start us, length us, event | category | flops | bytes accessed | tf_op | source)
XLA Modules:
  0.0 47.9 jit_solution(17330886664889476944)
XLA Ops:
  0.7 0.9 %slice-done = bf16[2,48,1536]{2,1,0:T(8,128)(2,1)S(1)} async-done(((bf16[3,48,1536]{2,1,0:T(8,128)(2,1)}), bf16[2,48,1536]{2,1,0:T(8,128)(2,1)S(1)}, s32[]{:S(2)}) %slice-start) | async-done | bytes 294936 | tf_op jit(solution)/shard_map/slice | solution.py:284
  1.7 3.1 %collective-permute-start.3 = (bf16[2,48,384]{2,1,0:T(8,128)(2,1)S(1)}, bf16[2,48,384]{2,1,0:T(8,128)(2,1)S(1)}, u32[]{:S(2)}, u32[]{:S(2)}) collective-permute-start(bf16[2,48,384]{2,1,0:T(8,128)(2,1)S(1)} %get-tuple-element.36), channel_id=1, source_target_pairs={{0,4},{2,6},{4,8},{6,10},{8,12},{10,14},{12,0},{14,2},{1,5},{3,7},... | collective-permute-start | bytes 221192 | tf_op jit(solution)/shard_map/ppermute | solution.py:263
  4.8 2.6 %collective-permute-start.4 = (bf16[2,48,384]{2,1,0:T(8,128)(2,1)S(1)}, bf16[2,48,384]{2,1,0:T(8,128)(2,1)S(1)}, u32[]{:S(2)}, u32[]{:S(2)}) collective-permute-start(bf16[2,48,384]{2,1,0:T(8,128)(2,1)S(1)} %get-tuple-element.35), channel_id=1, source_target_pairs={{0,8},{2,10},{4,12},{6,14},{8,0},{10,2},{12,4},{14,6},{1,9},{3,11}... | collective-permute-start | bytes 221192 | tf_op jit(solution)/shard_map/ppermute | solution.py:263
  7.4 1.3 %collective-permute-start.5 = (bf16[2,48,384]{2,1,0:T(8,128)(2,1)S(1)}, bf16[2,48,384]{2,1,0:T(8,128)(2,1)S(1)}, u32[]{:S(2)}, u32[]{:S(2)}) collective-permute-start(bf16[2,48,384]{2,1,0:T(8,128)(2,1)S(1)} %get-tuple-element.34), channel_id=1, source_target_pairs={{0,12},{2,14},{4,0},{6,2},{8,4},{10,6},{12,8},{14,10},{1,13},{3,15... | collective-permute-start | bytes 221192 | tf_op jit(solution)/shard_map/ppermute | solution.py:263
  8.8 0.7 %collective-permute-start.1 = (bf16[2,96,384]{2,1,0:T(8,128)(2,1)S(1)}, bf16[2,96,384]{2,1,0:T(8,128)(2,1)S(1)}, u32[]{:S(2)}, u32[]{:S(2)}) collective-permute-start(bf16[2,96,384]{2,1,0:T(8,128)(2,1)S(1)} %get-tuple-element.38), channel_id=1, source_target_pairs={{0,0},{1,8},{2,2},{3,10},{4,4},{5,12},{6,6},{7,14},{8,1},{9,9},{10... | collective-permute-start | bytes 442376 | tf_op jit(solution)/shard_map/ppermute | solution.py:272
  9.4 0.7 %collective-permute-start.2 = (bf16[2,96,384]{2,1,0:T(8,128)(2,1)S(1)}, bf16[2,96,384]{2,1,0:T(8,128)(2,1)S(1)}, u32[]{:S(2)}, u32[]{:S(2)}) collective-permute-start(bf16[2,96,384]{2,1,0:T(8,128)(2,1)S(1)} %get-tuple-element.37), channel_id=1, source_target_pairs={{0,4},{1,12},{2,6},{3,14},{4,0},{5,8},{6,2},{7,10},{8,5},{9,13},{1... | collective-permute-start | bytes 442376 | tf_op jit(solution)/shard_map/ppermute | solution.py:272
  10.2 1.0 %slice-done.1 = bf16[2,48,1536]{2,1,0:T(8,128)(2,1)S(1)} async-done(((bf16[3,48,1536]{2,1,0:T(8,128)(2,1)}), bf16[2,48,1536]{2,1,0:T(8,128)(2,1)S(1)}, s32[]{:S(2)}) %slice-start.1) | async-done | bytes 294936 | tf_op jit(solution)/shard_map/slice | solution.py:285
  11.1 2.6 %shard_map.77 = (bf16[4,48,384]{2,1,0:T(8,128)(2,1)}, bf16[4,48,384]{2,1,0:T(8,128)(2,1)}, bf16[4,48,384]{2,1,0:T(8,128)(2,1)}, bf16[4,48,384]{2,1,0:T(8,128)(2,1)}, bf16[4,256,384]{2,1,0:T(8,128)(2,1)}) custom-call(bf16[3,48,1536]{2,1,0:T(8,128)(2,1)} %first_ref, bf16[3,48,1536]{2,1,0:T(8,128)(2,1)} %second_ref.1, bf16[2,256,768]{2,1,0:T(8,128)(2,1)} %text_first_ref.1, ...), custom_call_target="tpu_custom_call" | custom-call | bytes 1048576 | tf_op jit(solution)/shard_map/pallas_call | solution.py:143
  13.8 1.4 %collective-permute-start = (bf16[4,48,384]{2,1,0:T(8,128)(2,1)}, bf16[4,48,384]{2,1,0:T(8,128)(2,1)S(1)}, u32[]{:S(2)}, u32[]{:S(2)}) collective-permute-start(bf16[4,48,384]{2,1,0:T(8,128)(2,1)} %get-tuple-element.19), channel_id=1, source_target_pairs={{0,4},{2,6},{4,8},{6,10},{8,12},{10,14},{12,0},{14,2},{1,5},{3,7},... | collective-permute-start | bytes 442376 | tf_op jit(solution)/shard_map/ppermute | solution.py:263
  15.3 0.1 pad_maximum_fusion.refs_0_
  15.4 1.6 %collective-permute-start.11 = (bf16[8,96,384]{2,1,0:T(8,128)(2,1)S(1)}, bf16[8,96,384]{2,1,0:T(8,128)(2,1)S(1)}, u32[]{:S(2)}, u32[]{:S(2)}) collective-permute-start(bf16[8,96,384]{2,1,0:T(8,128)(2,1)S(1)} %pad_maximum_fusion.refs_0_), channel_id=1, source_target_pairs={{0,2},{2,0},{4,6},{6,4},{8,10},{10,8},{12,14},{14,12},{1,3},{3,1},... | collective-permute-start | bytes 1769480 | tf_op jit(solution)/shard_map/ppermute | solution.py:275
  17.0 6.6 %collective-permute-start.6 = (bf16[4,48,384]{2,1,0:T(8,128)(2,1)}, bf16[4,48,384]{2,1,0:T(8,128)(2,1)}, u32[]{:S(2)}, u32[]{:S(2)}) collective-permute-start(bf16[4,48,384]{2,1,0:T(8,128)(2,1)} %get-tuple-element.23), channel_id=1, source_target_pairs={{0,8},{2,10},{4,12},{6,14},{8,0},{10,2},{12,4},{14,6},{1,9},{3,11}... | collective-permute-start | bytes 442376 | tf_op jit(solution)/shard_map/ppermute | solution.py:263
  23.9 3.4 %collective-permute-start.7 = (bf16[4,48,384]{2,1,0:T(8,128)(2,1)}, bf16[4,48,384]{2,1,0:T(8,128)(2,1)S(1)}, u32[]{:S(2)}, u32[]{:S(2)}) collective-permute-start(bf16[4,48,384]{2,1,0:T(8,128)(2,1)} %get-tuple-element.24), channel_id=1, source_target_pairs={{0,12},{2,14},{4,0},{6,2},{8,4},{10,6},{12,8},{14,10},{1,13},{3,15... | collective-permute-start | bytes 442376 | tf_op jit(solution)/shard_map/ppermute | solution.py:263
  27.4 2.4 %collective-permute-done.6 = bf16[4,48,384]{2,1,0:T(8,128)(2,1)} collective-permute-done((bf16[4,48,384]{2,1,0:T(8,128)(2,1)}, bf16[4,48,384]{2,1,0:T(8,128)(2,1)}, u32[]{:S(2)}, u32[]{:S(2)}) %collective-permute-start.6) | collective-permute-done | bytes 147488 | tf_op jit(solution)/shard_map/ppermute | solution.py:263
  29.8 0.9 %constant_dynamic-update-slice_fusion.1 = bf16[4,192,384]{2,1,0:T(8,128)(2,1)S(1)} fusion(bf16[4,192,384]{2,1,0:T(8,128)(2,1)S(1)} %constant_dynamic-update-slice_fusion.2, bf16[4,48,384]{2,1,0:T(8,128)(2,1)} %collective-permute-done.6), kind=kLoop, calls=%fused_computation.5 | loop fusion | bytes 294912
  30.7 0.8 %collective-permute-done.7 = bf16[4,48,384]{2,1,0:T(8,128)(2,1)S(1)} collective-permute-done((bf16[4,48,384]{2,1,0:T(8,128)(2,1)}, bf16[4,48,384]{2,1,0:T(8,128)(2,1)S(1)}, u32[]{:S(2)}, u32[]{:S(2)}) %collective-permute-start.7) | collective-permute-done | bytes 147488 | tf_op jit(solution)/shard_map/ppermute | solution.py:263
  31.5 0.1 collective-permute-start.9
  31.6 0.1 fusion.3
  31.9 0.5 %collective-permute-start.12 = (bf16[4,96,384]{2,1,0:T(8,128)(2,1)S(1)}, bf16[4,96,384]{2,1,0:T(8,128)(2,1)S(1)}, u32[]{:S(2)}, u32[]{:S(2)}) collective-permute-start(bf16[4,96,384]{2,1,0:T(8,128)(2,1)S(1)} %get-tuple-element.31), channel_id=1, source_target_pairs={{0,1},{1,0},{2,3},{3,2},{4,5},{5,4},{6,7},{7,6},{8,9},{9,8},{10,11... | collective-permute-start | bytes 884744 | tf_op jit(solution)/shard_map/ppermute | solution.py:278
  32.4 0.1 collective-permute-start.13
  32.5 0.1 add_bitcast_fusion
  32.7 1.0 %collective-permute-done.9.last_twin_ref = bf16[4,192,384]{2,1,0:T(8,128)(2,1)} collective-permute-done((bf16[4,192,384]{2,1,0:T(8,128)(2,1)S(1)}, bf16[4,192,384]{2,1,0:T(8,128)(2,1)}, u32[]{:S(2)}, u32[]{:S(2)}) %collective-permute-start.9) | collective-permute-done | bytes 589856 | tf_op jit(solution)/shard_map/ppermute | solution.py:278
  33.7 0.3 collective-permute-done.12.refs_3_
  34.0 0.4 collective-permute-done.13.refs_4_
  34.4 3.3 %shard_map.79 = (bf16[2,48,384]{2,1,0:T(8,128)(2,1)S(1)}, bf16[2,48,384]{2,1,0:T(8,128)(2,1)S(1)}, bf16[2,48,384]{2,1,0:T(8,128)(2,1)S(1)}) custom-call(f32[2,3]{1,0:T(2,128)S(1)} %fusion.2.scale_ref, s32[3,4]{1,0:T(4,128)S(1)} %add_add_fusion.order_ref, bf16[2,192,384]{2,1,0:T(8,128)(2,1)S(1)} %slice.30.queries_ref, bf16[4,256,384]{2,1,0:T(8,128)(2,1)S(1)} %copy-done, ...), custom_call_target="tpu_custom_call" | custom-call | flops 452984832 | bytes 3440640 | tf_op jit(solution)/shard_map/pallas_call | solution.py:233
  37.7 1.5 %collective-permute-start.14 = (bf16[2,48,384]{2,1,0:T(8,128)(2,1)S(1)}, bf16[2,48,384]{2,1,0:T(8,128)(2,1)S(1)}, u32[]{:S(2)}, u32[]{:S(2)}) collective-permute-start(bf16[2,48,384]{2,1,0:T(8,128)(2,1)S(1)} %get-tuple-element.27), channel_id=1, source_target_pairs={{0,8},{2,10},{4,12},{6,14},{8,0},{10,2},{12,4},{14,6},{1,9},{3,11}... | collective-permute-start | bytes 221192 | tf_op jit(solution)/shard_map/ppermute | solution.py:263
  39.2 2.8 %collective-permute-start.15 = (bf16[2,48,384]{2,1,0:T(8,128)(2,1)S(1)}, bf16[2,48,384]{2,1,0:T(8,128)(2,1)S(1)}, u32[]{:S(2)}, u32[]{:S(2)}) collective-permute-start(bf16[2,48,384]{2,1,0:T(8,128)(2,1)S(1)} %get-tuple-element.28), channel_id=1, source_target_pairs={{0,4},{2,6},{4,8},{6,10},{8,12},{10,14},{12,0},{14,2},{1,5},{3,7},... | collective-permute-start | bytes 221192 | tf_op jit(solution)/shard_map/ppermute | solution.py:263
  42.0 1.0 %collective-permute-start.16 = (bf16[2,48,384]{2,1,0:T(8,128)(2,1)S(1)}, bf16[2,48,384]{2,1,0:T(8,128)(2,1)S(1)}, u32[]{:S(2)}, u32[]{:S(2)}) collective-permute-start(bf16[2,48,384]{2,1,0:T(8,128)(2,1)S(1)} %get-tuple-element.29), channel_id=1, source_target_pairs={{0,12},{2,14},{4,0},{6,2},{8,4},{10,6},{12,8},{14,10},{1,13},{3,15... | collective-permute-start | bytes 221192 | tf_op jit(solution)/shard_map/ppermute | solution.py:263
  43.0 2.6 %shard_map.78 = bf16[2,48,384]{2,1,0:T(8,128)(2,1)S(1)} custom-call(f32[2,3]{1,0:T(2,128)S(1)} %fusion.2.scale_ref, s32[3,4]{1,0:T(4,128)S(1)} %add_add_fusion.order_ref, bf16[2,192,384]{2,1,0:T(8,128)(2,1)S(1)} %slice.30.queries_ref, bf16[4,256,384]{2,1,0:T(8,128)(2,1)S(1)} %copy-done, bf16[4,256,384]{2,1,0:T(8,128)(2,1)S(1)} %collective-permute-done.8.text_twin_ref, ...), custom_call_target="tpu_custom_call" | custom-call | flops 150994944 | bytes 3440640 | tf_op jit(solution)/shard_map/pallas_call | solution.py:233
  45.7 1.3 %collective-permute-done.15 = bf16[2,48,384]{2,1,0:T(8,128)(2,1)S(1)} collective-permute-done((bf16[2,48,384]{2,1,0:T(8,128)(2,1)S(1)}, bf16[2,48,384]{2,1,0:T(8,128)(2,1)S(1)}, u32[]{:S(2)}, u32[]{:S(2)}) %collective-permute-start.15) | collective-permute-done | bytes 73760 | tf_op jit(solution)/shard_map/ppermute | solution.py:263
  47.0 0.2 collective-permute-done.16
  47.2 0.7 %slice_bitcast_fusion = (bf16[48,1536]{1,0:T(8,128)(2,1)}, bf16[48,1536]{1,0:T(8,128)(2,1)}) fusion(bf16[2,48,1536]{2,1,0:T(8,128)(2,1)S(1)} %constant_dynamic-update-slice_fusion.4), kind=kLoop, calls=%fused_computation.2 | loop fusion | bytes 589824 | tf_op jit(solution)/shard_map/squeeze | solution.py:327
  (39 shorter events, 0.7 us)
Async XLA Ops:
  0.7 1.0 %slice-start = ((bf16[3,48,1536]{2,1,0:T(8,128)(2,1)}), bf16[2,48,1536]{2,1,0:T(8,128)(2,1)S(1)}, s32[]{:S(2)}) async-start(bf16[3,48,1536]{2,1,0:T(8,128)(2,1)} %first_ref), calls=%async_computation | async-start | bytes 589824 | tf_op jit(solution)/shard_map/slice | solution.py:284
  0.7 8.0 %copy-start.1 = (bf16[2,96,768]{2,1,0:T(8,128)(2,1)S(1)}, bf16[2,96,768]{2,1,0:T(8,128)(2,1)}, u32[]{:S(2)}) copy-start(bf16[2,96,768]{2,1,0:T(8,128)(2,1)} %param.8) | copy-start | bytes 884740
  1.7 12.1 %collective-permute-start.3 = (bf16[2,48,384]{2,1,0:T(8,128)(2,1)S(1)}, bf16[2,48,384]{2,1,0:T(8,128)(2,1)S(1)}, u32[]{:S(2)}, u32[]{:S(2)}) collective-permute-start(bf16[2,48,384]{2,1,0:T(8,128)(2,1)S(1)} %get-tuple-element.36), channel_id=1, source_target_pairs={{0,4},{2,6},{4,8},{6,10},{8,12},{10,14},{12,0},{14,2},{1,5},{3,7},... | collective-permute-start | bytes 221192 | tf_op jit(solution)/shard_map/ppermute | solution.py:263
  4.8 10.4 %collective-permute-start.4 = (bf16[2,48,384]{2,1,0:T(8,128)(2,1)S(1)}, bf16[2,48,384]{2,1,0:T(8,128)(2,1)S(1)}, u32[]{:S(2)}, u32[]{:S(2)}) collective-permute-start(bf16[2,48,384]{2,1,0:T(8,128)(2,1)S(1)} %get-tuple-element.35), channel_id=1, source_target_pairs={{0,8},{2,10},{4,12},{6,14},{8,0},{10,2},{12,4},{14,6},{1,9},{3,11}... | collective-permute-start | bytes 221192 | tf_op jit(solution)/shard_map/ppermute | solution.py:263
  7.4 7.8 %collective-permute-start.5 = (bf16[2,48,384]{2,1,0:T(8,128)(2,1)S(1)}, bf16[2,48,384]{2,1,0:T(8,128)(2,1)S(1)}, u32[]{:S(2)}, u32[]{:S(2)}) collective-permute-start(bf16[2,48,384]{2,1,0:T(8,128)(2,1)S(1)} %get-tuple-element.34), channel_id=1, source_target_pairs={{0,12},{2,14},{4,0},{6,2},{8,4},{10,6},{12,8},{14,10},{1,13},{3,15... | collective-permute-start | bytes 221192 | tf_op jit(solution)/shard_map/ppermute | solution.py:263
  8.8 6.5 %collective-permute-start.1 = (bf16[2,96,384]{2,1,0:T(8,128)(2,1)S(1)}, bf16[2,96,384]{2,1,0:T(8,128)(2,1)S(1)}, u32[]{:S(2)}, u32[]{:S(2)}) collective-permute-start(bf16[2,96,384]{2,1,0:T(8,128)(2,1)S(1)} %get-tuple-element.38), channel_id=1, source_target_pairs={{0,0},{1,8},{2,2},{3,10},{4,4},{5,12},{6,6},{7,14},{8,1},{9,9},{10... | collective-permute-start | bytes 442376 | tf_op jit(solution)/shard_map/ppermute | solution.py:272
  9.4 5.8 %collective-permute-start.2 = (bf16[2,96,384]{2,1,0:T(8,128)(2,1)S(1)}, bf16[2,96,384]{2,1,0:T(8,128)(2,1)S(1)}, u32[]{:S(2)}, u32[]{:S(2)}) collective-permute-start(bf16[2,96,384]{2,1,0:T(8,128)(2,1)S(1)} %get-tuple-element.37), channel_id=1, source_target_pairs={{0,4},{1,12},{2,6},{3,14},{4,0},{5,8},{6,2},{7,10},{8,5},{9,13},{1... | collective-permute-start | bytes 442376 | tf_op jit(solution)/shard_map/ppermute | solution.py:272
  10.2 1.0 %slice-start.1 = ((bf16[3,48,1536]{2,1,0:T(8,128)(2,1)}), bf16[2,48,1536]{2,1,0:T(8,128)(2,1)S(1)}, s32[]{:S(2)}) async-start(bf16[3,48,1536]{2,1,0:T(8,128)(2,1)} %first_ref), calls=%async_computation.1 | async-start | bytes 589824 | tf_op jit(solution)/shard_map/slice | solution.py:285
  13.8 13.5 %collective-permute-start = (bf16[4,48,384]{2,1,0:T(8,128)(2,1)}, bf16[4,48,384]{2,1,0:T(8,128)(2,1)S(1)}, u32[]{:S(2)}, u32[]{:S(2)}) collective-permute-start(bf16[4,48,384]{2,1,0:T(8,128)(2,1)} %get-tuple-element.19), channel_id=1, source_target_pairs={{0,4},{2,6},{4,8},{6,10},{8,12},{10,14},{12,0},{14,2},{1,5},{3,7},... | collective-permute-start | bytes 442376 | tf_op jit(solution)/shard_map/ppermute | solution.py:263
  15.3 1.7 %copy-start.2 = (bf16[4,48,384]{2,1,0:T(8,128)(2,1)S(1)}, bf16[4,48,384]{2,1,0:T(8,128)(2,1)}, u32[]{:S(2)}) copy-start(bf16[4,48,384]{2,1,0:T(8,128)(2,1)} %get-tuple-element.18) | copy-start | bytes 442372
  15.3 12.0 %copy-start = (bf16[4,256,384]{2,1,0:T(8,128)(2,1)S(1)}, bf16[4,256,384]{2,1,0:T(8,128)(2,1)}, u32[]{:S(2)}) copy-start(bf16[4,256,384]{2,1,0:T(8,128)(2,1)} %get-tuple-element.26.text_ref) | copy-start | bytes 2359300
  15.4 16.4 %collective-permute-start.11 = (bf16[8,96,384]{2,1,0:T(8,128)(2,1)S(1)}, bf16[8,96,384]{2,1,0:T(8,128)(2,1)S(1)}, u32[]{:S(2)}, u32[]{:S(2)}) collective-permute-start(bf16[8,96,384]{2,1,0:T(8,128)(2,1)S(1)} %pad_maximum_fusion.refs_0_), channel_id=1, source_target_pairs={{0,2},{2,0},{4,6},{6,4},{8,10},{10,8},{12,14},{14,12},{1,3},{3,1},... | collective-permute-start | bytes 1769480 | tf_op jit(solution)/shard_map/ppermute | solution.py:275
  17.0 6.6 %copy-start.3 = (s32[2,12]{1,0:T(2,128)S(1)}, s32[2,12]{1,0:T(2,128)}, u32[]{:S(2)}) copy-start(s32[2,12]{1,0:T(2,128)} %param.9) | copy-start | bytes 292
  17.0 12.8 %collective-permute-start.6 = (bf16[4,48,384]{2,1,0:T(8,128)(2,1)}, bf16[4,48,384]{2,1,0:T(8,128)(2,1)}, u32[]{:S(2)}, u32[]{:S(2)}) collective-permute-start(bf16[4,48,384]{2,1,0:T(8,128)(2,1)} %get-tuple-element.23), channel_id=1, source_target_pairs={{0,8},{2,10},{4,12},{6,14},{8,0},{10,2},{12,4},{14,6},{1,9},{3,11}... | collective-permute-start | bytes 442376 | tf_op jit(solution)/shard_map/ppermute | solution.py:263
  23.8 8.8 %collective-permute-start.10 = (bf16[8,96,384]{2,1,0:T(8,128)(2,1)S(1)}, bf16[8,96,384]{2,1,0:T(8,128)(2,1)}, u32[]{:S(2)}, u32[]{:S(2)}) collective-permute-start(bf16[8,96,384]{2,1,0:T(8,128)(2,1)S(1)} %pad_maximum_fusion.refs_0_), channel_id=1, source_target_pairs={{0,1},{1,0},{2,3},{3,2},{4,5},{5,4},{6,7},{7,6},{8,9},{9,8},{10,11... | collective-permute-start | bytes 1769480 | tf_op jit(solution)/shard_map/ppermute | solution.py:278
  23.9 7.6 %collective-permute-start.7 = (bf16[4,48,384]{2,1,0:T(8,128)(2,1)}, bf16[4,48,384]{2,1,0:T(8,128)(2,1)S(1)}, u32[]{:S(2)}, u32[]{:S(2)}) collective-permute-start(bf16[4,48,384]{2,1,0:T(8,128)(2,1)} %get-tuple-element.24), channel_id=1, source_target_pairs={{0,12},{2,14},{4,0},{6,2},{8,4},{10,6},{12,8},{14,10},{1,13},{3,15... | collective-permute-start | bytes 442376 | tf_op jit(solution)/shard_map/ppermute | solution.py:263
  27.3 6.4 %collective-permute-start.8 = (bf16[4,256,384]{2,1,0:T(8,128)(2,1)S(1)}, bf16[4,256,384]{2,1,0:T(8,128)(2,1)S(1)}, u32[]{:S(2)}, u32[]{:S(2)}) collective-permute-start(bf16[4,256,384]{2,1,0:T(8,128)(2,1)S(1)} %copy-done), channel_id=1, source_target_pairs={{0,1},{1,0},{2,3},{3,2},{4,5},{5,4},{6,7},{7,6},{8,9},{9,8},{10,11... | collective-permute-start | bytes 2359304 | tf_op jit(solution)/shard_map/ppermute | solution.py:278
  31.5 2.2 %collective-permute-start.9 = (bf16[4,192,384]{2,1,0:T(8,128)(2,1)S(1)}, bf16[4,192,384]{2,1,0:T(8,128)(2,1)}, u32[]{:S(2)}, u32[]{:S(2)}) collective-permute-start(bf16[4,192,384]{2,1,0:T(8,128)(2,1)S(1)} %constant_dynamic-update-slice_fusion.last_ref), channel_id=1, source_target_pairs={{0,1},{1,0},{2,3},{3,2},{4,5},{5,4},{6,7},{7,6},{8,9},{9,8},{10,11... | collective-permute-start | bytes 1769480 | tf_op jit(solution)/shard_map/ppermute | solution.py:278
  31.9 2.1 %collective-permute-start.12 = (bf16[4,96,384]{2,1,0:T(8,128)(2,1)S(1)}, bf16[4,96,384]{2,1,0:T(8,128)(2,1)S(1)}, u32[]{:S(2)}, u32[]{:S(2)}) collective-permute-start(bf16[4,96,384]{2,1,0:T(8,128)(2,1)S(1)} %get-tuple-element.31), channel_id=1, source_target_pairs={{0,1},{1,0},{2,3},{3,2},{4,5},{5,4},{6,7},{7,6},{8,9},{9,8},{10,11... | collective-permute-start | bytes 884744 | tf_op jit(solution)/shard_map/ppermute | solution.py:278
  32.4 2.0 %collective-permute-start.13 = (bf16[4,96,384]{2,1,0:T(8,128)(2,1)S(1)}, bf16[4,96,384]{2,1,0:T(8,128)(2,1)S(1)}, u32[]{:S(2)}, u32[]{:S(2)}) collective-permute-start(bf16[4,96,384]{2,1,0:T(8,128)(2,1)S(1)} %get-tuple-element.30), channel_id=1, source_target_pairs={{0,1},{1,0},{2,3},{3,2},{4,5},{5,4},{6,7},{7,6},{8,9},{9,8},{10,11... | collective-permute-start | bytes 884744 | tf_op jit(solution)/shard_map/ppermute | solution.py:278
  37.7 7.9 %collective-permute-start.14 = (bf16[2,48,384]{2,1,0:T(8,128)(2,1)S(1)}, bf16[2,48,384]{2,1,0:T(8,128)(2,1)S(1)}, u32[]{:S(2)}, u32[]{:S(2)}) collective-permute-start(bf16[2,48,384]{2,1,0:T(8,128)(2,1)S(1)} %get-tuple-element.27), channel_id=1, source_target_pairs={{0,8},{2,10},{4,12},{6,14},{8,0},{10,2},{12,4},{14,6},{1,9},{3,11}... | collective-permute-start | bytes 221192 | tf_op jit(solution)/shard_map/ppermute | solution.py:263
  39.2 7.8 %collective-permute-start.15 = (bf16[2,48,384]{2,1,0:T(8,128)(2,1)S(1)}, bf16[2,48,384]{2,1,0:T(8,128)(2,1)S(1)}, u32[]{:S(2)}, u32[]{:S(2)}) collective-permute-start(bf16[2,48,384]{2,1,0:T(8,128)(2,1)S(1)} %get-tuple-element.28), channel_id=1, source_target_pairs={{0,4},{2,6},{4,8},{6,10},{8,12},{10,14},{12,0},{14,2},{1,5},{3,7},... | collective-permute-start | bytes 221192 | tf_op jit(solution)/shard_map/ppermute | solution.py:263
  42.0 5.2 %collective-permute-start.16 = (bf16[2,48,384]{2,1,0:T(8,128)(2,1)S(1)}, bf16[2,48,384]{2,1,0:T(8,128)(2,1)S(1)}, u32[]{:S(2)}, u32[]{:S(2)}) collective-permute-start(bf16[2,48,384]{2,1,0:T(8,128)(2,1)S(1)} %get-tuple-element.29), channel_id=1, source_target_pairs={{0,12},{2,14},{4,0},{6,2},{8,4},{10,6},{12,8},{14,10},{1,13},{3,15... | collective-permute-start | bytes 221192 | tf_op jit(solution)/shard_map/ppermute | solution.py:263

commit v7 on v6

--- a/solution.py
+++ b/solution.py
@@ -235,7 +235,7 @@
         out_shape=[jax.ShapeDtypeStruct((2, rows, width), BF16)] * len(blocks),
         in_specs=[pl.BlockSpec(memory_space=pltpu.SMEM)] * len(scalars) + [in_vmem] * len(operands),
         out_specs=[in_vmem] * len(blocks),
-        compiler_params=pltpu.CompilerParams(vmem_limit_bytes=32 * 1024 * 1024),
+        compiler_params=pltpu.CompilerParams(vmem_limit_bytes=12 * 1024 * 1024),
         cost_estimate=pl.CostEstimate(
             flops=4 * rows * len(blocks) * keys * width,
             bytes_accessed=4 * width * (keys + count),
@@ -304,7 +304,7 @@
     owned = [owned[s] for s in range(layers)]
     away_twin = [other_core(away[0][:layers]), other_core(away[0][layers:])]
     last = jnp.concatenate(owned, 1)
-    near_twin = [other_core(near)]
+    near_twin = [other_core(after(near, owned[1]))]
     last_twin = other_core(last)
     text_twin = other_core(after(text, owned[1]))
     sets = [[near], near_twin, away, away_twin]

time: 48.4 us -> 48.4 us (level)
  no operation moved by 1% of the time
where the time goes in v7:
time: 48.4 us; the launch traced here: 47.9 us
  starting transfers between devices  27.6 us (57%)
  Pallas kernels  8.5 us (18%)
  waiting for transfers between devices  6.35 us (13%)
  local copies, waits for them, and re-layouts  3.98 us (8%)
  between operations  1.07 us (2%)
    ppermute x9, starting transfers between devices, layer_swap(): return x if shift == 0 else lax.ppermute(x, 'patch', pairs)  23.8 us
    pallas_call x2, Pallas kernels, call_both(): pl.pallas_call(functools.partial(both_kernel, parts=parts, blocks=blocks,...  5.87 us
    ppermute x9, waiting for transfers between devices, layer_swap(): return x if shift == 0 else lax.ppermute(x, 'patch', pairs)  4.6 us
    pallas_call x1, Pallas kernels, pack(): pl.pallas_call(kernel, out_shape=[jax.ShapeDtypeStruct(shape, BF16) for s...  2.63 us
    ppermute x5, waiting for transfers between devices, other_core(): return lax.ppermute(x, 'uly', [(0, 1), (1, 0)])  1.74 us
    ppermute x1, starting transfers between devices, other_column(): lax.ppermute(x, 'patch', [(p, p ^ 1) for p in range(layers * COLUMNS)])  1.58 us
    ppermute x2, starting transfers between devices, stale_round(): return lax.ppermute(x, ('patch', 'uly'), pairs)  1.41 us
    unnamed x11, local copies, waits for them, and re-layouts  0.99 us
  transfers between devices with their start and end apart: 17, of which 7 were waited for; matrix products, arithmetic and copies ran while one was open for 4% of the time, Pallas kernels for 11%

profile of v7, /device:TPU:0, one launch (start us, length us, event | category | flops | bytes accessed | tf_op | source)
XLA Modules:
  0.0 47.9 jit_solution(16327404245058681009)
XLA Ops:
  0.7 0.9 %slice-done = bf16[2,48,1536]{2,1,0:T(8,128)(2,1)S(1)} async-done(((bf16[3,48,1536]{2,1,0:T(8,128)(2,1)}), bf16[2,48,1536]{2,1,0:T(8,128)(2,1)S(1)}, s32[]{:S(2)}) %slice-start) | async-done | bytes 294936 | tf_op jit(solution)/shard_map/slice | solution.py:284
  1.7 3.1 %collective-permute-start.3 = (bf16[2,48,384]{2,1,0:T(8,128)(2,1)S(1)}, bf16[2,48,384]{2,1,0:T(8,128)(2,1)S(1)}, u32[]{:S(2)}, u32[]{:S(2)}) collective-permute-start(bf16[2,48,384]{2,1,0:T(8,128)(2,1)S(1)} %get-tuple-element.38), channel_id=1, source_target_pairs={{0,4},{2,6},{4,8},{6,10},{8,12},{10,14},{12,0},{14,2},{1,5},{3,7},... | collective-permute-start | bytes 221192 | tf_op jit(solution)/shard_map/ppermute | solution.py:263
  4.8 2.6 %collective-permute-start.4 = (bf16[2,48,384]{2,1,0:T(8,128)(2,1)S(1)}, bf16[2,48,384]{2,1,0:T(8,128)(2,1)S(1)}, u32[]{:S(2)}, u32[]{:S(2)}) collective-permute-start(bf16[2,48,384]{2,1,0:T(8,128)(2,1)S(1)} %get-tuple-element.37), channel_id=1, source_target_pairs={{0,8},{2,10},{4,12},{6,14},{8,0},{10,2},{12,4},{14,6},{1,9},{3,11}... | collective-permute-start | bytes 221192 | tf_op jit(solution)/shard_map/ppermute | solution.py:263
  7.4 1.3 %collective-permute-start.5 = (bf16[2,48,384]{2,1,0:T(8,128)(2,1)S(1)}, bf16[2,48,384]{2,1,0:T(8,128)(2,1)S(1)}, u32[]{:S(2)}, u32[]{:S(2)}) collective-permute-start(bf16[2,48,384]{2,1,0:T(8,128)(2,1)S(1)} %get-tuple-element.36), channel_id=1, source_target_pairs={{0,12},{2,14},{4,0},{6,2},{8,4},{10,6},{12,8},{14,10},{1,13},{3,15... | collective-permute-start | bytes 221192 | tf_op jit(solution)/shard_map/ppermute | solution.py:263
  8.8 0.7 %collective-permute-start.1 = (bf16[2,96,384]{2,1,0:T(8,128)(2,1)S(1)}, bf16[2,96,384]{2,1,0:T(8,128)(2,1)S(1)}, u32[]{:S(2)}, u32[]{:S(2)}) collective-permute-start(bf16[2,96,384]{2,1,0:T(8,128)(2,1)S(1)} %get-tuple-element.40), channel_id=1, source_target_pairs={{0,0},{1,8},{2,2},{3,10},{4,4},{5,12},{6,6},{7,14},{8,1},{9,9},{10... | collective-permute-start | bytes 442376 | tf_op jit(solution)/shard_map/ppermute | solution.py:272
  9.4 0.7 %collective-permute-start.2 = (bf16[2,96,384]{2,1,0:T(8,128)(2,1)S(1)}, bf16[2,96,384]{2,1,0:T(8,128)(2,1)S(1)}, u32[]{:S(2)}, u32[]{:S(2)}) collective-permute-start(bf16[2,96,384]{2,1,0:T(8,128)(2,1)S(1)} %get-tuple-element.39), channel_id=1, source_target_pairs={{0,4},{1,12},{2,6},{3,14},{4,0},{5,8},{6,2},{7,10},{8,5},{9,13},{1... | collective-permute-start | bytes 442376 | tf_op jit(solution)/shard_map/ppermute | solution.py:272
  10.2 1.0 %slice-done.1 = bf16[2,48,1536]{2,1,0:T(8,128)(2,1)S(1)} async-done(((bf16[3,48,1536]{2,1,0:T(8,128)(2,1)}), bf16[2,48,1536]{2,1,0:T(8,128)(2,1)S(1)}, s32[]{:S(2)}) %slice-start.1) | async-done | bytes 294936 | tf_op jit(solution)/shard_map/slice | solution.py:285
  11.1 2.6 %shard_map.77 = (bf16[4,48,384]{2,1,0:T(8,128)(2,1)}, bf16[4,48,384]{2,1,0:T(8,128)(2,1)}, bf16[4,48,384]{2,1,0:T(8,128)(2,1)}, bf16[4,48,384]{2,1,0:T(8,128)(2,1)}, bf16[4,256,384]{2,1,0:T(8,128)(2,1)}) custom-call(bf16[3,48,1536]{2,1,0:T(8,128)(2,1)} %first_ref, bf16[3,48,1536]{2,1,0:T(8,128)(2,1)} %second_ref.1, bf16[2,256,768]{2,1,0:T(8,128)(2,1)} %text_first_ref.1, ...), custom_call_target="tpu_custom_call" | custom-call | bytes 1048576 | tf_op jit(solution)/shard_map/pallas_call | solution.py:143
  13.8 1.4 %collective-permute-start = (bf16[4,48,384]{2,1,0:T(8,128)(2,1)}, bf16[4,48,384]{2,1,0:T(8,128)(2,1)S(1)}, u32[]{:S(2)}, u32[]{:S(2)}) collective-permute-start(bf16[4,48,384]{2,1,0:T(8,128)(2,1)} %get-tuple-element.20), channel_id=1, source_target_pairs={{0,4},{2,6},{4,8},{6,10},{8,12},{10,14},{12,0},{14,2},{1,5},{3,7},... | collective-permute-start | bytes 442376 | tf_op jit(solution)/shard_map/ppermute | solution.py:263
  15.3 0.1 pad_maximum_fusion.refs_0_
  15.4 1.6 %collective-permute-start.11 = (bf16[8,96,384]{2,1,0:T(8,128)(2,1)S(1)}, bf16[8,96,384]{2,1,0:T(8,128)(2,1)S(1)}, u32[]{:S(2)}, u32[]{:S(2)}) collective-permute-start(bf16[8,96,384]{2,1,0:T(8,128)(2,1)S(1)} %pad_maximum_fusion.refs_0_), channel_id=1, source_target_pairs={{0,2},{2,0},{4,6},{6,4},{8,10},{10,8},{12,14},{14,12},{1,3},{3,1},... | collective-permute-start | bytes 1769480 | tf_op jit(solution)/shard_map/ppermute | solution.py:275
  17.0 6.6 %collective-permute-start.6 = (bf16[4,48,384]{2,1,0:T(8,128)(2,1)}, bf16[4,48,384]{2,1,0:T(8,128)(2,1)}, u32[]{:S(2)}, u32[]{:S(2)}) collective-permute-start(bf16[4,48,384]{2,1,0:T(8,128)(2,1)} %get-tuple-element.24), channel_id=1, source_target_pairs={{0,8},{2,10},{4,12},{6,14},{8,0},{10,2},{12,4},{14,6},{1,9},{3,11}... | collective-permute-start | bytes 442376 | tf_op jit(solution)/shard_map/ppermute | solution.py:263
  23.9 3.4 %collective-permute-start.7 = (bf16[4,48,384]{2,1,0:T(8,128)(2,1)}, bf16[4,48,384]{2,1,0:T(8,128)(2,1)S(1)}, u32[]{:S(2)}, u32[]{:S(2)}) collective-permute-start(bf16[4,48,384]{2,1,0:T(8,128)(2,1)} %get-tuple-element.25), channel_id=1, source_target_pairs={{0,12},{2,14},{4,0},{6,2},{8,4},{10,6},{12,8},{14,10},{1,13},{3,15... | collective-permute-start | bytes 442376 | tf_op jit(solution)/shard_map/ppermute | solution.py:263
  27.4 2.5 %collective-permute-done.6 = bf16[4,48,384]{2,1,0:T(8,128)(2,1)} collective-permute-done((bf16[4,48,384]{2,1,0:T(8,128)(2,1)}, bf16[4,48,384]{2,1,0:T(8,128)(2,1)}, u32[]{:S(2)}, u32[]{:S(2)}) %collective-permute-start.6) | collective-permute-done | bytes 147488 | tf_op jit(solution)/shard_map/ppermute | solution.py:263
  29.8 0.9 %constant_dynamic-update-slice_fusion.1 = bf16[4,192,384]{2,1,0:T(8,128)(2,1)S(1)} fusion(bf16[4,192,384]{2,1,0:T(8,128)(2,1)S(1)} %constant_dynamic-update-slice_fusion.2, bf16[4,48,384]{2,1,0:T(8,128)(2,1)} %collective-permute-done.6), kind=kLoop, calls=%fused_computation.5 | loop fusion | bytes 294912
  30.8 0.7 %collective-permute-done.7 = bf16[4,48,384]{2,1,0:T(8,128)(2,1)S(1)} collective-permute-done((bf16[4,48,384]{2,1,0:T(8,128)(2,1)}, bf16[4,48,384]{2,1,0:T(8,128)(2,1)S(1)}, u32[]{:S(2)}, u32[]{:S(2)}) %collective-permute-start.7) | collective-permute-done | bytes 147488 | tf_op jit(solution)/shard_map/ppermute | solution.py:263
  31.5 0.1 collective-permute-start.9
  31.6 0.1 fusion.3
  31.9 0.5 %collective-permute-start.12 = (bf16[4,96,384]{2,1,0:T(8,128)(2,1)S(1)}, bf16[4,96,384]{2,1,0:T(8,128)(2,1)S(1)}, u32[]{:S(2)}, u32[]{:S(2)}) collective-permute-start(bf16[4,96,384]{2,1,0:T(8,128)(2,1)S(1)} %get-tuple-element.33), channel_id=1, source_target_pairs={{0,1},{1,0},{2,3},{3,2},{4,5},{5,4},{6,7},{7,6},{8,9},{9,8},{10,11... | collective-permute-start | bytes 884744 | tf_op jit(solution)/shard_map/ppermute | solution.py:278
  32.4 0.1 collective-permute-start.13
  32.5 0.1 add_bitcast_fusion
  32.7 1.0 %collective-permute-done.9.last_twin_ref = bf16[4,192,384]{2,1,0:T(8,128)(2,1)} collective-permute-done((bf16[4,192,384]{2,1,0:T(8,128)(2,1)S(1)}, bf16[4,192,384]{2,1,0:T(8,128)(2,1)}, u32[]{:S(2)}, u32[]{:S(2)}) %collective-permute-start.9) | collective-permute-done | bytes 589856 | tf_op jit(solution)/shard_map/ppermute | solution.py:278
  33.7 0.3 collective-permute-done.12.refs_3_
  34.0 0.4 collective-permute-done.13.refs_4_
  34.4 3.3 %shard_map.79 = (bf16[2,48,384]{2,1,0:T(8,128)(2,1)S(1)}, bf16[2,48,384]{2,1,0:T(8,128)(2,1)S(1)}, bf16[2,48,384]{2,1,0:T(8,128)(2,1)S(1)}) custom-call(f32[2,3]{1,0:T(2,128)S(1)} %fusion.2.scale_ref, s32[3,4]{1,0:T(4,128)S(1)} %add_add_fusion.order_ref, bf16[2,192,384]{2,1,0:T(8,128)(2,1)S(1)} %slice.30.queries_ref, bf16[4,256,384]{2,1,0:T(8,128)(2,1)S(1)} %copy-done, ...), custom_call_target="tpu_custom_call" | custom-call | flops 452984832 | bytes 3440640 | tf_op jit(solution)/shard_map/pallas_call | solution.py:233
  37.7 1.5 %collective-permute-start.14 = (bf16[2,48,384]{2,1,0:T(8,128)(2,1)S(1)}, bf16[2,48,384]{2,1,0:T(8,128)(2,1)S(1)}, u32[]{:S(2)}, u32[]{:S(2)}) collective-permute-start(bf16[2,48,384]{2,1,0:T(8,128)(2,1)S(1)} %get-tuple-element.29), channel_id=1, source_target_pairs={{0,8},{2,10},{4,12},{6,14},{8,0},{10,2},{12,4},{14,6},{1,9},{3,11}... | collective-permute-start | bytes 221192 | tf_op jit(solution)/shard_map/ppermute | solution.py:263
  39.3 2.8 %collective-permute-start.15 = (bf16[2,48,384]{2,1,0:T(8,128)(2,1)S(1)}, bf16[2,48,384]{2,1,0:T(8,128)(2,1)S(1)}, u32[]{:S(2)}, u32[]{:S(2)}) collective-permute-start(bf16[2,48,384]{2,1,0:T(8,128)(2,1)S(1)} %get-tuple-element.30), channel_id=1, source_target_pairs={{0,4},{2,6},{4,8},{6,10},{8,12},{10,14},{12,0},{14,2},{1,5},{3,7},... | collective-permute-start | bytes 221192 | tf_op jit(solution)/shard_map/ppermute | solution.py:263
  42.0 1.1 %collective-permute-start.16 = (bf16[2,48,384]{2,1,0:T(8,128)(2,1)S(1)}, bf16[2,48,384]{2,1,0:T(8,128)(2,1)S(1)}, u32[]{:S(2)}, u32[]{:S(2)}) collective-permute-start(bf16[2,48,384]{2,1,0:T(8,128)(2,1)S(1)} %get-tuple-element.31), channel_id=1, source_target_pairs={{0,12},{2,14},{4,0},{6,2},{8,4},{10,6},{12,8},{14,10},{1,13},{3,15... | collective-permute-start | bytes 221192 | tf_op jit(solution)/shard_map/ppermute | solution.py:263
  43.1 2.6 %shard_map.78 = bf16[2,48,384]{2,1,0:T(8,128)(2,1)S(1)} custom-call(f32[2,3]{1,0:T(2,128)S(1)} %fusion.2.scale_ref, s32[3,4]{1,0:T(4,128)S(1)} %add_add_fusion.order_ref, bf16[2,192,384]{2,1,0:T(8,128)(2,1)S(1)} %slice.30.queries_ref, bf16[4,256,384]{2,1,0:T(8,128)(2,1)S(1)} %copy-done, bf16[4,256,384]{2,1,0:T(8,128)(2,1)S(1)} %collective-permute-done.8.text_twin_ref, ...), custom_call_target="tpu_custom_call" | custom-call | flops 150994944 | bytes 3440640 | tf_op jit(solution)/shard_map/pallas_call | solution.py:233
  45.8 1.2 %collective-permute-done.15 = bf16[2,48,384]{2,1,0:T(8,128)(2,1)S(1)} collective-permute-done((bf16[2,48,384]{2,1,0:T(8,128)(2,1)S(1)}, bf16[2,48,384]{2,1,0:T(8,128)(2,1)S(1)}, u32[]{:S(2)}, u32[]{:S(2)}) %collective-permute-start.15) | collective-permute-done | bytes 73760 | tf_op jit(solution)/shard_map/ppermute | solution.py:263
  47.0 0.2 collective-permute-done.16
  47.2 0.7 %slice_bitcast_fusion = (bf16[48,1536]{1,0:T(8,128)(2,1)}, bf16[48,1536]{1,0:T(8,128)(2,1)}) fusion(bf16[2,48,1536]{2,1,0:T(8,128)(2,1)S(1)} %constant_dynamic-update-slice_fusion.4), kind=kLoop, calls=%fused_computation.2 | loop fusion | bytes 589824 | tf_op jit(solution)/shard_map/squeeze | solution.py:327
  (39 shorter events, 0.7 us)
Async XLA Ops:
  0.7 1.0 %slice-start = ((bf16[3,48,1536]{2,1,0:T(8,128)(2,1)}), bf16[2,48,1536]{2,1,0:T(8,128)(2,1)S(1)}, s32[]{:S(2)}) async-start(bf16[3,48,1536]{2,1,0:T(8,128)(2,1)} %first_ref), calls=%async_computation | async-start | bytes 589824 | tf_op jit(solution)/shard_map/slice | solution.py:284
  0.7 8.0 %copy-start.1 = (bf16[2,96,768]{2,1,0:T(8,128)(2,1)S(1)}, bf16[2,96,768]{2,1,0:T(8,128)(2,1)}, u32[]{:S(2)}) copy-start(bf16[2,96,768]{2,1,0:T(8,128)(2,1)} %param.8) | copy-start | bytes 884740
  1.7 12.1 %collective-permute-start.3 = (bf16[2,48,384]{2,1,0:T(8,128)(2,1)S(1)}, bf16[2,48,384]{2,1,0:T(8,128)(2,1)S(1)}, u32[]{:S(2)}, u32[]{:S(2)}) collective-permute-start(bf16[2,48,384]{2,1,0:T(8,128)(2,1)S(1)} %get-tuple-element.38), channel_id=1, source_target_pairs={{0,4},{2,6},{4,8},{6,10},{8,12},{10,14},{12,0},{14,2},{1,5},{3,7},... | collective-permute-start | bytes 221192 | tf_op jit(solution)/shard_map/ppermute | solution.py:263
  4.8 10.4 %collective-permute-start.4 = (bf16[2,48,384]{2,1,0:T(8,128)(2,1)S(1)}, bf16[2,48,384]{2,1,0:T(8,128)(2,1)S(1)}, u32[]{:S(2)}, u32[]{:S(2)}) collective-permute-start(bf16[2,48,384]{2,1,0:T(8,128)(2,1)S(1)} %get-tuple-element.37), channel_id=1, source_target_pairs={{0,8},{2,10},{4,12},{6,14},{8,0},{10,2},{12,4},{14,6},{1,9},{3,11}... | collective-permute-start | bytes 221192 | tf_op jit(solution)/shard_map/ppermute | solution.py:263
  7.4 7.8 %collective-permute-start.5 = (bf16[2,48,384]{2,1,0:T(8,128)(2,1)S(1)}, bf16[2,48,384]{2,1,0:T(8,128)(2,1)S(1)}, u32[]{:S(2)}, u32[]{:S(2)}) collective-permute-start(bf16[2,48,384]{2,1,0:T(8,128)(2,1)S(1)} %get-tuple-element.36), channel_id=1, source_target_pairs={{0,12},{2,14},{4,0},{6,2},{8,4},{10,6},{12,8},{14,10},{1,13},{3,15... | collective-permute-start | bytes 221192 | tf_op jit(solution)/shard_map/ppermute | solution.py:263
  8.8 6.5 %collective-permute-start.1 = (bf16[2,96,384]{2,1,0:T(8,128)(2,1)S(1)}, bf16[2,96,384]{2,1,0:T(8,128)(2,1)S(1)}, u32[]{:S(2)}, u32[]{:S(2)}) collective-permute-start(bf16[2,96,384]{2,1,0:T(8,128)(2,1)S(1)} %get-tuple-element.40), channel_id=1, source_target_pairs={{0,0},{1,8},{2,2},{3,10},{4,4},{5,12},{6,6},{7,14},{8,1},{9,9},{10... | collective-permute-start | bytes 442376 | tf_op jit(solution)/shard_map/ppermute | solution.py:272
  9.4 5.8 %collective-permute-start.2 = (bf16[2,96,384]{2,1,0:T(8,128)(2,1)S(1)}, bf16[2,96,384]{2,1,0:T(8,128)(2,1)S(1)}, u32[]{:S(2)}, u32[]{:S(2)}) collective-permute-start(bf16[2,96,384]{2,1,0:T(8,128)(2,1)S(1)} %get-tuple-element.39), channel_id=1, source_target_pairs={{0,4},{1,12},{2,6},{3,14},{4,0},{5,8},{6,2},{7,10},{8,5},{9,13},{1... | collective-permute-start | bytes 442376 | tf_op jit(solution)/shard_map/ppermute | solution.py:272
  10.2 1.0 %slice-start.1 = ((bf16[3,48,1536]{2,1,0:T(8,128)(2,1)}), bf16[2,48,1536]{2,1,0:T(8,128)(2,1)S(1)}, s32[]{:S(2)}) async-start(bf16[3,48,1536]{2,1,0:T(8,128)(2,1)} %first_ref), calls=%async_computation.1 | async-start | bytes 589824 | tf_op jit(solution)/shard_map/slice | solution.py:285
  13.8 10.0 %collective-permute-start = (bf16[4,48,384]{2,1,0:T(8,128)(2,1)}, bf16[4,48,384]{2,1,0:T(8,128)(2,1)S(1)}, u32[]{:S(2)}, u32[]{:S(2)}) collective-permute-start(bf16[4,48,384]{2,1,0:T(8,128)(2,1)} %get-tuple-element.20), channel_id=1, source_target_pairs={{0,4},{2,6},{4,8},{6,10},{8,12},{10,14},{12,0},{14,2},{1,5},{3,7},... | collective-permute-start | bytes 442376 | tf_op jit(solution)/shard_map/ppermute | solution.py:263
  15.3 1.7 %copy-start.2 = (bf16[4,48,384]{2,1,0:T(8,128)(2,1)S(1)}, bf16[4,48,384]{2,1,0:T(8,128)(2,1)}, u32[]{:S(2)}) copy-start(bf16[4,48,384]{2,1,0:T(8,128)(2,1)} %get-tuple-element.19) | copy-start | bytes 442372
  15.3 12.0 %copy-start = (bf16[4,256,384]{2,1,0:T(8,128)(2,1)S(1)}, bf16[4,256,384]{2,1,0:T(8,128)(2,1)}, u32[]{:S(2)}) copy-start(bf16[4,256,384]{2,1,0:T(8,128)(2,1)} %get-tuple-element.27.text_ref) | copy-start | bytes 2359300
  15.4 16.4 %collective-permute-start.11 = (bf16[8,96,384]{2,1,0:T(8,128)(2,1)S(1)}, bf16[8,96,384]{2,1,0:T(8,128)(2,1)S(1)}, u32[]{:S(2)}, u32[]{:S(2)}) collective-permute-start(bf16[8,96,384]{2,1,0:T(8,128)(2,1)S(1)} %pad_maximum_fusion.refs_0_), channel_id=1, source_target_pairs={{0,2},{2,0},{4,6},{6,4},{8,10},{10,8},{12,14},{14,12},{1,3},{3,1},... | collective-permute-start | bytes 1769480 | tf_op jit(solution)/shard_map/ppermute | solution.py:275
  17.0 6.6 %copy-start.3 = (s32[2,12]{1,0:T(2,128)S(1)}, s32[2,12]{1,0:T(2,128)}, u32[]{:S(2)}) copy-start(s32[2,12]{1,0:T(2,128)} %param.9) | copy-start | bytes 292
  17.0 12.8 %collective-permute-start.6 = (bf16[4,48,384]{2,1,0:T(8,128)(2,1)}, bf16[4,48,384]{2,1,0:T(8,128)(2,1)}, u32[]{:S(2)}, u32[]{:S(2)}) collective-permute-start(bf16[4,48,384]{2,1,0:T(8,128)(2,1)} %get-tuple-element.24), channel_id=1, source_target_pairs={{0,8},{2,10},{4,12},{6,14},{8,0},{10,2},{12,4},{14,6},{1,9},{3,11}... | collective-permute-start | bytes 442376 | tf_op jit(solution)/shard_map/ppermute | solution.py:263
  23.8 8.8 %collective-permute-start.10 = (bf16[8,96,384]{2,1,0:T(8,128)(2,1)S(1)}, bf16[8,96,384]{2,1,0:T(8,128)(2,1)}, u32[]{:S(2)}, u32[]{:S(2)}) collective-permute-start(bf16[8,96,384]{2,1,0:T(8,128)(2,1)S(1)} %pad_maximum_fusion.refs_0_), channel_id=1, source_target_pairs={{0,1},{1,0},{2,3},{3,2},{4,5},{5,4},{6,7},{7,6},{8,9},{9,8},{10,11... | collective-permute-start | bytes 1769480 | tf_op jit(solution)/shard_map/ppermute | solution.py:278
  23.9 7.6 %collective-permute-start.7 = (bf16[4,48,384]{2,1,0:T(8,128)(2,1)}, bf16[4,48,384]{2,1,0:T(8,128)(2,1)S(1)}, u32[]{:S(2)}, u32[]{:S(2)}) collective-permute-start(bf16[4,48,384]{2,1,0:T(8,128)(2,1)} %get-tuple-element.25), channel_id=1, source_target_pairs={{0,12},{2,14},{4,0},{6,2},{8,4},{10,6},{12,8},{14,10},{1,13},{3,15... | collective-permute-start | bytes 442376 | tf_op jit(solution)/shard_map/ppermute | solution.py:263
  27.3 6.4 %collective-permute-start.8 = (bf16[4,256,384]{2,1,0:T(8,128)(2,1)S(1)}, bf16[4,256,384]{2,1,0:T(8,128)(2,1)S(1)}, u32[]{:S(2)}, u32[]{:S(2)}) collective-permute-start(bf16[4,256,384]{2,1,0:T(8,128)(2,1)S(1)} %copy-done), channel_id=1, source_target_pairs={{0,1},{1,0},{2,3},{3,2},{4,5},{5,4},{6,7},{7,6},{8,9},{9,8},{10,11... | collective-permute-start | bytes 2359304 | tf_op jit(solution)/shard_map/ppermute | solution.py:278
  31.5 2.2 %collective-permute-start.9 = (bf16[4,192,384]{2,1,0:T(8,128)(2,1)S(1)}, bf16[4,192,384]{2,1,0:T(8,128)(2,1)}, u32[]{:S(2)}, u32[]{:S(2)}) collective-permute-start(bf16[4,192,384]{2,1,0:T(8,128)(2,1)S(1)} %constant_dynamic-update-slice_fusion.last_ref), channel_id=1, source_target_pairs={{0,1},{1,0},{2,3},{3,2},{4,5},{5,4},{6,7},{7,6},{8,9},{9,8},{10,11... | collective-permute-start | bytes 1769480 | tf_op jit(solution)/shard_map/ppermute | solution.py:278
  31.9 2.1 %collective-permute-start.12 = (bf16[4,96,384]{2,1,0:T(8,128)(2,1)S(1)}, bf16[4,96,384]{2,1,0:T(8,128)(2,1)S(1)}, u32[]{:S(2)}, u32[]{:S(2)}) collective-permute-start(bf16[4,96,384]{2,1,0:T(8,128)(2,1)S(1)} %get-tuple-element.33), channel_id=1, source_target_pairs={{0,1},{1,0},{2,3},{3,2},{4,5},{5,4},{6,7},{7,6},{8,9},{9,8},{10,11... | collective-permute-start | bytes 884744 | tf_op jit(solution)/shard_map/ppermute | solution.py:278
  32.4 2.0 %collective-permute-start.13 = (bf16[4,96,384]{2,1,0:T(8,128)(2,1)S(1)}, bf16[4,96,384]{2,1,0:T(8,128)(2,1)S(1)}, u32[]{:S(2)}, u32[]{:S(2)}) collective-permute-start(bf16[4,96,384]{2,1,0:T(8,128)(2,1)S(1)} %get-tuple-element.32), channel_id=1, source_target_pairs={{0,1},{1,0},{2,3},{3,2},{4,5},{5,4},{6,7},{7,6},{8,9},{9,8},{10,11... | collective-permute-start | bytes 884744 | tf_op jit(solution)/shard_map/ppermute | solution.py:278
  37.7 8.0 %collective-permute-start.14 = (bf16[2,48,384]{2,1,0:T(8,128)(2,1)S(1)}, bf16[2,48,384]{2,1,0:T(8,128)(2,1)S(1)}, u32[]{:S(2)}, u32[]{:S(2)}) collective-permute-start(bf16[2,48,384]{2,1,0:T(8,128)(2,1)S(1)} %get-tuple-element.29), channel_id=1, source_target_pairs={{0,8},{2,10},{4,12},{6,14},{8,0},{10,2},{12,4},{14,6},{1,9},{3,11}... | collective-permute-start | bytes 221192 | tf_op jit(solution)/shard_map/ppermute | solution.py:263
  39.3 7.7 %collective-permute-start.15 = (bf16[2,48,384]{2,1,0:T(8,128)(2,1)S(1)}, bf16[2,48,384]{2,1,0:T(8,128)(2,1)S(1)}, u32[]{:S(2)}, u32[]{:S(2)}) collective-permute-start(bf16[2,48,384]{2,1,0:T(8,128)(2,1)S(1)} %get-tuple-element.30), channel_id=1, source_target_pairs={{0,4},{2,6},{4,8},{6,10},{8,12},{10,14},{12,0},{14,2},{1,5},{3,7},... | collective-permute-start | bytes 221192 | tf_op jit(solution)/shard_map/ppermute | solution.py:263
  42.0 5.2 %collective-permute-start.16 = (bf16[2,48,384]{2,1,0:T(8,128)(2,1)S(1)}, bf16[2,48,384]{2,1,0:T(8,128)(2,1)S(1)}, u32[]{:S(2)}, u32[]{:S(2)}) collective-permute-start(bf16[2,48,384]{2,1,0:T(8,128)(2,1)S(1)} %get-tuple-element.31), channel_id=1, source_target_pairs={{0,12},{2,14},{4,0},{6,2},{8,4},{10,6},{12,8},{14,10},{1,13},{3,15... | collective-permute-start | bytes 221192 | tf_op jit(solution)/shard_map/ppermute | solution.py:263

commit v8 on v7

--- a/solution.py
+++ b/solution.py
@@ -306,7 +306,7 @@
     last = jnp.concatenate(owned, 1)
     near_twin = [other_core(after(near, owned[1]))]
     last_twin = other_core(last)
-    text_twin = other_core(after(text, owned[1]))
+    text_twin = other_core(text)
     sets = [[near], near_twin, away, away_twin]
 
     scales = jnp.exp2(lax.dynamic_slice_in_dim(stale_exponent, layer * heads, heads, 1).astype(F32))

time: 48.4 us -> 48.3 us (level)
  starting transfers between devices: 27.6 us -> 28.9 us
  local copies, waits for them, and re-layouts: 3.98 us -> 3.07 us
    ppermute x5, starting transfers between devices: 0.79 us -> 2.25 us  [other_core(): return lax.ppermute(x, 'uly', [(0, 1), (1, 0)])]
    unnamed x11, local copies, waits for them, and re-layouts: 0.99 us -> 0.08 us
  transfers between devices with their start and end apart: 17 -> 17, of which waited for: 7 -> 7; matrix products, arithmetic and copies ran while one was open for 4% -> 2% of each run, Pallas kernels for 11% -> 10%
where the time goes in v8:
time: 48.3 us; the launch traced here: 48 us
  starting transfers between devices  28.9 us (60%)
  Pallas kernels  8.15 us (17%)
  waiting for transfers between devices  6.43 us (13%)
  local copies, waits for them, and re-layouts  3.07 us (6%)
  between operations  1.07 us (2%)
    ppermute x9, starting transfers between devices, layer_swap(): return x if shift == 0 else lax.ppermute(x, 'patch', pairs)  23.6 us
    pallas_call x2, Pallas kernels, call_both(): pl.pallas_call(functools.partial(both_kernel, parts=parts, blocks=blocks,...  5.51 us
    ppermute x9, waiting for transfers between devices, layer_swap(): return x if shift == 0 else lax.ppermute(x, 'patch', pairs)  5.02 us
    pallas_call x1, Pallas kernels, pack(): pl.pallas_call(kernel, out_shape=[jax.ShapeDtypeStruct(shape, BF16) for s...  2.63 us
    ppermute x5, starting transfers between devices, other_core(): return lax.ppermute(x, 'uly', [(0, 1), (1, 0)])  2.25 us
    ppermute x1, starting transfers between devices, other_column(): lax.ppermute(x, 'patch', [(p, p ^ 1) for p in range(layers * COLUMNS)])  1.58 us
    ppermute x5, waiting for transfers between devices, other_core(): return lax.ppermute(x, 'uly', [(0, 1), (1, 0)])  1.41 us
    ppermute x2, starting transfers between devices, stale_round(): return lax.ppermute(x, ('patch', 'uly'), pairs)  1.41 us
  transfers between devices with their start and end apart: 17, of which 7 were waited for; matrix products, arithmetic and copies ran while one was open for 2% of the time, Pallas kernels for 10%

profile of v8, /device:TPU:0, one launch (start us, length us, event | category | flops | bytes accessed | tf_op | source)
XLA Modules:
  0.0 48.0 jit_solution(7400847059193692728)
XLA Ops:
  0.7 0.9 %slice-done = bf16[2,48,1536]{2,1,0:T(8,128)(2,1)S(1)} async-done(((bf16[3,48,1536]{2,1,0:T(8,128)(2,1)}), bf16[2,48,1536]{2,1,0:T(8,128)(2,1)S(1)}, s32[]{:S(2)}) %slice-start) | async-done | bytes 294936 | tf_op jit(solution)/shard_map/slice | solution.py:284
  1.7 3.1 %collective-permute-start.3 = (bf16[2,48,384]{2,1,0:T(8,128)(2,1)S(1)}, bf16[2,48,384]{2,1,0:T(8,128)(2,1)S(1)}, u32[]{:S(2)}, u32[]{:S(2)}) collective-permute-start(bf16[2,48,384]{2,1,0:T(8,128)(2,1)S(1)} %get-tuple-element.36), channel_id=1, source_target_pairs={{0,4},{2,6},{4,8},{6,10},{8,12},{10,14},{12,0},{14,2},{1,5},{3,7},... | collective-permute-start | bytes 221192 | tf_op jit(solution)/shard_map/ppermute | solution.py:263
  4.8 2.6 %collective-permute-start.4 = (bf16[2,48,384]{2,1,0:T(8,128)(2,1)S(1)}, bf16[2,48,384]{2,1,0:T(8,128)(2,1)S(1)}, u32[]{:S(2)}, u32[]{:S(2)}) collective-permute-start(bf16[2,48,384]{2,1,0:T(8,128)(2,1)S(1)} %get-tuple-element.35), channel_id=1, source_target_pairs={{0,8},{2,10},{4,12},{6,14},{8,0},{10,2},{12,4},{14,6},{1,9},{3,11}... | collective-permute-start | bytes 221192 | tf_op jit(solution)/shard_map/ppermute | solution.py:263
  7.4 1.3 %collective-permute-start.5 = (bf16[2,48,384]{2,1,0:T(8,128)(2,1)S(1)}, bf16[2,48,384]{2,1,0:T(8,128)(2,1)S(1)}, u32[]{:S(2)}, u32[]{:S(2)}) collective-permute-start(bf16[2,48,384]{2,1,0:T(8,128)(2,1)S(1)} %get-tuple-element.34), channel_id=1, source_target_pairs={{0,12},{2,14},{4,0},{6,2},{8,4},{10,6},{12,8},{14,10},{1,13},{3,15... | collective-permute-start | bytes 221192 | tf_op jit(solution)/shard_map/ppermute | solution.py:263
  8.8 0.7 %collective-permute-start.1 = (bf16[2,96,384]{2,1,0:T(8,128)(2,1)S(1)}, bf16[2,96,384]{2,1,0:T(8,128)(2,1)S(1)}, u32[]{:S(2)}, u32[]{:S(2)}) collective-permute-start(bf16[2,96,384]{2,1,0:T(8,128)(2,1)S(1)} %get-tuple-element.38), channel_id=1, source_target_pairs={{0,0},{1,8},{2,2},{3,10},{4,4},{5,12},{6,6},{7,14},{8,1},{9,9},{10... | collective-permute-start | bytes 442376 | tf_op jit(solution)/shard_map/ppermute | solution.py:272
  9.4 0.7 %collective-permute-start.2 = (bf16[2,96,384]{2,1,0:T(8,128)(2,1)S(1)}, bf16[2,96,384]{2,1,0:T(8,128)(2,1)S(1)}, u32[]{:S(2)}, u32[]{:S(2)}) collective-permute-start(bf16[2,96,384]{2,1,0:T(8,128)(2,1)S(1)} %get-tuple-element.37), channel_id=1, source_target_pairs={{0,4},{1,12},{2,6},{3,14},{4,0},{5,8},{6,2},{7,10},{8,5},{9,13},{1... | collective-permute-start | bytes 442376 | tf_op jit(solution)/shard_map/ppermute | solution.py:272
  10.2 1.0 %slice-done.1 = bf16[2,48,1536]{2,1,0:T(8,128)(2,1)S(1)} async-done(((bf16[3,48,1536]{2,1,0:T(8,128)(2,1)}), bf16[2,48,1536]{2,1,0:T(8,128)(2,1)S(1)}, s32[]{:S(2)}) %slice-start.1) | async-done | bytes 294936 | tf_op jit(solution)/shard_map/slice | solution.py:285
  11.1 2.6 %shard_map.77 = (bf16[4,48,384]{2,1,0:T(8,128)(2,1)}, bf16[4,48,384]{2,1,0:T(8,128)(2,1)}, bf16[4,48,384]{2,1,0:T(8,128)(2,1)}, bf16[4,48,384]{2,1,0:T(8,128)(2,1)}, bf16[4,256,384]{2,1,0:T(8,128)(2,1)}) custom-call(bf16[3,48,1536]{2,1,0:T(8,128)(2,1)} %first_ref, bf16[3,48,1536]{2,1,0:T(8,128)(2,1)} %second_ref.1, bf16[2,256,768]{2,1,0:T(8,128)(2,1)} %text_first_ref.1, ...), custom_call_target="tpu_custom_call" | custom-call | bytes 1048576 | tf_op jit(solution)/shard_map/pallas_call | solution.py:143
  13.8 1.4 %collective-permute-start = (bf16[4,48,384]{2,1,0:T(8,128)(2,1)}, bf16[4,48,384]{2,1,0:T(8,128)(2,1)S(1)}, u32[]{:S(2)}, u32[]{:S(2)}) collective-permute-start(bf16[4,48,384]{2,1,0:T(8,128)(2,1)} %get-tuple-element.19), channel_id=1, source_target_pairs={{0,4},{2,6},{4,8},{6,10},{8,12},{10,14},{12,0},{14,2},{1,5},{3,7},... | collective-permute-start | bytes 442376 | tf_op jit(solution)/shard_map/ppermute | solution.py:263
  15.2 1.1 %collective-permute-start.8 = (bf16[4,256,384]{2,1,0:T(8,128)(2,1)}, bf16[4,256,384]{2,1,0:T(8,128)(2,1)S(1)}, u32[]{:S(2)}, u32[]{:S(2)}) collective-permute-start(bf16[4,256,384]{2,1,0:T(8,128)(2,1)} %get-tuple-element.25.text_ref), channel_id=1, source_target_pairs={{0,1},{1,0},{2,3},{3,2},{4,5},{5,4},{6,7},{7,6},{8,9},{9,8},{10,11... | collective-permute-start | bytes 2359304 | tf_op jit(solution)/shard_map/ppermute | solution.py:278
  16.4 0.1 pad_maximum_fusion.refs_0_
  16.5 1.6 %collective-permute-start.11 = (bf16[8,96,384]{2,1,0:T(8,128)(2,1)S(1)}, bf16[8,96,384]{2,1,0:T(8,128)(2,1)S(1)}, u32[]{:S(2)}, u32[]{:S(2)}) collective-permute-start(bf16[8,96,384]{2,1,0:T(8,128)(2,1)S(1)} %pad_maximum_fusion.refs_0_), channel_id=1, source_target_pairs={{0,2},{2,0},{4,6},{6,4},{8,10},{10,8},{12,14},{14,12},{1,3},{3,1},... | collective-permute-start | bytes 1769480 | tf_op jit(solution)/shard_map/ppermute | solution.py:275
  18.1 5.5 %collective-permute-start.6 = (bf16[4,48,384]{2,1,0:T(8,128)(2,1)}, bf16[4,48,384]{2,1,0:T(8,128)(2,1)S(1)}, u32[]{:S(2)}, u32[]{:S(2)}) collective-permute-start(bf16[4,48,384]{2,1,0:T(8,128)(2,1)} %get-tuple-element.23), channel_id=1, source_target_pairs={{0,8},{2,10},{4,12},{6,14},{8,0},{10,2},{12,4},{14,6},{1,9},{3,11}... | collective-permute-start | bytes 442376 | tf_op jit(solution)/shard_map/ppermute | solution.py:263
  23.9 3.4 %collective-permute-start.7 = (bf16[4,48,384]{2,1,0:T(8,128)(2,1)}, bf16[4,48,384]{2,1,0:T(8,128)(2,1)S(1)}, u32[]{:S(2)}, u32[]{:S(2)}) collective-permute-start(bf16[4,48,384]{2,1,0:T(8,128)(2,1)} %get-tuple-element.24), channel_id=1, source_target_pairs={{0,12},{2,14},{4,0},{6,2},{8,4},{10,6},{12,8},{14,10},{1,13},{3,15... | collective-permute-start | bytes 442376 | tf_op jit(solution)/shard_map/ppermute | solution.py:263
  27.3 2.3 %collective-permute-done.6 = bf16[4,48,384]{2,1,0:T(8,128)(2,1)S(1)} collective-permute-done((bf16[4,48,384]{2,1,0:T(8,128)(2,1)}, bf16[4,48,384]{2,1,0:T(8,128)(2,1)S(1)}, u32[]{:S(2)}, u32[]{:S(2)}) %collective-permute-start.6) | collective-permute-done | bytes 147488 | tf_op jit(solution)/shard_map/ppermute | solution.py:263
  29.7 1.8 %collective-permute-done.7 = bf16[4,48,384]{2,1,0:T(8,128)(2,1)S(1)} collective-permute-done((bf16[4,48,384]{2,1,0:T(8,128)(2,1)}, bf16[4,48,384]{2,1,0:T(8,128)(2,1)S(1)}, u32[]{:S(2)}, u32[]{:S(2)}) %collective-permute-start.7) | collective-permute-done | bytes 147488 | tf_op jit(solution)/shard_map/ppermute | solution.py:263
  31.5 0.1 collective-permute-start.9
  31.6 0.1 fusion.3
  31.9 0.8 %collective-permute-start.12 = (bf16[4,96,384]{2,1,0:T(8,128)(2,1)S(1)}, bf16[4,96,384]{2,1,0:T(8,128)(2,1)S(1)}, u32[]{:S(2)}, u32[]{:S(2)}) collective-permute-start(bf16[4,96,384]{2,1,0:T(8,128)(2,1)S(1)} %get-tuple-element.31), channel_id=1, source_target_pairs={{0,1},{1,0},{2,3},{3,2},{4,5},{5,4},{6,7},{7,6},{8,9},{9,8},{10,11... | collective-permute-start | bytes 884744 | tf_op jit(solution)/shard_map/ppermute | solution.py:278
  32.7 0.1 collective-permute-start.13
  32.8 0.1 add_bitcast_fusion
  33.0 0.7 %collective-permute-done.9.last_twin_ref = bf16[4,192,384]{2,1,0:T(8,128)(2,1)} collective-permute-done((bf16[4,192,384]{2,1,0:T(8,128)(2,1)S(1)}, bf16[4,192,384]{2,1,0:T(8,128)(2,1)}, u32[]{:S(2)}, u32[]{:S(2)}) %collective-permute-start.9) | collective-permute-done | bytes 589856 | tf_op jit(solution)/shard_map/ppermute | solution.py:278
  33.7 0.3 collective-permute-done.12.refs_3_
  34.0 0.4 collective-permute-done.13.refs_4_
  34.4 3.1 %shard_map.79 = (bf16[2,48,384]{2,1,0:T(8,128)(2,1)S(1)}, bf16[2,48,384]{2,1,0:T(8,128)(2,1)S(1)}, bf16[2,48,384]{2,1,0:T(8,128)(2,1)S(1)}) custom-call(f32[2,3]{1,0:T(2,128)S(1)} %fusion.2.scale_ref, s32[3,4]{1,0:T(4,128)S(1)} %add_add_fusion.order_ref, bf16[2,192,384]{2,1,0:T(8,128)(2,1)S(1)} %slice.30.queries_ref, bf16[4,256,384]{2,1,0:T(8,128)(2,1)S(1)} %copy-done, ...), custom_call_target="tpu_custom_call" | custom-call | flops 452984832 | bytes 3440640 | tf_op jit(solution)/shard_map/pallas_call | solution.py:233
  37.5 2.5 %collective-permute-start.14 = (bf16[2,48,384]{2,1,0:T(8,128)(2,1)S(1)}, bf16[2,48,384]{2,1,0:T(8,128)(2,1)S(1)}, u32[]{:S(2)}, u32[]{:S(2)}) collective-permute-start(bf16[2,48,384]{2,1,0:T(8,128)(2,1)S(1)} %get-tuple-element.27), channel_id=1, source_target_pairs={{0,8},{2,10},{4,12},{6,14},{8,0},{10,2},{12,4},{14,6},{1,9},{3,11}... | collective-permute-start | bytes 221192 | tf_op jit(solution)/shard_map/ppermute | solution.py:263
  40.0 1.8 %collective-permute-start.15 = (bf16[2,48,384]{2,1,0:T(8,128)(2,1)S(1)}, bf16[2,48,384]{2,1,0:T(8,128)(2,1)S(1)}, u32[]{:S(2)}, u32[]{:S(2)}) collective-permute-start(bf16[2,48,384]{2,1,0:T(8,128)(2,1)S(1)} %get-tuple-element.28), channel_id=1, source_target_pairs={{0,4},{2,6},{4,8},{6,10},{8,12},{10,14},{12,0},{14,2},{1,5},{3,7},... | collective-permute-start | bytes 221192 | tf_op jit(solution)/shard_map/ppermute | solution.py:263
  41.9 2.0 %collective-permute-start.16 = (bf16[2,48,384]{2,1,0:T(8,128)(2,1)S(1)}, bf16[2,48,384]{2,1,0:T(8,128)(2,1)S(1)}, u32[]{:S(2)}, u32[]{:S(2)}) collective-permute-start(bf16[2,48,384]{2,1,0:T(8,128)(2,1)S(1)} %get-tuple-element.29), channel_id=1, source_target_pairs={{0,12},{2,14},{4,0},{6,2},{8,4},{10,6},{12,8},{14,10},{1,13},{3,15... | collective-permute-start | bytes 221192 | tf_op jit(solution)/shard_map/ppermute | solution.py:263
  43.8 2.4 %shard_map.78 = bf16[2,48,384]{2,1,0:T(8,128)(2,1)S(1)} custom-call(f32[2,3]{1,0:T(2,128)S(1)} %fusion.2.scale_ref, s32[3,4]{1,0:T(4,128)S(1)} %add_add_fusion.order_ref, bf16[2,192,384]{2,1,0:T(8,128)(2,1)S(1)} %slice.30.queries_ref, bf16[4,256,384]{2,1,0:T(8,128)(2,1)S(1)} %copy-done, bf16[4,256,384]{2,1,0:T(8,128)(2,1)S(1)} %collective-permute-done.8.text_twin_ref, ...), custom_call_target="tpu_custom_call" | custom-call | flops 150994944 | bytes 3440640 | tf_op jit(solution)/shard_map/pallas_call | solution.py:233
  46.3 0.5 %collective-permute-done.15 = bf16[2,48,384]{2,1,0:T(8,128)(2,1)S(1)} collective-permute-done((bf16[2,48,384]{2,1,0:T(8,128)(2,1)S(1)}, bf16[2,48,384]{2,1,0:T(8,128)(2,1)S(1)}, u32[]{:S(2)}, u32[]{:S(2)}) %collective-permute-start.15) | collective-permute-done | bytes 73760 | tf_op jit(solution)/shard_map/ppermute | solution.py:263
  46.9 0.4 collective-permute-done.16
  47.3 0.7 %slice_bitcast_fusion = (bf16[48,1536]{1,0:T(8,128)(2,1)}, bf16[48,1536]{1,0:T(8,128)(2,1)}) fusion(bf16[2,48,1536]{2,1,0:T(8,128)(2,1)S(1)} %constant_dynamic-update-slice_fusion.4), kind=kLoop, calls=%fused_computation.2 | loop fusion | bytes 589824 | tf_op jit(solution)/shard_map/squeeze | solution.py:327
  (39 shorter events, 0.7 us)
Async XLA Ops:
  0.7 1.0 %slice-start = ((bf16[3,48,1536]{2,1,0:T(8,128)(2,1)}), bf16[2,48,1536]{2,1,0:T(8,128)(2,1)S(1)}, s32[]{:S(2)}) async-start(bf16[3,48,1536]{2,1,0:T(8,128)(2,1)} %first_ref), calls=%async_computation | async-start | bytes 589824 | tf_op jit(solution)/shard_map/slice | solution.py:284
  0.7 8.0 %copy-start.1 = (bf16[2,96,768]{2,1,0:T(8,128)(2,1)S(1)}, bf16[2,96,768]{2,1,0:T(8,128)(2,1)}, u32[]{:S(2)}) copy-start(bf16[2,96,768]{2,1,0:T(8,128)(2,1)} %param.8) | copy-start | bytes 884740
  1.7 12.1 %collective-permute-start.3 = (bf16[2,48,384]{2,1,0:T(8,128)(2,1)S(1)}, bf16[2,48,384]{2,1,0:T(8,128)(2,1)S(1)}, u32[]{:S(2)}, u32[]{:S(2)}) collective-permute-start(bf16[2,48,384]{2,1,0:T(8,128)(2,1)S(1)} %get-tuple-element.36), channel_id=1, source_target_pairs={{0,4},{2,6},{4,8},{6,10},{8,12},{10,14},{12,0},{14,2},{1,5},{3,7},... | collective-permute-start | bytes 221192 | tf_op jit(solution)/shard_map/ppermute | solution.py:263
  4.8 10.4 %collective-permute-start.4 = (bf16[2,48,384]{2,1,0:T(8,128)(2,1)S(1)}, bf16[2,48,384]{2,1,0:T(8,128)(2,1)S(1)}, u32[]{:S(2)}, u32[]{:S(2)}) collective-permute-start(bf16[2,48,384]{2,1,0:T(8,128)(2,1)S(1)} %get-tuple-element.35), channel_id=1, source_target_pairs={{0,8},{2,10},{4,12},{6,14},{8,0},{10,2},{12,4},{14,6},{1,9},{3,11}... | collective-permute-start | bytes 221192 | tf_op jit(solution)/shard_map/ppermute | solution.py:263
  7.4 9.0 %collective-permute-start.5 = (bf16[2,48,384]{2,1,0:T(8,128)(2,1)S(1)}, bf16[2,48,384]{2,1,0:T(8,128)(2,1)S(1)}, u32[]{:S(2)}, u32[]{:S(2)}) collective-permute-start(bf16[2,48,384]{2,1,0:T(8,128)(2,1)S(1)} %get-tuple-element.34), channel_id=1, source_target_pairs={{0,12},{2,14},{4,0},{6,2},{8,4},{10,6},{12,8},{14,10},{1,13},{3,15... | collective-permute-start | bytes 221192 | tf_op jit(solution)/shard_map/ppermute | solution.py:263
  8.8 7.6 %collective-permute-start.1 = (bf16[2,96,384]{2,1,0:T(8,128)(2,1)S(1)}, bf16[2,96,384]{2,1,0:T(8,128)(2,1)S(1)}, u32[]{:S(2)}, u32[]{:S(2)}) collective-permute-start(bf16[2,96,384]{2,1,0:T(8,128)(2,1)S(1)} %get-tuple-element.38), channel_id=1, source_target_pairs={{0,0},{1,8},{2,2},{3,10},{4,4},{5,12},{6,6},{7,14},{8,1},{9,9},{10... | collective-permute-start | bytes 442376 | tf_op jit(solution)/shard_map/ppermute | solution.py:272
  9.4 7.0 %collective-permute-start.2 = (bf16[2,96,384]{2,1,0:T(8,128)(2,1)S(1)}, bf16[2,96,384]{2,1,0:T(8,128)(2,1)S(1)}, u32[]{:S(2)}, u32[]{:S(2)}) collective-permute-start(bf16[2,96,384]{2,1,0:T(8,128)(2,1)S(1)} %get-tuple-element.37), channel_id=1, source_target_pairs={{0,4},{1,12},{2,6},{3,14},{4,0},{5,8},{6,2},{7,10},{8,5},{9,13},{1... | collective-permute-start | bytes 442376 | tf_op jit(solution)/shard_map/ppermute | solution.py:272
  10.2 1.0 %slice-start.1 = ((bf16[3,48,1536]{2,1,0:T(8,128)(2,1)}), bf16[2,48,1536]{2,1,0:T(8,128)(2,1)S(1)}, s32[]{:S(2)}) async-start(bf16[3,48,1536]{2,1,0:T(8,128)(2,1)} %first_ref), calls=%async_computation.1 | async-start | bytes 589824 | tf_op jit(solution)/shard_map/slice | solution.py:285
  13.8 10.0 %collective-permute-start = (bf16[4,48,384]{2,1,0:T(8,128)(2,1)}, bf16[4,48,384]{2,1,0:T(8,128)(2,1)S(1)}, u32[]{:S(2)}, u32[]{:S(2)}) collective-permute-start(bf16[4,48,384]{2,1,0:T(8,128)(2,1)} %get-tuple-element.19), channel_id=1, source_target_pairs={{0,4},{2,6},{4,8},{6,10},{8,12},{10,14},{12,0},{14,2},{1,5},{3,7},... | collective-permute-start | bytes 442376 | tf_op jit(solution)/shard_map/ppermute | solution.py:263
  15.2 17.8 %collective-permute-start.8 = (bf16[4,256,384]{2,1,0:T(8,128)(2,1)}, bf16[4,256,384]{2,1,0:T(8,128)(2,1)S(1)}, u32[]{:S(2)}, u32[]{:S(2)}) collective-permute-start(bf16[4,256,384]{2,1,0:T(8,128)(2,1)} %get-tuple-element.25.text_ref), channel_id=1, source_target_pairs={{0,1},{1,0},{2,3},{3,2},{4,5},{5,4},{6,7},{7,6},{8,9},{9,8},{10,11... | collective-permute-start | bytes 2359304 | tf_op jit(solution)/shard_map/ppermute | solution.py:278
  16.4 1.7 %copy-start.2 = (bf16[4,48,384]{2,1,0:T(8,128)(2,1)S(1)}, bf16[4,48,384]{2,1,0:T(8,128)(2,1)}, u32[]{:S(2)}) copy-start(bf16[4,48,384]{2,1,0:T(8,128)(2,1)} %get-tuple-element.18) | copy-start | bytes 442372
  16.5 15.3 %collective-permute-start.11 = (bf16[8,96,384]{2,1,0:T(8,128)(2,1)S(1)}, bf16[8,96,384]{2,1,0:T(8,128)(2,1)S(1)}, u32[]{:S(2)}, u32[]{:S(2)}) collective-permute-start(bf16[8,96,384]{2,1,0:T(8,128)(2,1)S(1)} %pad_maximum_fusion.refs_0_), channel_id=1, source_target_pairs={{0,2},{2,0},{4,6},{6,4},{8,10},{10,8},{12,14},{14,12},{1,3},{3,1},... | collective-permute-start | bytes 1769480 | tf_op jit(solution)/shard_map/ppermute | solution.py:275
  18.1 5.5 %copy-start.3 = (s32[2,12]{1,0:T(2,128)S(1)}, s32[2,12]{1,0:T(2,128)}, u32[]{:S(2)}) copy-start(s32[2,12]{1,0:T(2,128)} %param.9) | copy-start | bytes 292
  18.1 11.5 %collective-permute-start.6 = (bf16[4,48,384]{2,1,0:T(8,128)(2,1)}, bf16[4,48,384]{2,1,0:T(8,128)(2,1)S(1)}, u32[]{:S(2)}, u32[]{:S(2)}) collective-permute-start(bf16[4,48,384]{2,1,0:T(8,128)(2,1)} %get-tuple-element.23), channel_id=1, source_target_pairs={{0,8},{2,10},{4,12},{6,14},{8,0},{10,2},{12,4},{14,6},{1,9},{3,11}... | collective-permute-start | bytes 442376 | tf_op jit(solution)/shard_map/ppermute | solution.py:263
  23.8 9.2 %collective-permute-start.10 = (bf16[8,96,384]{2,1,0:T(8,128)(2,1)S(1)}, bf16[8,96,384]{2,1,0:T(8,128)(2,1)S(1)}, u32[]{:S(2)}, u32[]{:S(2)}) collective-permute-start(bf16[8,96,384]{2,1,0:T(8,128)(2,1)S(1)} %pad_maximum_fusion.refs_0_), channel_id=1, source_target_pairs={{0,1},{1,0},{2,3},{3,2},{4,5},{5,4},{6,7},{7,6},{8,9},{9,8},{10,11... | collective-permute-start | bytes 1769480 | tf_op jit(solution)/shard_map/ppermute | solution.py:278
  23.9 7.6 %collective-permute-start.7 = (bf16[4,48,384]{2,1,0:T(8,128)(2,1)}, bf16[4,48,384]{2,1,0:T(8,128)(2,1)S(1)}, u32[]{:S(2)}, u32[]{:S(2)}) collective-permute-start(bf16[4,48,384]{2,1,0:T(8,128)(2,1)} %get-tuple-element.24), channel_id=1, source_target_pairs={{0,12},{2,14},{4,0},{6,2},{8,4},{10,6},{12,8},{14,10},{1,13},{3,15... | collective-permute-start | bytes 442376 | tf_op jit(solution)/shard_map/ppermute | solution.py:263
  31.5 2.2 %collective-permute-start.9 = (bf16[4,192,384]{2,1,0:T(8,128)(2,1)S(1)}, bf16[4,192,384]{2,1,0:T(8,128)(2,1)}, u32[]{:S(2)}, u32[]{:S(2)}) collective-permute-start(bf16[4,192,384]{2,1,0:T(8,128)(2,1)S(1)} %constant_dynamic-update-slice_fusion.last_ref), channel_id=1, source_target_pairs={{0,1},{1,0},{2,3},{3,2},{4,5},{5,4},{6,7},{7,6},{8,9},{9,8},{10,11... | collective-permute-start | bytes 1769480 | tf_op jit(solution)/shard_map/ppermute | solution.py:278
  31.8 2.6 %copy-start = (bf16[4,256,384]{2,1,0:T(8,128)(2,1)S(1)}, bf16[4,256,384]{2,1,0:T(8,128)(2,1)}, u32[]{:S(2)}) copy-start(bf16[4,256,384]{2,1,0:T(8,128)(2,1)} %get-tuple-element.25.text_ref) | copy-start | bytes 2359300
  31.9 2.1 %collective-permute-start.12 = (bf16[4,96,384]{2,1,0:T(8,128)(2,1)S(1)}, bf16[4,96,384]{2,1,0:T(8,128)(2,1)S(1)}, u32[]{:S(2)}, u32[]{:S(2)}) collective-permute-start(bf16[4,96,384]{2,1,0:T(8,128)(2,1)S(1)} %get-tuple-element.31), channel_id=1, source_target_pairs={{0,1},{1,0},{2,3},{3,2},{4,5},{5,4},{6,7},{7,6},{8,9},{9,8},{10,11... | collective-permute-start | bytes 884744 | tf_op jit(solution)/shard_map/ppermute | solution.py:278
  32.7 1.7 %collective-permute-start.13 = (bf16[4,96,384]{2,1,0:T(8,128)(2,1)S(1)}, bf16[4,96,384]{2,1,0:T(8,128)(2,1)S(1)}, u32[]{:S(2)}, u32[]{:S(2)}) collective-permute-start(bf16[4,96,384]{2,1,0:T(8,128)(2,1)S(1)} %get-tuple-element.30), channel_id=1, source_target_pairs={{0,1},{1,0},{2,3},{3,2},{4,5},{5,4},{6,7},{7,6},{8,9},{9,8},{10,11... | collective-permute-start | bytes 884744 | tf_op jit(solution)/shard_map/ppermute | solution.py:278
  37.5 8.7 %collective-permute-start.14 = (bf16[2,48,384]{2,1,0:T(8,128)(2,1)S(1)}, bf16[2,48,384]{2,1,0:T(8,128)(2,1)S(1)}, u32[]{:S(2)}, u32[]{:S(2)}) collective-permute-start(bf16[2,48,384]{2,1,0:T(8,128)(2,1)S(1)} %get-tuple-element.27), channel_id=1, source_target_pairs={{0,8},{2,10},{4,12},{6,14},{8,0},{10,2},{12,4},{14,6},{1,9},{3,11}... | collective-permute-start | bytes 221192 | tf_op jit(solution)/shard_map/ppermute | solution.py:263
  40.0 6.8 %collective-permute-start.15 = (bf16[2,48,384]{2,1,0:T(8,128)(2,1)S(1)}, bf16[2,48,384]{2,1,0:T(8,128)(2,1)S(1)}, u32[]{:S(2)}, u32[]{:S(2)}) collective-permute-start(bf16[2,48,384]{2,1,0:T(8,128)(2,1)S(1)} %get-tuple-element.28), channel_id=1, source_target_pairs={{0,4},{2,6},{4,8},{6,10},{8,12},{10,14},{12,0},{14,2},{1,5},{3,7},... | collective-permute-start | bytes 221192 | tf_op jit(solution)/shard_map/ppermute | solution.py:263
  41.9 5.4 %collective-permute-start.16 = (bf16[2,48,384]{2,1,0:T(8,128)(2,1)S(1)}, bf16[2,48,384]{2,1,0:T(8,128)(2,1)S(1)}, u32[]{:S(2)}, u32[]{:S(2)}) collective-permute-start(bf16[2,48,384]{2,1,0:T(8,128)(2,1)S(1)} %get-tuple-element.29), channel_id=1, source_target_pairs={{0,12},{2,14},{4,0},{6,2},{8,4},{10,6},{12,8},{14,10},{1,13},{3,15... | collective-permute-start | bytes 221192 | tf_op jit(solution)/shard_map/ppermute | solution.py:263

commit v9 on v8

--- a/solution.py
+++ b/solution.py
@@ -282,7 +282,7 @@
 
     shared = [columns_of(stale_cache, (layer + k) % rounds) for k in range(rounds)]
     away_parts = [columns_of(fresh_first[1:], (layer + s) % layers) for s in range(1, layers)]
-    shared += [columns_of(after(fresh_first, *away_parts)[1:], layer), *away_parts]
+    shared += [columns_of(after(fresh_first, *away_parts, *shared)[1:], layer), *away_parts]
     *owned, text = pack(
         functools.partial(pack_owned_kernel, layers=layers),
         [(4, rows, width)] * layers + [(4, text_rows, width)],

time: 48.3 us -> 48.3 us (level)
  no operation moved by 1% of the time
where the time goes in v9:
time: 48.3 us; the launch traced here: 48 us
  starting transfers between devices  28.9 us (60%)
  Pallas kernels  8.15 us (17%)
  waiting for transfers between devices  6.43 us (13%)
  local copies, waits for them, and re-layouts  3.07 us (6%)
  between operations  1.07 us (2%)
    ppermute x9, starting transfers between devices, layer_swap(): return x if shift == 0 else lax.ppermute(x, 'patch', pairs)  23.6 us
    pallas_call x2, Pallas kernels, call_both(): pl.pallas_call(functools.partial(both_kernel, parts=parts, blocks=blocks,...  5.51 us
    ppermute x9, waiting for transfers between devices, layer_swap(): return x if shift == 0 else lax.ppermute(x, 'patch', pairs)  5.02 us
    pallas_call x1, Pallas kernels, pack(): pl.pallas_call(kernel, out_shape=[jax.ShapeDtypeStruct(shape, BF16) for s...  2.63 us
    ppermute x5, starting transfers between devices, other_core(): return lax.ppermute(x, 'uly', [(0, 1), (1, 0)])  2.25 us
    ppermute x1, starting transfers between devices, other_column(): lax.ppermute(x, 'patch', [(p, p ^ 1) for p in range(layers * COLUMNS)])  1.58 us
    ppermute x5, waiting for transfers between devices, other_core(): return lax.ppermute(x, 'uly', [(0, 1), (1, 0)])  1.41 us
    ppermute x2, starting transfers between devices, stale_round(): return lax.ppermute(x, ('patch', 'uly'), pairs)  1.41 us
  transfers between devices with their start and end apart: 17, of which 7 were waited for; matrix products, arithmetic and copies ran while one was open for 2% of the time, Pallas kernels for 10%

profile of v9, /device:TPU:0, one launch (start us, length us, event | category | flops | bytes accessed | tf_op | source)
XLA Modules:
  0.0 48.0 jit_solution(7400847059193692728)
XLA Ops:
  0.7 0.9 %slice-done = bf16[2,48,1536]{2,1,0:T(8,128)(2,1)S(1)} async-done(((bf16[3,48,1536]{2,1,0:T(8,128)(2,1)}), bf16[2,48,1536]{2,1,0:T(8,128)(2,1)S(1)}, s32[]{:S(2)}) %slice-start) | async-done | bytes 294936 | tf_op jit(solution)/shard_map/slice | solution.py:284
  1.7 3.1 %collective-permute-start.3 = (bf16[2,48,384]{2,1,0:T(8,128)(2,1)S(1)}, bf16[2,48,384]{2,1,0:T(8,128)(2,1)S(1)}, u32[]{:S(2)}, u32[]{:S(2)}) collective-permute-start(bf16[2,48,384]{2,1,0:T(8,128)(2,1)S(1)} %get-tuple-element.36), channel_id=1, source_target_pairs={{0,4},{2,6},{4,8},{6,10},{8,12},{10,14},{12,0},{14,2},{1,5},{3,7},... | collective-permute-start | bytes 221192 | tf_op jit(solution)/shard_map/ppermute | solution.py:263
  4.8 2.6 %collective-permute-start.4 = (bf16[2,48,384]{2,1,0:T(8,128)(2,1)S(1)}, bf16[2,48,384]{2,1,0:T(8,128)(2,1)S(1)}, u32[]{:S(2)}, u32[]{:S(2)}) collective-permute-start(bf16[2,48,384]{2,1,0:T(8,128)(2,1)S(1)} %get-tuple-element.35), channel_id=1, source_target_pairs={{0,8},{2,10},{4,12},{6,14},{8,0},{10,2},{12,4},{14,6},{1,9},{3,11}... | collective-permute-start | bytes 221192 | tf_op jit(solution)/shard_map/ppermute | solution.py:263
  7.4 1.3 %collective-permute-start.5 = (bf16[2,48,384]{2,1,0:T(8,128)(2,1)S(1)}, bf16[2,48,384]{2,1,0:T(8,128)(2,1)S(1)}, u32[]{:S(2)}, u32[]{:S(2)}) collective-permute-start(bf16[2,48,384]{2,1,0:T(8,128)(2,1)S(1)} %get-tuple-element.34), channel_id=1, source_target_pairs={{0,12},{2,14},{4,0},{6,2},{8,4},{10,6},{12,8},{14,10},{1,13},{3,15... | collective-permute-start | bytes 221192 | tf_op jit(solution)/shard_map/ppermute | solution.py:263
  8.8 0.7 %collective-permute-start.1 = (bf16[2,96,384]{2,1,0:T(8,128)(2,1)S(1)}, bf16[2,96,384]{2,1,0:T(8,128)(2,1)S(1)}, u32[]{:S(2)}, u32[]{:S(2)}) collective-permute-start(bf16[2,96,384]{2,1,0:T(8,128)(2,1)S(1)} %get-tuple-element.38), channel_id=1, source_target_pairs={{0,0},{1,8},{2,2},{3,10},{4,4},{5,12},{6,6},{7,14},{8,1},{9,9},{10... | collective-permute-start | bytes 442376 | tf_op jit(solution)/shard_map/ppermute | solution.py:272
  9.4 0.7 %collective-permute-start.2 = (bf16[2,96,384]{2,1,0:T(8,128)(2,1)S(1)}, bf16[2,96,384]{2,1,0:T(8,128)(2,1)S(1)}, u32[]{:S(2)}, u32[]{:S(2)}) collective-permute-start(bf16[2,96,384]{2,1,0:T(8,128)(2,1)S(1)} %get-tuple-element.37), channel_id=1, source_target_pairs={{0,4},{1,12},{2,6},{3,14},{4,0},{5,8},{6,2},{7,10},{8,5},{9,13},{1... | collective-permute-start | bytes 442376 | tf_op jit(solution)/shard_map/ppermute | solution.py:272
  10.2 1.0 %slice-done.1 = bf16[2,48,1536]{2,1,0:T(8,128)(2,1)S(1)} async-done(((bf16[3,48,1536]{2,1,0:T(8,128)(2,1)}), bf16[2,48,1536]{2,1,0:T(8,128)(2,1)S(1)}, s32[]{:S(2)}) %slice-start.1) | async-done | bytes 294936 | tf_op jit(solution)/shard_map/slice | solution.py:285
  11.1 2.6 %shard_map.77 = (bf16[4,48,384]{2,1,0:T(8,128)(2,1)}, bf16[4,48,384]{2,1,0:T(8,128)(2,1)}, bf16[4,48,384]{2,1,0:T(8,128)(2,1)}, bf16[4,48,384]{2,1,0:T(8,128)(2,1)}, bf16[4,256,384]{2,1,0:T(8,128)(2,1)}) custom-call(bf16[3,48,1536]{2,1,0:T(8,128)(2,1)} %first_ref, bf16[3,48,1536]{2,1,0:T(8,128)(2,1)} %second_ref.1, bf16[2,256,768]{2,1,0:T(8,128)(2,1)} %text_first_ref.1, ...), custom_call_target="tpu_custom_call" | custom-call | bytes 1048576 | tf_op jit(solution)/shard_map/pallas_call | solution.py:143
  13.8 1.4 %collective-permute-start = (bf16[4,48,384]{2,1,0:T(8,128)(2,1)}, bf16[4,48,384]{2,1,0:T(8,128)(2,1)S(1)}, u32[]{:S(2)}, u32[]{:S(2)}) collective-permute-start(bf16[4,48,384]{2,1,0:T(8,128)(2,1)} %get-tuple-element.19), channel_id=1, source_target_pairs={{0,4},{2,6},{4,8},{6,10},{8,12},{10,14},{12,0},{14,2},{1,5},{3,7},... | collective-permute-start | bytes 442376 | tf_op jit(solution)/shard_map/ppermute | solution.py:263
  15.2 1.1 %collective-permute-start.8 = (bf16[4,256,384]{2,1,0:T(8,128)(2,1)}, bf16[4,256,384]{2,1,0:T(8,128)(2,1)S(1)}, u32[]{:S(2)}, u32[]{:S(2)}) collective-permute-start(bf16[4,256,384]{2,1,0:T(8,128)(2,1)} %get-tuple-element.25.text_ref), channel_id=1, source_target_pairs={{0,1},{1,0},{2,3},{3,2},{4,5},{5,4},{6,7},{7,6},{8,9},{9,8},{10,11... | collective-permute-start | bytes 2359304 | tf_op jit(solution)/shard_map/ppermute | solution.py:278
  16.4 0.1 pad_maximum_fusion.refs_0_
  16.5 1.6 %collective-permute-start.11 = (bf16[8,96,384]{2,1,0:T(8,128)(2,1)S(1)}, bf16[8,96,384]{2,1,0:T(8,128)(2,1)S(1)}, u32[]{:S(2)}, u32[]{:S(2)}) collective-permute-start(bf16[8,96,384]{2,1,0:T(8,128)(2,1)S(1)} %pad_maximum_fusion.refs_0_), channel_id=1, source_target_pairs={{0,2},{2,0},{4,6},{6,4},{8,10},{10,8},{12,14},{14,12},{1,3},{3,1},... | collective-permute-start | bytes 1769480 | tf_op jit(solution)/shard_map/ppermute | solution.py:275
  18.1 5.5 %collective-permute-start.6 = (bf16[4,48,384]{2,1,0:T(8,128)(2,1)}, bf16[4,48,384]{2,1,0:T(8,128)(2,1)S(1)}, u32[]{:S(2)}, u32[]{:S(2)}) collective-permute-start(bf16[4,48,384]{2,1,0:T(8,128)(2,1)} %get-tuple-element.23), channel_id=1, source_target_pairs={{0,8},{2,10},{4,12},{6,14},{8,0},{10,2},{12,4},{14,6},{1,9},{3,11}... | collective-permute-start | bytes 442376 | tf_op jit(solution)/shard_map/ppermute | solution.py:263
  23.9 3.4 %collective-permute-start.7 = (bf16[4,48,384]{2,1,0:T(8,128)(2,1)}, bf16[4,48,384]{2,1,0:T(8,128)(2,1)S(1)}, u32[]{:S(2)}, u32[]{:S(2)}) collective-permute-start(bf16[4,48,384]{2,1,0:T(8,128)(2,1)} %get-tuple-element.24), channel_id=1, source_target_pairs={{0,12},{2,14},{4,0},{6,2},{8,4},{10,6},{12,8},{14,10},{1,13},{3,15... | collective-permute-start | bytes 442376 | tf_op jit(solution)/shard_map/ppermute | solution.py:263
  27.3 2.3 %collective-permute-done.6 = bf16[4,48,384]{2,1,0:T(8,128)(2,1)S(1)} collective-permute-done((bf16[4,48,384]{2,1,0:T(8,128)(2,1)}, bf16[4,48,384]{2,1,0:T(8,128)(2,1)S(1)}, u32[]{:S(2)}, u32[]{:S(2)}) %collective-permute-start.6) | collective-permute-done | bytes 147488 | tf_op jit(solution)/shard_map/ppermute | solution.py:263
  29.7 1.8 %collective-permute-done.7 = bf16[4,48,384]{2,1,0:T(8,128)(2,1)S(1)} collective-permute-done((bf16[4,48,384]{2,1,0:T(8,128)(2,1)}, bf16[4,48,384]{2,1,0:T(8,128)(2,1)S(1)}, u32[]{:S(2)}, u32[]{:S(2)}) %collective-permute-start.7) | collective-permute-done | bytes 147488 | tf_op jit(solution)/shard_map/ppermute | solution.py:263
  31.5 0.1 collective-permute-start.9
  31.6 0.1 fusion.3
  31.9 0.8 %collective-permute-start.12 = (bf16[4,96,384]{2,1,0:T(8,128)(2,1)S(1)}, bf16[4,96,384]{2,1,0:T(8,128)(2,1)S(1)}, u32[]{:S(2)}, u32[]{:S(2)}) collective-permute-start(bf16[4,96,384]{2,1,0:T(8,128)(2,1)S(1)} %get-tuple-element.31), channel_id=1, source_target_pairs={{0,1},{1,0},{2,3},{3,2},{4,5},{5,4},{6,7},{7,6},{8,9},{9,8},{10,11... | collective-permute-start | bytes 884744 | tf_op jit(solution)/shard_map/ppermute | solution.py:278
  32.7 0.1 collective-permute-start.13
  32.8 0.1 add_bitcast_fusion
  33.0 0.7 %collective-permute-done.9.last_twin_ref = bf16[4,192,384]{2,1,0:T(8,128)(2,1)} collective-permute-done((bf16[4,192,384]{2,1,0:T(8,128)(2,1)S(1)}, bf16[4,192,384]{2,1,0:T(8,128)(2,1)}, u32[]{:S(2)}, u32[]{:S(2)}) %collective-permute-start.9) | collective-permute-done | bytes 589856 | tf_op jit(solution)/shard_map/ppermute | solution.py:278
  33.7 0.3 collective-permute-done.12.refs_3_
  34.0 0.4 collective-permute-done.13.refs_4_
  34.4 3.1 %shard_map.79 = (bf16[2,48,384]{2,1,0:T(8,128)(2,1)S(1)}, bf16[2,48,384]{2,1,0:T(8,128)(2,1)S(1)}, bf16[2,48,384]{2,1,0:T(8,128)(2,1)S(1)}) custom-call(f32[2,3]{1,0:T(2,128)S(1)} %fusion.2.scale_ref, s32[3,4]{1,0:T(4,128)S(1)} %add_add_fusion.order_ref, bf16[2,192,384]{2,1,0:T(8,128)(2,1)S(1)} %slice.30.queries_ref, bf16[4,256,384]{2,1,0:T(8,128)(2,1)S(1)} %copy-done, ...), custom_call_target="tpu_custom_call" | custom-call | flops 452984832 | bytes 3440640 | tf_op jit(solution)/shard_map/pallas_call | solution.py:233
  37.5 2.5 %collective-permute-start.14 = (bf16[2,48,384]{2,1,0:T(8,128)(2,1)S(1)}, bf16[2,48,384]{2,1,0:T(8,128)(2,1)S(1)}, u32[]{:S(2)}, u32[]{:S(2)}) collective-permute-start(bf16[2,48,384]{2,1,0:T(8,128)(2,1)S(1)} %get-tuple-element.27), channel_id=1, source_target_pairs={{0,8},{2,10},{4,12},{6,14},{8,0},{10,2},{12,4},{14,6},{1,9},{3,11}... | collective-permute-start | bytes 221192 | tf_op jit(solution)/shard_map/ppermute | solution.py:263
  40.0 1.8 %collective-permute-start.15 = (bf16[2,48,384]{2,1,0:T(8,128)(2,1)S(1)}, bf16[2,48,384]{2,1,0:T(8,128)(2,1)S(1)}, u32[]{:S(2)}, u32[]{:S(2)}) collective-permute-start(bf16[2,48,384]{2,1,0:T(8,128)(2,1)S(1)} %get-tuple-element.28), channel_id=1, source_target_pairs={{0,4},{2,6},{4,8},{6,10},{8,12},{10,14},{12,0},{14,2},{1,5},{3,7},... | collective-permute-start | bytes 221192 | tf_op jit(solution)/shard_map/ppermute | solution.py:263
  41.9 2.0 %collective-permute-start.16 = (bf16[2,48,384]{2,1,0:T(8,128)(2,1)S(1)}, bf16[2,48,384]{2,1,0:T(8,128)(2,1)S(1)}, u32[]{:S(2)}, u32[]{:S(2)}) collective-permute-start(bf16[2,48,384]{2,1,0:T(8,128)(2,1)S(1)} %get-tuple-element.29), channel_id=1, source_target_pairs={{0,12},{2,14},{4,0},{6,2},{8,4},{10,6},{12,8},{14,10},{1,13},{3,15... | collective-permute-start | bytes 221192 | tf_op jit(solution)/shard_map/ppermute | solution.py:263
  43.8 2.4 %shard_map.78 = bf16[2,48,384]{2,1,0:T(8,128)(2,1)S(1)} custom-call(f32[2,3]{1,0:T(2,128)S(1)} %fusion.2.scale_ref, s32[3,4]{1,0:T(4,128)S(1)} %add_add_fusion.order_ref, bf16[2,192,384]{2,1,0:T(8,128)(2,1)S(1)} %slice.30.queries_ref, bf16[4,256,384]{2,1,0:T(8,128)(2,1)S(1)} %copy-done, bf16[4,256,384]{2,1,0:T(8,128)(2,1)S(1)} %collective-permute-done.8.text_twin_ref, ...), custom_call_target="tpu_custom_call" | custom-call | flops 150994944 | bytes 3440640 | tf_op jit(solution)/shard_map/pallas_call | solution.py:233
  46.3 0.5 %collective-permute-done.15 = bf16[2,48,384]{2,1,0:T(8,128)(2,1)S(1)} collective-permute-done((bf16[2,48,384]{2,1,0:T(8,128)(2,1)S(1)}, bf16[2,48,384]{2,1,0:T(8,128)(2,1)S(1)}, u32[]{:S(2)}, u32[]{:S(2)}) %collective-permute-start.15) | collective-permute-done | bytes 73760 | tf_op jit(solution)/shard_map/ppermute | solution.py:263
  46.9 0.4 collective-permute-done.16
  47.3 0.7 %slice_bitcast_fusion = (bf16[48,1536]{1,0:T(8,128)(2,1)}, bf16[48,1536]{1,0:T(8,128)(2,1)}) fusion(bf16[2,48,1536]{2,1,0:T(8,128)(2,1)S(1)} %constant_dynamic-update-slice_fusion.4), kind=kLoop, calls=%fused_computation.2 | loop fusion | bytes 589824 | tf_op jit(solution)/shard_map/squeeze | solution.py:327
  (39 shorter events, 0.7 us)
Async XLA Ops:
  0.7 1.0 %slice-start = ((bf16[3,48,1536]{2,1,0:T(8,128)(2,1)}), bf16[2,48,1536]{2,1,0:T(8,128)(2,1)S(1)}, s32[]{:S(2)}) async-start(bf16[3,48,1536]{2,1,0:T(8,128)(2,1)} %first_ref), calls=%async_computation | async-start | bytes 589824 | tf_op jit(solution)/shard_map/slice | solution.py:284
  0.7 8.0 %copy-start.1 = (bf16[2,96,768]{2,1,0:T(8,128)(2,1)S(1)}, bf16[2,96,768]{2,1,0:T(8,128)(2,1)}, u32[]{:S(2)}) copy-start(bf16[2,96,768]{2,1,0:T(8,128)(2,1)} %param.8) | copy-start | bytes 884740
  1.7 12.1 %collective-permute-start.3 = (bf16[2,48,384]{2,1,0:T(8,128)(2,1)S(1)}, bf16[2,48,384]{2,1,0:T(8,128)(2,1)S(1)}, u32[]{:S(2)}, u32[]{:S(2)}) collective-permute-start(bf16[2,48,384]{2,1,0:T(8,128)(2,1)S(1)} %get-tuple-element.36), channel_id=1, source_target_pairs={{0,4},{2,6},{4,8},{6,10},{8,12},{10,14},{12,0},{14,2},{1,5},{3,7},... | collective-permute-start | bytes 221192 | tf_op jit(solution)/shard_map/ppermute | solution.py:263
  4.8 10.4 %collective-permute-start.4 = (bf16[2,48,384]{2,1,0:T(8,128)(2,1)S(1)}, bf16[2,48,384]{2,1,0:T(8,128)(2,1)S(1)}, u32[]{:S(2)}, u32[]{:S(2)}) collective-permute-start(bf16[2,48,384]{2,1,0:T(8,128)(2,1)S(1)} %get-tuple-element.35), channel_id=1, source_target_pairs={{0,8},{2,10},{4,12},{6,14},{8,0},{10,2},{12,4},{14,6},{1,9},{3,11}... | collective-permute-start | bytes 221192 | tf_op jit(solution)/shard_map/ppermute | solution.py:263
  7.4 9.0 %collective-permute-start.5 = (bf16[2,48,384]{2,1,0:T(8,128)(2,1)S(1)}, bf16[2,48,384]{2,1,0:T(8,128)(2,1)S(1)}, u32[]{:S(2)}, u32[]{:S(2)}) collective-permute-start(bf16[2,48,384]{2,1,0:T(8,128)(2,1)S(1)} %get-tuple-element.34), channel_id=1, source_target_pairs={{0,12},{2,14},{4,0},{6,2},{8,4},{10,6},{12,8},{14,10},{1,13},{3,15... | collective-permute-start | bytes 221192 | tf_op jit(solution)/shard_map/ppermute | solution.py:263
  8.8 7.6 %collective-permute-start.1 = (bf16[2,96,384]{2,1,0:T(8,128)(2,1)S(1)}, bf16[2,96,384]{2,1,0:T(8,128)(2,1)S(1)}, u32[]{:S(2)}, u32[]{:S(2)}) collective-permute-start(bf16[2,96,384]{2,1,0:T(8,128)(2,1)S(1)} %get-tuple-element.38), channel_id=1, source_target_pairs={{0,0},{1,8},{2,2},{3,10},{4,4},{5,12},{6,6},{7,14},{8,1},{9,9},{10... | collective-permute-start | bytes 442376 | tf_op jit(solution)/shard_map/ppermute | solution.py:272
  9.4 7.0 %collective-permute-start.2 = (bf16[2,96,384]{2,1,0:T(8,128)(2,1)S(1)}, bf16[2,96,384]{2,1,0:T(8,128)(2,1)S(1)}, u32[]{:S(2)}, u32[]{:S(2)}) collective-permute-start(bf16[2,96,384]{2,1,0:T(8,128)(2,1)S(1)} %get-tuple-element.37), channel_id=1, source_target_pairs={{0,4},{1,12},{2,6},{3,14},{4,0},{5,8},{6,2},{7,10},{8,5},{9,13},{1... | collective-permute-start | bytes 442376 | tf_op jit(solution)/shard_map/ppermute | solution.py:272
  10.2 1.0 %slice-start.1 = ((bf16[3,48,1536]{2,1,0:T(8,128)(2,1)}), bf16[2,48,1536]{2,1,0:T(8,128)(2,1)S(1)}, s32[]{:S(2)}) async-start(bf16[3,48,1536]{2,1,0:T(8,128)(2,1)} %first_ref), calls=%async_computation.1 | async-start | bytes 589824 | tf_op jit(solution)/shard_map/slice | solution.py:285
  13.8 10.0 %collective-permute-start = (bf16[4,48,384]{2,1,0:T(8,128)(2,1)}, bf16[4,48,384]{2,1,0:T(8,128)(2,1)S(1)}, u32[]{:S(2)}, u32[]{:S(2)}) collective-permute-start(bf16[4,48,384]{2,1,0:T(8,128)(2,1)} %get-tuple-element.19), channel_id=1, source_target_pairs={{0,4},{2,6},{4,8},{6,10},{8,12},{10,14},{12,0},{14,2},{1,5},{3,7},... | collective-permute-start | bytes 442376 | tf_op jit(solution)/shard_map/ppermute | solution.py:263
  15.2 17.8 %collective-permute-start.8 = (bf16[4,256,384]{2,1,0:T(8,128)(2,1)}, bf16[4,256,384]{2,1,0:T(8,128)(2,1)S(1)}, u32[]{:S(2)}, u32[]{:S(2)}) collective-permute-start(bf16[4,256,384]{2,1,0:T(8,128)(2,1)} %get-tuple-element.25.text_ref), channel_id=1, source_target_pairs={{0,1},{1,0},{2,3},{3,2},{4,5},{5,4},{6,7},{7,6},{8,9},{9,8},{10,11... | collective-permute-start | bytes 2359304 | tf_op jit(solution)/shard_map/ppermute | solution.py:278
  16.4 1.7 %copy-start.2 = (bf16[4,48,384]{2,1,0:T(8,128)(2,1)S(1)}, bf16[4,48,384]{2,1,0:T(8,128)(2,1)}, u32[]{:S(2)}) copy-start(bf16[4,48,384]{2,1,0:T(8,128)(2,1)} %get-tuple-element.18) | copy-start | bytes 442372
  16.5 15.3 %collective-permute-start.11 = (bf16[8,96,384]{2,1,0:T(8,128)(2,1)S(1)}, bf16[8,96,384]{2,1,0:T(8,128)(2,1)S(1)}, u32[]{:S(2)}, u32[]{:S(2)}) collective-permute-start(bf16[8,96,384]{2,1,0:T(8,128)(2,1)S(1)} %pad_maximum_fusion.refs_0_), channel_id=1, source_target_pairs={{0,2},{2,0},{4,6},{6,4},{8,10},{10,8},{12,14},{14,12},{1,3},{3,1},... | collective-permute-start | bytes 1769480 | tf_op jit(solution)/shard_map/ppermute | solution.py:275
  18.1 5.5 %copy-start.3 = (s32[2,12]{1,0:T(2,128)S(1)}, s32[2,12]{1,0:T(2,128)}, u32[]{:S(2)}) copy-start(s32[2,12]{1,0:T(2,128)} %param.9) | copy-start | bytes 292
  18.1 11.5 %collective-permute-start.6 = (bf16[4,48,384]{2,1,0:T(8,128)(2,1)}, bf16[4,48,384]{2,1,0:T(8,128)(2,1)S(1)}, u32[]{:S(2)}, u32[]{:S(2)}) collective-permute-start(bf16[4,48,384]{2,1,0:T(8,128)(2,1)} %get-tuple-element.23), channel_id=1, source_target_pairs={{0,8},{2,10},{4,12},{6,14},{8,0},{10,2},{12,4},{14,6},{1,9},{3,11}... | collective-permute-start | bytes 442376 | tf_op jit(solution)/shard_map/ppermute | solution.py:263
  23.8 9.2 %collective-permute-start.10 = (bf16[8,96,384]{2,1,0:T(8,128)(2,1)S(1)}, bf16[8,96,384]{2,1,0:T(8,128)(2,1)S(1)}, u32[]{:S(2)}, u32[]{:S(2)}) collective-permute-start(bf16[8,96,384]{2,1,0:T(8,128)(2,1)S(1)} %pad_maximum_fusion.refs_0_), channel_id=1, source_target_pairs={{0,1},{1,0},{2,3},{3,2},{4,5},{5,4},{6,7},{7,6},{8,9},{9,8},{10,11... | collective-permute-start | bytes 1769480 | tf_op jit(solution)/shard_map/ppermute | solution.py:278
  23.9 7.6 %collective-permute-start.7 = (bf16[4,48,384]{2,1,0:T(8,128)(2,1)}, bf16[4,48,384]{2,1,0:T(8,128)(2,1)S(1)}, u32[]{:S(2)}, u32[]{:S(2)}) collective-permute-start(bf16[4,48,384]{2,1,0:T(8,128)(2,1)} %get-tuple-element.24), channel_id=1, source_target_pairs={{0,12},{2,14},{4,0},{6,2},{8,4},{10,6},{12,8},{14,10},{1,13},{3,15... | collective-permute-start | bytes 442376 | tf_op jit(solution)/shard_map/ppermute | solution.py:263
  31.5 2.2 %collective-permute-start.9 = (bf16[4,192,384]{2,1,0:T(8,128)(2,1)S(1)}, bf16[4,192,384]{2,1,0:T(8,128)(2,1)}, u32[]{:S(2)}, u32[]{:S(2)}) collective-permute-start(bf16[4,192,384]{2,1,0:T(8,128)(2,1)S(1)} %constant_dynamic-update-slice_fusion.last_ref), channel_id=1, source_target_pairs={{0,1},{1,0},{2,3},{3,2},{4,5},{5,4},{6,7},{7,6},{8,9},{9,8},{10,11... | collective-permute-start | bytes 1769480 | tf_op jit(solution)/shard_map/ppermute | solution.py:278
  31.8 2.6 %copy-start = (bf16[4,256,384]{2,1,0:T(8,128)(2,1)S(1)}, bf16[4,256,384]{2,1,0:T(8,128)(2,1)}, u32[]{:S(2)}) copy-start(bf16[4,256,384]{2,1,0:T(8,128)(2,1)} %get-tuple-element.25.text_ref) | copy-start | bytes 2359300
  31.9 2.1 %collective-permute-start.12 = (bf16[4,96,384]{2,1,0:T(8,128)(2,1)S(1)}, bf16[4,96,384]{2,1,0:T(8,128)(2,1)S(1)}, u32[]{:S(2)}, u32[]{:S(2)}) collective-permute-start(bf16[4,96,384]{2,1,0:T(8,128)(2,1)S(1)} %get-tuple-element.31), channel_id=1, source_target_pairs={{0,1},{1,0},{2,3},{3,2},{4,5},{5,4},{6,7},{7,6},{8,9},{9,8},{10,11... | collective-permute-start | bytes 884744 | tf_op jit(solution)/shard_map/ppermute | solution.py:278
  32.7 1.7 %collective-permute-start.13 = (bf16[4,96,384]{2,1,0:T(8,128)(2,1)S(1)}, bf16[4,96,384]{2,1,0:T(8,128)(2,1)S(1)}, u32[]{:S(2)}, u32[]{:S(2)}) collective-permute-start(bf16[4,96,384]{2,1,0:T(8,128)(2,1)S(1)} %get-tuple-element.30), channel_id=1, source_target_pairs={{0,1},{1,0},{2,3},{3,2},{4,5},{5,4},{6,7},{7,6},{8,9},{9,8},{10,11... | collective-permute-start | bytes 884744 | tf_op jit(solution)/shard_map/ppermute | solution.py:278
  37.5 8.7 %collective-permute-start.14 = (bf16[2,48,384]{2,1,0:T(8,128)(2,1)S(1)}, bf16[2,48,384]{2,1,0:T(8,128)(2,1)S(1)}, u32[]{:S(2)}, u32[]{:S(2)}) collective-permute-start(bf16[2,48,384]{2,1,0:T(8,128)(2,1)S(1)} %get-tuple-element.27), channel_id=1, source_target_pairs={{0,8},{2,10},{4,12},{6,14},{8,0},{10,2},{12,4},{14,6},{1,9},{3,11}... | collective-permute-start | bytes 221192 | tf_op jit(solution)/shard_map/ppermute | solution.py:263
  40.0 6.8 %collective-permute-start.15 = (bf16[2,48,384]{2,1,0:T(8,128)(2,1)S(1)}, bf16[2,48,384]{2,1,0:T(8,128)(2,1)S(1)}, u32[]{:S(2)}, u32[]{:S(2)}) collective-permute-start(bf16[2,48,384]{2,1,0:T(8,128)(2,1)S(1)} %get-tuple-element.28), channel_id=1, source_target_pairs={{0,4},{2,6},{4,8},{6,10},{8,12},{10,14},{12,0},{14,2},{1,5},{3,7},... | collective-permute-start | bytes 221192 | tf_op jit(solution)/shard_map/ppermute | solution.py:263
  41.9 5.4 %collective-permute-start.16 = (bf16[2,48,384]{2,1,0:T(8,128)(2,1)S(1)}, bf16[2,48,384]{2,1,0:T(8,128)(2,1)S(1)}, u32[]{:S(2)}, u32[]{:S(2)}) collective-permute-start(bf16[2,48,384]{2,1,0:T(8,128)(2,1)S(1)} %get-tuple-element.29), channel_id=1, source_target_pairs={{0,12},{2,14},{4,0},{6,2},{8,4},{10,6},{12,8},{14,10},{1,13},{3,15... | collective-permute-start | bytes 221192 | tf_op jit(solution)/shard_map/ppermute | solution.py:263
